TPU v7x, 32 devices: a whole 2x2x4 slice. The times are simulated.
32 devices in a mesh: pair: 4 (over y, x), slab: 8 (over z, core).
Axes of the slice: x: 2, y: 2, z: 4, core: 2. Of those that a mesh axis runs over, the one named last changes fastest.
Arguments:
- r_slabs: float32 [12288, 12288], P('slab', 'pair'), may hold values from -2 to 2, as said below
- basis: float32 [12288, 12288], P('slab', 'pair'), may hold values from -0.0546875 to 0.0546875
- owners: int32 [256], P('slab'), may hold values from 0 to 255, as said below
- plan: int32 [2, 64], replicated, may hold values from 0 to 63, as said below
Outputs:
- r_out: float32 [12288, 12288], P('slab', 'pair')
- v_out: float32 [12288, 12288], P('slab', 'pair')
Inputs may be any that keep to these rules, and one draw needn't show every extreme that they name: `r_slabs`: in natural row order R is upper triangular with a diagonal between 1 and 2. `owners`: A permutation of the 256 row blocks; of the 32 stored row blocks on each index of slab, exactly 4 belong to the natural range of rows of each index of slab. `plan`: each row is a permutation of the 64 column blocks; slots 2q and 2q + 1 form a pair.
All inputs are finite; a program needn't handle non-finite values.
Results may differ from a plain program's by a relative error of at most 0.0003.
Values sent between devices are 32-bit elements; how exact they have to be, the bound alone decides.
No kernel may reach another device: no remote copies, remote signals or barrier semaphores. Data moves between devices by JAX's collectives and lax.ppermute only.
A program may use at most 192 MiB of HBM per device.

v0:
```python
import jax
import jax.numpy as jnp
from jax import lax
from jax.sharding import PartitionSpec as P

BLK = 192


HIGH = lax.Precision.HIGHEST
EPSILON = 1e-06


def rotations(cross_gram, col_norms):
    width = cross_gram.shape[-1]
    scale_a = lax.rsqrt(col_norms[:, :width])
    scale_b = lax.rsqrt(col_norms[:, width:])
    normed = cross_gram * scale_a[:, :, None] * scale_b[:, None, :]
    frobenius = jnp.sqrt(jnp.sum(normed * normed, axis=(1, 2)))
    coupling = normed / (1.0 + frobenius)[:, None, None]
    outer_a = jnp.einsum("pik,pjk->pij", coupling, coupling, precision=HIGH)
    outer_b = jnp.einsum("pki,pkj->pij", coupling, coupling, precision=HIGH)
    identity = jnp.eye(width, dtype=cross_gram.dtype)
    left_poly = (
        identity
        - 0.5 * outer_a
        + 0.375 * jnp.einsum("pik,pkj->pij", outer_a, outer_a, precision=HIGH)
    )
    right_poly = (
        identity
        - 0.5 * outer_b
        + 0.375 * jnp.einsum("pik,pkj->pij", outer_b, outer_b, precision=HIGH)
    )
    upper_half = jnp.concatenate(
        [left_poly, -jnp.einsum("pik,pkj->pij", coupling, right_poly, precision=HIGH)], axis=2
    )
    lower_half = jnp.concatenate(
        [jnp.einsum("pki,pkj->pij", coupling, left_poly, precision=HIGH), right_poly], axis=2
    )
    return jnp.concatenate([upper_half, lower_half], axis=1)


def rotate(paired, turns):
    return jnp.einsum("npk,pkj->npj", paired, turns, precision=HIGH)


def local_terms(paired):
    width = paired.shape[2] // 2
    cross_gram = jnp.einsum(
        "npi,npj->pij", paired[:, :, :width], paired[:, :, width:], precision=HIGH
    )
    squares = jnp.sum(paired * paired, axis=0)
    return (cross_gram, squares)


def row_settle(owners):
    table = lax.all_gather(owners, "slab", axis=0, tiled=True)
    per_device = owners.shape[0]
    total = table.shape[0]
    slab_index = lax.axis_index("slab")
    stored_at = jnp.argsort(table)
    wanted = slab_index * per_device + jnp.arange(per_device, dtype=jnp.int32)
    source = jnp.take(stored_at, wanted) // per_device
    arrival = jnp.argsort(source * total + jnp.arange(per_device, dtype=jnp.int32))
    return jnp.argsort(arrival)


def natural_order(r_slabs, owners, settle_rows, sender):
    per_device = owners.shape[0]
    blocks = r_slabs.reshape(per_device, r_slabs.shape[0] // per_device, r_slabs.shape[1])
    packed = jnp.take(blocks, jnp.argsort(owners), axis=0)
    arrived = sender(packed)
    placed = jnp.take(arrived, settle_rows, axis=0)
    return placed.reshape(r_slabs.shape)


def column_pass(r_local, basis, plan, mover, summer):
    steps = plan.shape[0]
    nblocks = plan.shape[1]
    previous = jnp.arange(nblocks, dtype=jnp.int32)
    pair_index = lax.axis_index("pair")
    row_count = r_local.shape[0]
    local_count = r_local.shape[1] // BLK
    r_slots = r_local.reshape(row_count, local_count, BLK)
    v_slots = basis.reshape(row_count, local_count, BLK)
    start = pair_index * local_count
    for step in range(steps):
        current = plan[step]
        old_place = jnp.argsort(previous)
        holding = lax.dynamic_slice_in_dim(previous, start, local_count)
        target = jnp.take(jnp.argsort(current), holding)
        outgoing = jnp.argsort(target)
        r_sent = jnp.take(r_slots, outgoing, axis=1)
        v_sent = jnp.take(v_slots, outgoing, axis=1)
        r_got, v_got = mover(r_sent, v_sent)
        arriving = lax.dynamic_slice_in_dim(current, start, local_count)
        source = jnp.take(old_place, arriving) // local_count
        arrival = jnp.argsort(source * nblocks + jnp.arange(local_count, dtype=jnp.int32))
        settle = jnp.argsort(arrival)
        r_pairs = jnp.take(r_got, settle, axis=1).reshape(row_count, local_count // 2, 2 * BLK)
        v_pairs = jnp.take(v_got, settle, axis=1).reshape(row_count, local_count // 2, 2 * BLK)
        cross_gram, squares = local_terms(r_pairs)
        cross_gram, squares = summer(cross_gram, squares)
        turns = rotations(cross_gram, squares + EPSILON)
        r_slots = rotate(r_pairs, turns).reshape(row_count, local_count, BLK)
        v_slots = rotate(v_pairs, turns).reshape(row_count, local_count, BLK)
        previous = current
    return (
        r_slots.reshape(row_count, local_count * BLK),
        v_slots.reshape(row_count, local_count * BLK),
    )


def shards(r_slabs, basis, owners, plan):
    settle_rows = row_settle(owners)

    def send_natural(packed):
        return lax.all_to_all(packed, "slab", split_axis=0, concat_axis=0, tiled=True)

    def block_mover(r_sent, v_sent):
        return (
            lax.all_to_all(r_sent, "pair", split_axis=1, concat_axis=1, tiled=True),
            lax.all_to_all(v_sent, "pair", split_axis=1, concat_axis=1, tiled=True),
        )

    def block_summer(cross_gram, squares):
        return lax.psum((cross_gram, squares), "slab")

    r_local = natural_order(r_slabs, owners, settle_rows, send_natural)
    r_out, v_out = column_pass(r_local, basis, plan, block_mover, block_summer)
    return (r_out, v_out)


def solution(mesh):
    placed = (P("slab", "pair"), P("slab", "pair"), P("slab"), P())
    return jax.shard_map(
        shards,
        mesh=mesh,
        in_specs=placed,
        out_specs=(P("slab", "pair"), P("slab", "pair")),
        check_vma=False,
    )
```

profile of v0, /device:TPU:8, one launch (start us, length us, event | category | flops | bytes accessed | tf_op | source)
XLA Modules:
  0.0 1811.7 jit_solution(13314523107603083000)
XLA Ops:
  24.6 16.0 gather_fusion.1
  40.6 13.0 broadcast_select_fusion.5
  60.6 18.6 %copy.27 = f32[1536,3072]{0,1:T(8,128)} copy(f32[1536,3072]{1,0:T(8,128)} %param.11) | data formatting | bytes 37748736 | tf_op args[1]
  83.4 15.8 gather_fusion.11
  102.4 363.3 %all-to-all-done = f32[32,48,3072]{2,1,0:T(8,128)} async-done(((f32[32,48,3072]{2,1,0:T(8,128)}), f32[32,48,3072]{2,1,0:T(8,128)}, u32[]{:S(2)}, u32[]{:S(2)}) %all-to-all-start) | async-done | bytes 18874400 | tf_op jit(solution)/shard_map/all_to_all | solution.py:117
  465.7 16.0 gather_fusion.2
  481.7 13.1 broadcast_select_fusion.4
  494.8 25.9 %reshape_reshape.9 = f32[1536,16,192]{2,1,0:T(8,128)} reshape(f32[32,48,3072]{2,1,0:T(8,128)} %broadcast_select_fusion.4) | data formatting | bytes 37748736 | tf_op jit(solution)/shard_map/reshape;reshape | solution.py:83
  520.7 22.9 %copy.18 = f32[1536,16,192]{0,2,1:T(8,128)} copy(f32[1536,16,192]{2,1,0:T(8,128)} %reshape_reshape.9) | data formatting | bytes 37748736 | tf_op jit(solution)/shard_map/reshape;reshape | solution.py:83
  543.5 15.4 gather_fusion.4
  558.9 21.0 %select_bitcast_fusion.1 = (f32[1536,16,192]{0,2,1:T(8,128)}, f32[1536,16,192]{0,2,1:T(8,128)S(1)}) fusion(f32[16,1536,192]{1,2,0:T(8,128)} %gather_fusion.11, pred[16]{0:T(512)(128)(4,1)S(1)} %compare_and_fusion.4, f32[16,1536,192]{1,2,0:T(8,128)} %gather_fusion.4), kind=kLoop, calls=%fused_computation.20 | loop fusion | flops 9437184 | bytes 75497488 | tf_op jit(solution)/shard_map/jit(_take)/select_n | solution.py:93
  580.0 210.2 %all_to_all.25 = f32[1536,16,192]{0,2,1:T(8,128)} all-to-all(f32[1536,16,192]{0,2,1:T(8,128)S(1)} %get-tuple-element.50), channel_id=1, replica_groups=mesh['pair'=4,'slab'=8] {'pair'}, dimensions={1} | all-to-all | bytes 37748736 | tf_op jit(solution)/shard_map/all_to_all | solution.py:121
  807.9 15.8 gather_fusion.6
  848.1 153.9 %all-to-all-done.3 = f32[1536,16,192]{0,2,1:T(8,128)} async-done(((f32[1536,16,192]{0,2,1:T(8,128)}), f32[1536,16,192]{0,2,1:T(8,128)}, u32[]{:S(2)}, u32[]{:S(2)}) %all-to-all-start.3) | async-done | bytes 18874400 | tf_op jit(solution)/shard_map/all_to_all | solution.py:122
  1002.0 15.9 gather_fusion.12
  1017.9 13.1 broadcast_select_fusion.1
  1031.1 25.2 %psum.29 = f32[8,384]{1,0:T(8,128)S(1)} all-reduce(f32[8,384]{1,0:T(8,128)S(1)} %reduce_sum.41), channel_id=1, replica_groups=mesh['pair'=4,'slab'=8] {'slab'}, use_global_device_ids=true, to_apply=%region_11.15 | all-reduce | flops 3072 | bytes 24576 | tf_op jit(solution)/shard_map/psum | solution.py:126
  1075.1 35.4 %fusion.11 = f32[8,384,1536]{2,1,0:T(8,128)} fusion(f32[1536,8,384]{0,2,1:T(8,128)S(1)} %bitcast.74, f32[8,192,192]{2,1,0:T(8,128)S(1)} %multiply_add_fusion.2, f32[8,192,192]{2,1,0:T(8,128)S(1)} %fusion.27, f32[8,192,192]{2,1,0:T(8,128)} %convolution_negate_fusion.1, f32[8,192,192]{2,1,0:T(8,128)S(1)} %multiply_add_fusion.3), kind=kOutput, calls=%fused_computation.40 | convolution fusion | flops 21746810880 | bytes 42467328 | tf_op jit(solution)/shard_map/npk,pkj->npj/dot_general | solution.py:43
  1110.5 37.0 %fusion.10 = f32[8,384,1536]{2,1,0:T(8,128)} fusion(f32[1536,8,384]{0,2,1:T(8,128)} %bitcast.79, f32[8,192,192]{2,1,0:T(8,128)S(1)} %multiply_add_fusion.2, f32[8,192,192]{2,1,0:T(8,128)S(1)} %fusion.27, f32[8,192,192]{2,1,0:T(8,128)} %convolution_negate_fusion.1, f32[8,192,192]{2,1,0:T(8,128)S(1)} %multiply_add_fusion.3), kind=kOutput, calls=%fused_computation.39 | convolution fusion | flops 21746810880 | bytes 42467328 | tf_op jit(solution)/shard_map/npk,pkj->npj/dot_general | solution.py:43
  1147.5 15.8 gather_fusion.13
  1163.2 15.8 gather_fusion.8
  1179.0 21.0 %select_bitcast_fusion = (f32[1536,16,192]{0,2,1:T(8,128)}, f32[1536,16,192]{0,2,1:T(8,128)S(1)}) fusion(f32[16,1536,192]{1,2,0:T(8,128)} %gather_fusion.13, pred[16]{0:T(512)(128)(4,1)S(1)} %compare_and_fusion.1, f32[16,1536,192]{1,2,0:T(8,128)} %gather_fusion.8), kind=kLoop, calls=%fused_computation.19 | loop fusion | flops 9437184 | bytes 75497488 | tf_op jit(solution)/shard_map/jit(_take)/select_n | solution.py:93
  1200.0 207.4 %all_to_all.26 = f32[1536,16,192]{0,2,1:T(8,128)} all-to-all(f32[1536,16,192]{0,2,1:T(8,128)S(1)} %get-tuple-element.48), channel_id=1, replica_groups=mesh['pair'=4,'slab'=8] {'pair'}, dimensions={1} | all-to-all | bytes 37748736 | tf_op jit(solution)/shard_map/all_to_all | solution.py:121
  1418.3 15.8 gather_fusion.10
  1458.5 157.6 %all-to-all-done.4 = f32[1536,16,192]{0,2,1:T(8,128)} async-done(((f32[1536,16,192]{0,2,1:T(8,128)}), f32[1536,16,192]{0,2,1:T(8,128)}, u32[]{:S(2)}, u32[]{:S(2)}) %all-to-all-start.4) | async-done | bytes 18874400 | tf_op jit(solution)/shard_map/all_to_all | solution.py:122
  1616.1 16.0 gather_fusion.14
  1632.1 13.0 broadcast_select_fusion
  1645.2 31.0 %psum.31 = f32[8,384]{1,0:T(8,128)S(1)} all-reduce(f32[8,384]{1,0:T(8,128)S(1)} %reduce_sum.44), channel_id=1, replica_groups=mesh['pair'=4,'slab'=8] {'slab'}, use_global_device_ids=true, to_apply=%region_19.23 | all-reduce | flops 3072 | bytes 24576 | tf_op jit(solution)/shard_map/psum | solution.py:126
  1694.9 35.7 %fusion.9 = f32[8,384,1536]{2,1,0:T(8,128)} fusion(f32[1536,8,384]{0,2,1:T(8,128)S(1)} %bitcast.70, f32[8,192,192]{2,1,0:T(8,128)S(1)} %multiply_add_fusion, f32[8,192,192]{2,1,0:T(8,128)S(1)} %fusion.20, f32[8,192,192]{2,1,0:T(8,128)} %convolution_negate_fusion, f32[8,192,192]{2,1,0:T(8,128)S(1)} %multiply_add_fusion.1), kind=kOutput, calls=%fused_computation.38 | convolution fusion | flops 21746810880 | bytes 42467328 | tf_op jit(solution)/shard_map/npk,pkj->npj/dot_general | solution.py:43
  1730.6 18.6 %copy.32 = f32[1536,3072]{1,0:T(8,128)} copy(f32[1536,3072]{0,1:T(8,128)} %bitcast.81) | data formatting | bytes 37748736
  1749.2 36.8 %fusion.8 = f32[8,384,1536]{2,1,0:T(8,128)} fusion(f32[1536,8,384]{0,2,1:T(8,128)} %bitcast.78, f32[8,192,192]{2,1,0:T(8,128)S(1)} %multiply_add_fusion, f32[8,192,192]{2,1,0:T(8,128)} %copy-done.4, f32[8,192,192]{2,1,0:T(8,128)} %convolution_negate_fusion, f32[8,192,192]{2,1,0:T(8,128)S(1)} %multiply_add_fusion.1), kind=kOutput, calls=%fused_computation.37 | convolution fusion | flops 21746810880 | bytes 42467328 | tf_op jit(solution)/shard_map/npk,pkj->npj/dot_general | solution.py:43
  1786.0 18.6 %copy.33 = f32[1536,3072]{1,0:T(8,128)} copy(f32[1536,3072]{0,1:T(8,128)} %bitcast.80) | data formatting | bytes 37748736
  (145 shorter events, 145.5 us)
Async XLA Ops:
  53.6 412.1 %all-to-all-start = ((f32[32,48,3072]{2,1,0:T(8,128)}), f32[32,48,3072]{2,1,0:T(8,128)}, u32[]{:S(2)}, u32[]{:S(2)}) async-start(f32[32,48,3072]{2,1,0:T(8,128)} %broadcast_select_fusion.5), calls=%async_computation | async-start | bytes 37748736 | tf_op jit(solution)/shard_map/all_to_all | solution.py:117
  60.6 18.7 %copy-start.10 = (s32[2,64]{1,0:T(2,128)S(1)}, s32[2,64]{1,0:T(2,128)}, u32[]{:S(2)}) copy-start(s32[2,64]{1,0:T(2,128)} %param.13) | copy-start | bytes 1540
  81.3 17.9 copy-start
  790.2 211.8 %all-to-all-start.3 = ((f32[1536,16,192]{0,2,1:T(8,128)}), f32[1536,16,192]{0,2,1:T(8,128)}, u32[]{:S(2)}, u32[]{:S(2)}) async-start(f32[1536,16,192]{0,2,1:T(8,128)} %get-tuple-element.49), calls=%async_computation.3 | async-start | bytes 37748736 | tf_op jit(solution)/shard_map/all_to_all | solution.py:122
  798.0 258.4 %all-reduce.4.cloned.1.call-start = ((), (), s32[]{:S(2)}) async-start(), calls=%async_computation.5 | async-start | bytes 3145728 | tf_op jit(solution)/shard_map/psum | solution.py:126
  807.9 258.9 %copy-start.5 = (f32[192,192]{1,0:T(8,128)}, f32[192,192]{1,0:T(8,128)S(1)}, u32[]{:S(2)}) copy-start(f32[192,192]{1,0:T(8,128)S(1)} %fusion.14) | copy-start | bytes 442372
  831.4 6.9 copy-start.3
  1056.4 2.0 copy-start.8
  1058.4 16.6 slice-start.5
  1062.3 12.8 slice-start.6
  1064.2 10.8 slice-start.7
  1066.8 8.3 slice-start.8
  1068.7 6.4 slice-start.9
  1407.4 7.7 copy-start.9
  1407.4 7.7 copy-start.1
  1407.4 208.7 %all-to-all-start.4 = ((f32[1536,16,192]{0,2,1:T(8,128)}), f32[1536,16,192]{0,2,1:T(8,128)}, u32[]{:S(2)}, u32[]{:S(2)}) async-start(f32[1536,16,192]{0,2,1:T(8,128)} %get-tuple-element.47), calls=%async_computation.4 | async-start | bytes 37748736 | tf_op jit(solution)/shard_map/all_to_all | solution.py:122
  1415.0 261.3 %all-reduce.6.cloned.1.call-start = ((), (), s32[]{:S(2)}) async-start(), calls=%async_computation.6 | async-start | bytes 3145728 | tf_op jit(solution)/shard_map/psum | solution.py:126
  1441.7 6.9 copy-start.2
  1676.3 2.0 copy-start.7
  1678.3 3.9 copy-start.6
  1678.3 16.6 slice-start
  1682.2 12.7 slice-start.1
  1684.0 10.8 slice-start.2
  1686.6 8.2 slice-start.3
  1688.5 6.3 slice-start.4
  1691.8 3.0 copy-start.4
Sparse Core Ops, SparseCore 0:
  848.2 63.7 all-reduce.3
  1458.6 63.8 all-reduce.5
where the time goes:
time: 1830 us; the launch traced here: 1810 us
  waiting for transfers between devices  675 us (37%)
  blocking collectives  482 us (26%)
  local copies, waits for them, and re-layouts  283 us (15%)
  matrix products  198 us (11%)
  other arithmetic  136 us (7%)
  starting transfers between devices  22.5 us (1%)
    all_to_all x2, blocking collectives, block_mover(): lax.all_to_all(r_sent, 'pair', split_axis=1, concat_axis=1, tiled=True)  418 us
    all_to_all x1, waiting for transfers between devices, send_natural(): lax.all_to_all(packed, 'slab', split_axis=0, concat_axis=0, tiled=True)  363 us
    all_to_all x2, waiting for transfers between devices, block_mover(): lax.all_to_all(v_sent, 'pair', split_axis=1, concat_axis=1, tiled=True)  312 us
    dot_general x4, matrix products, rotate(): return jnp.einsum('npk,pkj->npj', paired, turns, precision=HIGH)  145 us
    unnamed x48, local copies, waits for them, and re-layouts  71.8 us
    psum x2, blocking collectives, block_summer(): return lax.psum((cross_gram, squares), 'slab')  56.3 us
    another operation x2, local copies, waits for them, and re-layouts, column_pass(): r_slots = r_local.reshape(row_count, local_count, BLK)  48.8 us
    select_n x2, other arithmetic, column_pass(): v_sent = jnp.take(v_slots, outgoing, axis=1)  42 us
  transfers between devices with their start and end apart: 5, of which 3 were waited for; matrix products, arithmetic and copies ran while one was open for 10% of the time, Pallas kernels for 0%

commit v1 on v0

v1 whole, which is shorter than its diff:
```python
import functools

import jax
import jax.numpy as jnp
from jax import lax
from jax.experimental import pallas as pl
from jax.experimental.pallas import tpu as pltpu
from jax.sharding import PartitionSpec as P

BLK = 192
ROWB = 48
WIN = 256
EPSILON = 1e-06
HIGH = lax.Precision.HIGH
VMEM_LIMIT = 48 * 1024 * 1024


def rotations(cross_gram, norms_a, norms_b):
    width = cross_gram.shape[-1]
    scale_a = lax.rsqrt(norms_a)
    scale_b = lax.rsqrt(norms_b)
    normed = cross_gram * scale_a[:, :, None] * scale_b[:, None, :]
    frobenius = jnp.sqrt(jnp.sum(normed * normed, axis=(1, 2)))
    coupling = normed / (1.0 + frobenius)[:, None, None]
    outer_a = jnp.einsum("pik,pjk->pij", coupling, coupling, precision=HIGH)
    outer_b = jnp.einsum("pki,pkj->pij", coupling, coupling, precision=HIGH)
    identity = jnp.eye(width, dtype=cross_gram.dtype)
    left_poly = (
        identity
        - 0.5 * outer_a
        + 0.375 * jnp.einsum("pik,pkj->pij", outer_a, outer_a, precision=HIGH)
    )
    right_poly = (
        identity
        - 0.5 * outer_b
        + 0.375 * jnp.einsum("pik,pkj->pij", outer_b, outer_b, precision=HIGH)
    )
    upper_half = jnp.concatenate(
        [left_poly, -jnp.einsum("pik,pkj->pij", coupling, right_poly, precision=HIGH)], axis=2
    )
    lower_half = jnp.concatenate(
        [jnp.einsum("pki,pkj->pij", coupling, left_poly, precision=HIGH), right_poly], axis=2
    )
    return jnp.concatenate([upper_half, lower_half], axis=1)


def turns_of(sums):
    cross_gram = sums[:, :BLK, :BLK]
    norms_a = sums[:, BLK, :BLK] + EPSILON
    norms_b = sums[:, BLK + 1, :BLK] + EPSILON
    return rotations(cross_gram, norms_a, norms_b)


def move_tables(place, me, groups, count):
    total = place.shape[0]
    units = count // groups
    slots = jnp.arange(total, dtype=jnp.int32)
    source, local = place // count, place % count
    target = slots // count
    same = (target[:, None] == target[None, :]) & (source[:, None] == source[None, :])
    rank = jnp.sum((same & (slots[None, :] < slots[:, None])).astype(jnp.int32), axis=1)
    offset = jnp.arange(groups, dtype=jnp.int32)
    unit = jnp.arange(units, dtype=jnp.int32)
    chosen = (
        (source == me)[None, None, :]
        & (target[None, None, :] == (me ^ offset)[:, None, None])
        & (rank[None, None, :] == unit[None, :, None])
    )
    send = jnp.sum(jnp.where(chosen, local[None, None, :], 0), axis=2).reshape(groups * units)
    mine = lax.dynamic_slice_in_dim(source ^ me, me * count, count)
    order = lax.dynamic_slice_in_dim(rank, me * count, count)
    return send, mine, order


def rank_among(kind):
    index = jnp.arange(kind.shape[-1], dtype=jnp.int32)
    same = (kind[..., :, None] == kind[..., None, :]) & (index[None, :] < index[:, None])
    return jnp.sum(same.astype(jnp.int32), axis=-1)


def shifted(window, left):
    return pltpu.roll(window, WIN - 64 if left else 64, 1)


def low_half(window, odd):
    return jnp.where(odd == 1, shifted(window, True), window)


def merge(first, first_odd, second, second_odd):
    a = low_half(first, first_odd)
    b = jnp.where(second_odd == 1, second, shifted(second, False))
    lane = lax.broadcasted_iota(jnp.int32, (first.shape[0], 128), 1)
    middle = jnp.where(lane < 64, a[:, 128:], b[:, :128])
    return jnp.concatenate([a[:, :128], middle, b[:, 128:]], axis=1)


def unit_width(units):
    return max(WIN, units * BLK)


def pack_kernel(groups, units, blocks, send, rows_at, *refs):
    sources, outs = refs[:blocks], refs[blocks:]
    size = sources[0].shape[0]
    for i, x_ref in enumerate(sources):
        rows = slice(i * size, (i + 1) * size)

        def window(place):
            block = send[place]
            strip = (3 * block) // 2
            return x_ref[:, pl.ds(pl.multiple_of(strip * 128, 128), WIN)], block % 2

        for group in range(groups):
            if units == 1:
                w, odd = window(group)
                outs[group][rows, :] = low_half(w, odd)
            for j in range(0, units - 1, 2):
                w0, odd0 = window(group * units + j)
                w1, odd1 = window(group * units + j + 1)
                outs[group][rows, BLK * j : BLK * (j + 2)] = merge(w0, odd0, w1, odd1)


def pack(x, send, rows_at, block_rows, groups, units):
    total = rows_at.shape[0]
    blocks = 4 if total % 4 == 0 else 1
    width = unit_width(units)

    def block_at(k):
        return pl.BlockSpec(
            (block_rows, x.shape[1]), lambda i, send, at: (at[i * blocks + k], 0)
        )

    return pl.pallas_call(
        functools.partial(pack_kernel, groups, units, blocks),
        grid_spec=pltpu.PrefetchScalarGridSpec(
            num_scalar_prefetch=2,
            grid=(total // blocks,),
            in_specs=[block_at(k) for k in range(blocks)],
            out_specs=[pl.BlockSpec((blocks * block_rows, width), lambda i, *_: (i, 0))]
            * groups,
        ),
        out_shape=[jax.ShapeDtypeStruct((total * block_rows, width), jnp.float32)] * groups,
        compiler_params=pltpu.CompilerParams(vmem_limit_bytes=VMEM_LIMIT),
        cost_estimate=pl.CostEstimate(
            flops=0,
            bytes_accessed=2 * 4 * total * block_rows * x.shape[1],
            transcendentals=0,
        ),
        name="pack",
    )(send, rows_at, *[x] * blocks)


def halves(x):
    high = x.astype(jnp.bfloat16)
    return high, (x - high.astype(jnp.float32)).astype(jnp.bfloat16)


def product(a, b, dims):
    (ah, al), (bh, bl) = a, b
    dot = functools.partial(
        lax.dot_general, dimension_numbers=(dims, ((), ())), preferred_element_type=jnp.float32
    )
    return dot(ah, bh) + (dot(al, bh) + dot(ah, bl))


def fetcher(arrive, order, sources, win, sems, row0, rows):
    def start(q, slot):
        for side in range(2):
            at = arrive[2 * q + side]
            strip = (3 * order[2 * q + side]) // 2
            for k, source in enumerate(sources):

                @pl.when(at == k)
                def _():
                    pltpu.make_async_copy(
                        source.at[
                            pl.ds(row0, rows), pl.ds(pl.multiple_of(strip * 128, 128), WIN)
                        ],
                        win.at[slot, side],
                        sems.at[slot, side],
                    ).start()

    def wait(slot):
        for side in range(2):
            pltpu.make_async_copy(
                sources[0].at[pl.ds(row0, rows), pl.ds(0, WIN)],
                win.at[slot, side],
                sems.at[slot, side],
            ).wait()

    return start, wait


def pipelined(start, wait):
    q, last = pl.program_id(0), pl.num_programs(0)
    slot = lax.rem(q, 2)

    @pl.when(q == 0)
    def _():
        start(0, 0)

    @pl.when(q + 1 < last)
    def _():
        start(q + 1, 1 - slot)

    wait(slot)
    return q, slot


def tile_of(rows):
    return 256 if rows % 256 == 0 else rows


def pair_tile(win, slot, start, tile):
    rows = pl.ds(pl.multiple_of(start, 8), tile)
    return jnp.concatenate([win[slot, 0, rows, :], win[slot, 1, rows, :]], axis=1)


def spread(turn, odd, other_odd):
    gap = jnp.zeros((WIN - BLK, 2 * BLK), jnp.float32)

    def placed(part, odd):
        return jnp.where(
            odd == 1, jnp.concatenate([gap, part]), jnp.concatenate([part, gap])
        )

    return jnp.concatenate([placed(turn[:BLK], odd), placed(turn[BLK:], other_odd)])


def long_halves(turn):
    high, low = halves(turn)
    return jnp.concatenate([high, high, low])


def turned_tile(x, long_turn):
    high, low = halves(x)
    return jnp.dot(
        jnp.concatenate([high, low, high], axis=1), long_turn, preferred_element_type=jnp.float32
    )


def gram_kernel(groups, arrive, order, *refs):
    sources, (out, win, sems) = refs[:groups], refs[groups:]
    rows = win.shape[2]
    q, slot = pipelined(*fetcher(arrive, order, sources, win, sems, 0, rows))
    tile = tile_of(rows)
    total = jnp.zeros((WIN, WIN), jnp.float32)
    squares = jnp.zeros((8, 2 * WIN), jnp.float32)
    for step in range(rows // tile):
        x = pair_tile(win, slot, step * tile, tile)
        high, low = halves(x)
        total += product(
            (high[:, :WIN], low[:, :WIN]), (high[:, WIN:], low[:, WIN:]), ((0,), (0,))
        )
        squares += jnp.sum((x * x).reshape(tile // 8, 8, 2 * WIN), axis=0)
    odd, other_odd = order[2 * q] % 2, order[2 * q + 1] % 2
    total = jnp.where(odd == 1, total[WIN - BLK :], total[:BLK])
    out[0, :BLK, :] = low_half(total, other_odd)
    norms = jnp.broadcast_to(jnp.sum(squares, axis=0, keepdims=True), (8, 2 * WIN))
    row = lax.broadcasted_iota(jnp.int32, (8, WIN), 0)
    out[0, BLK:, :] = jnp.where(
        row == 0, low_half(norms[:, :WIN], odd), low_half(norms[:, WIN:], other_odd)
    )


def gram(sources, arrive, order):
    groups, rows = len(sources), sources[0].shape[0]
    pairs = arrive.shape[0] // 2
    return pl.pallas_call(
        functools.partial(gram_kernel, groups),
        grid_spec=pltpu.PrefetchScalarGridSpec(
            num_scalar_prefetch=2,
            grid=(pairs,),
            in_specs=[pl.BlockSpec(memory_space=pl.ANY)] * groups,
            out_specs=pl.BlockSpec((1, BLK + 8, WIN), lambda q, *_: (q, 0, 0)),
            scratch_shapes=[
                pltpu.VMEM((2, 2, rows, WIN), jnp.float32),
                pltpu.SemaphoreType.DMA((2, 2)),
            ],
        ),
        out_shape=jax.ShapeDtypeStruct((pairs, BLK + 8, WIN), jnp.float32),
        compiler_params=pltpu.CompilerParams(vmem_limit_bytes=VMEM_LIMIT),
        cost_estimate=pl.CostEstimate(
            flops=6 * pairs * rows * WIN * WIN,
            bytes_accessed=8 * pairs * rows * WIN,
            transcendentals=0,
        ),
        name="cross_products",
    )(arrive, order, *sources)


def rotate_kernel(groups, row0, given, arrive, order, *refs):
    sources, turn = refs[:groups], refs[groups]
    out, win, sems = refs[groups + 1 + given :]
    rows = win.shape[2]
    q, slot = pipelined(*fetcher(arrive, order, sources, win, sems, row0, rows))
    tile = tile_of(rows)
    long_turn = long_halves(spread(turn[0], order[2 * q] % 2, order[2 * q + 1] % 2))
    for step in range(rows // tile):
        x = pair_tile(win, slot, step * tile, tile)
        out[step * tile : (step + 1) * tile, :] = turned_tile(x, long_turn)


def rotate(sources, arrive, order, turns, row0, rows, into=None, shape=None, at=0):
    groups = len(sources)
    pairs = arrive.shape[0] // 2
    shape = shape or (rows, pairs * 2 * BLK)
    given = [] if into is None else [into]
    return pl.pallas_call(
        functools.partial(rotate_kernel, groups, row0, len(given)),
        grid_spec=pltpu.PrefetchScalarGridSpec(
            num_scalar_prefetch=2,
            grid=(pairs,),
            in_specs=[pl.BlockSpec(memory_space=pl.ANY)] * groups
            + [pl.BlockSpec((1, 2 * BLK, 2 * BLK), lambda q, *_: (q, 0, 0))]
            + [pl.BlockSpec(memory_space=pl.ANY)] * len(given),
            out_specs=pl.BlockSpec((rows, 2 * BLK), lambda q, *_: (at, q)),
            scratch_shapes=[
                pltpu.VMEM((2, 2, rows, WIN), jnp.float32),
                pltpu.SemaphoreType.DMA((2, 2)),
            ],
        ),
        out_shape=jax.ShapeDtypeStruct(shape, jnp.float32),
        input_output_aliases={groups + 3: 0} if given else {},
        compiler_params=pltpu.CompilerParams(vmem_limit_bytes=VMEM_LIMIT),
        cost_estimate=pl.CostEstimate(
            flops=6 * pairs * rows * 4 * BLK * BLK,
            bytes_accessed=4 * pairs * rows * (2 * WIN + 2 * BLK),
            transcendentals=0,
        ),
        name="rotate",
    )(arrive, order, *sources, turns, *given)


def slab_pack_kernel(groups, *refs):
    sources, (out, held, in_sems, out_sems) = refs[:groups], refs[groups:]
    slabs, rows, _ = out.shape
    width = sources[0].shape[1]
    arrivals = []
    for o in range(slabs):
        for g in range(groups):
            copy = pltpu.make_async_copy(
                sources[g].at[pl.ds(o * rows, rows), :],
                held.at[o, :, pl.ds(g * width, width)],
                in_sems.at[o, g],
            )
            copy.start()
            arrivals.append(copy)
    departures = []
    for o in range(slabs):
        for copy in arrivals[o * groups : (o + 1) * groups]:
            copy.wait()
        copy = pltpu.make_async_copy(held.at[o], out.at[o], out_sems.at[o])
        copy.start()
        departures.append(copy)
    for copy in departures:
        copy.wait()


def slab_pack(sources, slabs):
    groups = len(sources)
    rows, width = sources[0].shape[0] // slabs, sources[0].shape[1]
    shape = (slabs, rows, groups * width)
    return pl.pallas_call(
        functools.partial(slab_pack_kernel, groups),
        in_specs=[pl.BlockSpec(memory_space=pl.ANY)] * groups,
        out_specs=pl.BlockSpec(memory_space=pl.ANY),
        scratch_shapes=[
            pltpu.VMEM(shape, jnp.float32),
            pltpu.SemaphoreType.DMA((slabs, groups)),
            pltpu.SemaphoreType.DMA((slabs,)),
        ],
        out_shape=jax.ShapeDtypeStruct(shape, jnp.float32),
        compiler_params=pltpu.CompilerParams(vmem_limit_bytes=VMEM_LIMIT),
        cost_estimate=pl.CostEstimate(
            flops=0, bytes_accessed=8 * slabs * rows * groups * width, transcendentals=0
        ),
        name="slab_pack",
    )(*sources)


def settle_kernel(strips, given, arrive, order, natural, source, turn, *refs):
    out, win, done, sems, out_sems = refs[given:]
    rows = source.shape[0]

    def start(q, slot):
        for side in range(2):
            strip = arrive[2 * q + side] * strips + (3 * order[2 * q + side]) // 2
            columns = pl.ds(pl.multiple_of(strip * 128, 128), WIN)
            pltpu.make_async_copy(
                source.at[:, columns], win.at[slot, side], sems.at[slot, side]
            ).start()

    def wait(slot):
        for side in range(2):
            pltpu.make_async_copy(
                source.at[:, pl.ds(0, WIN)], win.at[slot, side], sems.at[slot, side]
            ).wait()

    q, slot = pipelined(start, wait)
    tile = tile_of(rows)
    long_turn = long_halves(spread(turn[0], order[2 * q] % 2, order[2 * q + 1] % 2))

    def written(at):
        pltpu.make_async_copy(done.at[at], done.at[at], out_sems.at[at]).wait()

    @pl.when(q >= 2)
    def _():
        written(slot)

    for step in range(rows // tile):
        x = pair_tile(win, slot, step * tile, tile)
        done[slot, step * tile : (step + 1) * tile, :] = turned_tile(x, long_turn)

    columns = pl.ds(pl.multiple_of(q * 2 * BLK, 128), 2 * BLK)
    for block in range(rows // ROWB):
        pltpu.make_async_copy(
            done.at[slot, pl.ds(block * ROWB, ROWB), :],
            out.at[pl.ds(pl.multiple_of(natural[block] * ROWB, 8), ROWB), columns],
            out_sems.at[slot],
        ).start()

    @pl.when(q == pl.num_programs(0) - 1)
    def _():
        written(slot)

        @pl.when(q >= 1)
        def _():
            written(1 - slot)


def settle(source, arrive, order, natural, turns, strips, shape, into=None):
    source = source.reshape(-1, source.shape[2])
    rows = source.shape[0]
    pairs = arrive.shape[0] // 2
    given = [] if into is None else [into]
    return pl.pallas_call(
        functools.partial(settle_kernel, strips, len(given)),
        grid_spec=pltpu.PrefetchScalarGridSpec(
            num_scalar_prefetch=3,
            grid=(pairs,),
            in_specs=[pl.BlockSpec(memory_space=pl.ANY)]
            + [pl.BlockSpec((1, 2 * BLK, 2 * BLK), lambda q, *_: (q, 0, 0))]
            + [pl.BlockSpec(memory_space=pl.ANY)] * len(given),
            out_specs=pl.BlockSpec(memory_space=pl.ANY),
            scratch_shapes=[
                pltpu.VMEM((2, 2, rows, WIN), jnp.float32),
                pltpu.VMEM((2, rows, 2 * BLK), jnp.float32),
                pltpu.SemaphoreType.DMA((2, 2)),
                pltpu.SemaphoreType.DMA((2,)),
            ],
        ),
        out_shape=jax.ShapeDtypeStruct(shape, jnp.float32),
        input_output_aliases={5: 0} if given else {},
        compiler_params=pltpu.CompilerParams(vmem_limit_bytes=VMEM_LIMIT),
        cost_estimate=pl.CostEstimate(
            flops=6 * pairs * rows * 4 * BLK * BLK,
            bytes_accessed=4 * pairs * rows * (2 * WIN + 2 * BLK),
            transcendentals=0,
        ),
        name="settle",
    )(arrive, order, natural, source, turns, *given)


def swap(arrays, axis):
    count = len(arrays)
    return [arrays[0]] + [
        lax.ppermute(arrays[o], axis, [(i, i ^ o) for i in range(count)]) for o in range(1, count)
    ]


def after(arrays, earlier):
    arrays, earlier = lax.optimization_barrier((list(arrays), list(earlier)))
    return arrays, earlier


def shards(groups, slabs, r_slabs, basis, owners, plan):
    rows = r_slabs.shape[0]
    count = r_slabs.shape[1] // BLK
    units = count // groups
    strips = unit_width(units) // 128
    row_blocks = owners.shape[0]
    each = row_blocks // slabs
    chunks = 2 if each % 2 == 0 else 1
    per = each // chunks
    part = rows // chunks
    pair_index = lax.axis_index("pair")
    slab_index = lax.axis_index("slab")

    send_0, arrive_0, order_0 = move_tables(plan[0], pair_index, groups, count)
    slot_ids = jnp.arange(plan.shape[1], dtype=jnp.int32)
    place_1 = jnp.sum(
        jnp.where(plan[0][None, :] == plan[1][:, None], slot_ids[None, :], 0), axis=1
    )
    send_1, arrive_1, order_1 = move_tables(place_1, pair_index, groups, count)

    goes_to = owners // row_blocks
    rank = rank_among(goes_to)
    spot = (rank // per) * (slabs * per) + goes_to * per + rank % per
    index = jnp.arange(row_blocks, dtype=jnp.int32)
    rows_at = jnp.sum(jnp.where(spot[None, :] == index[:, None], index[None, :], 0), axis=1)
    table = lax.all_gather(owners, "slab", axis=0, tiled=True).reshape(slabs, row_blocks)
    table_to = table // row_blocks
    table_rank = rank_among(table_to)
    per_rank = jnp.arange(each, dtype=jnp.int32)
    hit = (table_to == slab_index)[:, None, :] & (table_rank[:, None, :] == per_rank[None, :, None])
    where_to = jnp.sum(jnp.where(hit, (table % row_blocks)[:, None, :], 0), axis=2)
    natural = [
        where_to[:, c * per : (c + 1) * per].reshape(slabs * per) for c in range(chunks)
    ]

    steps = part // ROWB
    straight = [
        jnp.arange(steps, dtype=jnp.int32) + c * steps for c in range(chunks)
    ]

    def summed(*parts):
        return lax.psum(functools.reduce(jnp.add, parts), "slab")

    r_sent = pack(r_slabs, send_0, rows_at, ROWB, groups, units)
    r_got = swap(r_sent, "pair")
    v_sent = [pack(basis, send_0, straight[c], ROWB, groups, units) for c in range(chunks)]

    v_got = [None] * chunks
    v_sent[0], (r_got, natural) = after(v_sent[0], (r_got, natural))
    v_got[0] = swap(v_sent[0], "pair")
    turns = turns_of(summed(gram(r_got, arrive_0, order_0)))

    def second(sources, row0):
        turned = rotate(sources, arrive_0, order_0, turns, row0, part)
        return pack(turned, send_1, straight[0], ROWB, groups, units)

    r_two = []
    for c in range(chunks):
        sent = second(r_got, c * part)
        if c == 0:
            sent, v_got[0] = after(sent, v_got[0])
        else:
            sent, r_two[-1] = after(sent, r_two[-1])
        r_two.append(swap(sent, "pair"))
    for c in range(1, chunks):
        v_sent[c], r_two[-1] = after(v_sent[c], r_two[-1])
        v_got[c] = swap(v_sent[c], "pair")

    v_next = [second(v_got[0], 0)]
    packed = [slab_pack(r_two[c], slabs) for c in range(chunks)]
    sums = functools.reduce(jnp.add, [gram(r_two[c], arrive_1, order_1) for c in range(chunks)])
    (v_next[0], packed[1:], sums), v_got[-1] = after((v_next[0], packed[1:], sums), v_got[-1])
    r_home = [lax.all_to_all(packed[c], "slab", 0, 0, tiled=True) for c in range(chunks)]
    v_two = [swap(v_next[0], "pair")]
    turns_1 = turns_of(summed(sums))
    for c in range(1, chunks):
        sent, v_two[-1] = after(second(v_got[c], 0), v_two[-1])
        v_two.append(swap(sent, "pair"))

    r_out = v_out = None
    for c in range(chunks):
        if c > 0:
            (v_two[c], r_home[c]), (r_out, v_out) = after((v_two[c], r_home[c]), (r_out, v_out))
        r_out = settle(
            r_home[c], arrive_1, order_1, natural[c], turns_1, strips, r_slabs.shape, r_out
        )
        v_out = rotate(v_two[c], arrive_1, order_1, turns_1, 0, part, v_out, basis.shape, c)
    return r_out, v_out


def solution(mesh):
    placed = (P("slab", "pair"), P("slab", "pair"), P("slab"), P())
    return jax.shard_map(
        functools.partial(shards, mesh.shape["pair"], mesh.shape["slab"]),
        mesh=mesh,
        in_specs=placed,
        out_specs=(P("slab", "pair"), P("slab", "pair")),
        check_vma=False,
    )
```

time: 1830 us -> 1030 us (0.56)
  blocking collectives: 482 us -> 8.45 us
  local copies, waits for them, and re-layouts: 283 us -> 16.2 us
  Pallas kernels: 0 us -> 248 us
  matrix products: 198 us -> 18.5 us
  other arithmetic: 136 us -> 17.5 us
    all_to_all x3 -> x2, waiting for transfers between devices: 675 us -> 0.01 us  [shards(): lax.all_to_all(packed[c], 'slab', 0, 0, tiled=True)]
    ppermute x0 -> x21, waiting for transfers between devices: none -> 450 us  [swap(): lax.ppermute(arrays[o], axis, [(i, i ^ o) for i in range(count)])]
    all_to_all x2 -> x0, blocking collectives: 418 us -> none  [block_mover(): lax.all_to_all(r_sent, 'pair', split_axis=1, concat_axis=1, tiled=True)]
    pallas_call x0 -> x20, Pallas kernels: none -> 248 us  [the longest x6 103 us: rotate(): pl.pallas_call(functools.partial(rotate_kernel, groups, row0, len(given))...]
    psum x2, waiting for transfers between devices: 0.01 us -> 218 us  [summed(): return lax.psum(functools.reduce(jnp.add, parts), 'slab')]
    dot_general x6 -> x0, matrix products: 165 us -> none  [the longest x4 145 us: rotate(): return jnp.einsum('npk,pkj->npj', paired, turns, precision=HIGH)]
    gather x15 -> x0, local copies, waits for them, and re-layouts: 162 us -> none  [the longest x2 31.9 us: column_pass(): jnp.take(v_got, settle, axis=1)]
    select_n x17 -> x5, other arithmetic: 95 us -> 0.69 us  [the longest x1 0.66 us: shards(): goes_to = owners // row_blocks]
  transfers between devices with their start and end apart: 5 -> 25, of which waited for: 3 -> 13; matrix products, arithmetic and copies ran while one was open for 10% -> 3% of each run, Pallas kernels for 0% -> 17%
where the time goes in v1:
time: 1030 us
  waiting for transfers between devices  668 us (65%)
  Pallas kernels  248 us (24%)
  starting transfers between devices  36.2 us (4%)
  matrix products  18.5 us (2%)
  other arithmetic  17.5 us (2%)
  local copies, waits for them, and re-layouts  16.2 us (2%)
  between operations  15.3 us (1%)
    ppermute x21, waiting for transfers between devices, swap(): lax.ppermute(arrays[o], axis, [(i, i ^ o) for i in range(count)])  450 us
    psum x2, waiting for transfers between devices, summed(): return lax.psum(functools.reduce(jnp.add, parts), 'slab')  218 us
    pallas_call x6, Pallas kernels, rotate(): pl.pallas_call(functools.partial(rotate_kernel, groups, row0, len(given))...  103 us
    pallas_call x7, Pallas kernels, pack(): pl.pallas_call(functools.partial(pack_kernel, groups, units, blocks), gri...  68.7 us
    pallas_call x2, Pallas kernels, settle(): pl.pallas_call(functools.partial(settle_kernel, strips, len(given)), grid...  33.3 us
    pallas_call x3, Pallas kernels, gram(): pl.pallas_call(functools.partial(gram_kernel, groups), grid_spec=pltpu.Pr...  32.9 us
    ppermute x21, starting transfers between devices, swap(): lax.ppermute(arrays[o], axis, [(i, i ^ o) for i in range(count)])  24.5 us
  transfers between devices with their start and end apart: 25, of which 13 were waited for; matrix products, arithmetic and copies ran while one was open for 3% of the time, Pallas kernels for 17%

profile of v1, /device:TPU:8, one launch (start us, length us, event | category | flops | bytes accessed | tf_op | source)
XLA Modules:
  0.0 1027.8 jit_solution(17752916700971638726)
XLA Ops:
  11.1 16.4 %pack.8 = (f32[1536,768]{1,0:T(8,128)S(1)}, f32[1536,768]{1,0:T(8,128)}, f32[1536,768]{1,0:T(8,128)}, f32[1536,768]{1,0:T(8,128)}) custom-call(s32[16]{0:T(128)S(1)} %reshape.485.send, s32[32]{0:T(128)S(1)} %select_reduce_fusion.2.rows_at, f32[1536,3072]{1,0:T(8,128)} %refs_3_.4, f32[1536,3072]{1,0:T(8,128)} %refs_3_.4, f32[1536,3072]{1,0:T(8,128)} %refs_3_.4, ...), custom_call_target="tpu_custom_call" | custom-call | bytes 37748736 | tf_op jit(solution)/shard_map/pack/pallas_call | solution.py:132
  34.7 8.4 all-reduce
  44.0 9.2 pack.7
  54.7 79.9 %collective-permute-done.refs_1_ = f32[1536,768]{1,0:T(8,128)} collective-permute-done((f32[1536,768]{1,0:T(8,128)}, f32[1536,768]{1,0:T(8,128)}, u32[]{:S(2)}, u32[]{:S(2)}) %collective-permute-start) | collective-permute-done | bytes 4718624 | tf_op jit(solution)/shard_map/ppermute | solution.py:467
  134.6 101.2 %collective-permute-done.1.refs_2_ = f32[1536,768]{1,0:T(8,128)} collective-permute-done((f32[1536,768]{1,0:T(8,128)}, f32[1536,768]{1,0:T(8,128)}, u32[]{:S(2)}, u32[]{:S(2)}) %collective-permute-start.1) | collective-permute-done | bytes 4718624 | tf_op jit(solution)/shard_map/ppermute | solution.py:467
  235.9 14.5 %cross_products.3 = f32[8,200,256]{2,1,0:T(8,128)} custom-call(s32[16]{0:T(128)S(1)} %dynamic_slice.14.arrive, s32[16]{0:T(128)S(1)} %dynamic_slice.15.order, f32[1536,768]{1,0:T(8,128)} %copy-done.2, f32[1536,768]{1,0:T(8,128)} %collective-permute-done.refs_1_, f32[1536,768]{1,0:T(8,128)} %collective-permute-done.1.refs_2_, ...), custom_call_target="tpu_custom_call" | custom-call | flops 4831838208 | bytes 25165824 | tf_op jit(solution)/shard_map/cross_products/pallas_call | solution.py:268
  254.3 58.0 %all-reduce.4.cloned.1.call-done = f32[8,200,256]{2,1,0:T(8,128)} async-done(((f32[8,200,256]{2,1,0:T(8,128)}), f32[8,200,256]{2,1,0:T(8,128)}) %all-reduce.4.cloned.1.call-update) | async-done | bytes 1638416 | tf_op jit(solution)/shard_map/psum | solution.py:517
  327.5 17.2 %rotate.6.refs_0_.refs_1_.refs_2_.refs_3_ = f32[768,3072]{1,0:T(8,128)} custom-call(s32[16]{0:T(128)S(1)} %dynamic_slice.14.arrive, s32[16]{0:T(128)S(1)} %dynamic_slice.15.order, f32[1536,768]{1,0:T(8,128)S(1)} %bitcast.40, f32[1536,768]{1,0:T(8,128)} %collective-permute-done.refs_1_, f32[1536,768]{1,0:T(8,128)} %collective-permute-done.1.refs_2_, ...), custom_call_target="tpu_custom_call" | custom-call | flops 5435817984 | bytes 22020096 | tf_op jit(solution)/shard_map/rotate/pallas_call | solution.py:308
  344.8 8.3 pack.9
  358.2 17.1 %rotate.8.refs_0_.refs_1_.refs_2_.refs_3_ = f32[768,3072]{1,0:T(8,128)} custom-call(s32[16]{0:T(128)S(1)} %dynamic_slice.14.arrive, s32[16]{0:T(128)S(1)} %dynamic_slice.15.order, f32[1536,768]{1,0:T(8,128)S(1)} %bitcast.40, f32[1536,768]{1,0:T(8,128)} %collective-permute-done.refs_1_, f32[1536,768]{1,0:T(8,128)} %collective-permute-done.1.refs_2_, ...), custom_call_target="tpu_custom_call" | custom-call | flops 5435817984 | bytes 22020096 | tf_op jit(solution)/shard_map/rotate/pallas_call | solution.py:308
  375.3 8.3 pack.12
  386.3 22.5 %collective-permute-done.6.refs_1_ = f32[768,768]{1,0:T(8,128)S(1)} collective-permute-done((f32[768,768]{1,0:T(8,128)S(1)}, f32[768,768]{1,0:T(8,128)S(1)}, u32[]{:S(2)}, u32[]{:S(2)}) %collective-permute-start.6) | collective-permute-done | bytes 2359328 | tf_op jit(solution)/shard_map/ppermute | solution.py:467
  408.9 47.8 %collective-permute-done.7.refs_2_ = f32[768,768]{1,0:T(8,128)} collective-permute-done((f32[768,768]{1,0:T(8,128)}, f32[768,768]{1,0:T(8,128)}, u32[]{:S(2)}, u32[]{:S(2)}) %collective-permute-start.7) | collective-permute-done | bytes 2359328 | tf_op jit(solution)/shard_map/ppermute | solution.py:467
  463.2 6.0 all-to-all-start.1
  472.7 9.1 pack.11
  481.8 41.7 %collective-permute-done.9.refs_1_ = f32[768,768]{1,0:T(8,128)S(1)} collective-permute-done((f32[768,768]{1,0:T(8,128)}, f32[768,768]{1,0:T(8,128)S(1)}, u32[]{:S(2)}, u32[]{:S(2)}) %collective-permute-start.9) | collective-permute-done | bytes 2359328 | tf_op jit(solution)/shard_map/ppermute | solution.py:467
  524.0 50.3 %collective-permute-done.11.refs_3_ = f32[768,768]{1,0:T(8,128)} collective-permute-done((f32[768,768]{1,0:T(8,128)}, f32[768,768]{1,0:T(8,128)}, u32[]{:S(2)}, u32[]{:S(2)}) %collective-permute-start.11) | collective-permute-done | bytes 2359328 | tf_op jit(solution)/shard_map/ppermute | solution.py:467
  577.9 17.1 %rotate.7.refs_0_.refs_1_.refs_2_.refs_3_ = f32[768,3072]{1,0:T(8,128)} custom-call(s32[16]{0:T(128)S(1)} %dynamic_slice.14.arrive, s32[16]{0:T(128)S(1)} %dynamic_slice.15.order, f32[768,768]{1,0:T(8,128)S(1)} %copy-done.8, f32[768,768]{1,0:T(8,128)} %collective-permute-done.3.refs_1_, f32[768,768]{1,0:T(8,128)} %collective-permute-done.4.refs_2_, ...), custom_call_target="tpu_custom_call" | custom-call | flops 5435817984 | bytes 22020096 | tf_op jit(solution)/shard_map/rotate/pallas_call | solution.py:308
  595.0 8.4 pack.10
  606.2 9.3 cross_products.4
  620.6 9.1 cross_products.5
  631.1 46.6 %collective-permute-done.13.refs_2_ = f32[768,768]{1,0:T(8,128)} collective-permute-done((f32[768,768]{1,0:T(8,128)}, f32[768,768]{1,0:T(8,128)}, u32[]{:S(2)}, u32[]{:S(2)}) %collective-permute-start.13) | collective-permute-done | bytes 2359328 | tf_op jit(solution)/shard_map/ppermute | solution.py:467
  677.8 5.6 all-to-all-start
  686.9 17.5 %rotate.9.refs_0_.refs_1_.refs_2_.refs_3_ = f32[768,3072]{1,0:T(8,128)} custom-call(s32[16]{0:T(128)S(1)} %dynamic_slice.14.arrive, s32[16]{0:T(128)S(1)} %dynamic_slice.15.order, f32[768,768]{1,0:T(8,128)S(1)} %copy-done.12, f32[768,768]{1,0:T(8,128)} %collective-permute-done.12.refs_1_, f32[768,768]{1,0:T(8,128)} %collective-permute-done.13.refs_2_, ...), custom_call_target="tpu_custom_call" | custom-call | flops 5435817984 | bytes 22020096 | tf_op jit(solution)/shard_map/rotate/pallas_call | solution.py:308
  704.5 9.0 pack.13
  713.4 159.7 %all-reduce.6.cloned.1.call-done = f32[8,200,256]{2,1,0:T(8,128)} async-done(((f32[8,200,256]{2,1,0:T(8,128)}), f32[8,200,256]{2,1,0:T(8,128)}) %all-reduce.6.cloned.1.call-update) | async-done | bytes 1638416 | tf_op jit(solution)/shard_map/psum | solution.py:517
  891.8 17.3 %rotate.10.refs_5_ = f32[1536,3072]{1,0:T(8,128)} custom-call(s32[16]{0:T(128)S(1)} %dynamic_slice.12.arrive, s32[16]{0:T(128)S(1)} %dynamic_slice.13.order, f32[768,768]{1,0:T(8,128)S(1)} %copy-done.10, f32[768,768]{1,0:T(8,128)} %collective-permute-done.15.refs_1_, f32[768,768]{1,0:T(8,128)} %collective-permute-done.16.refs_2_, ...), custom_call_target="tpu_custom_call" | custom-call | flops 5435817984 | bytes 22020096 | tf_op jit(solution)/shard_map/rotate/pallas_call | solution.py:308
  909.2 16.6 %settle.2.refs_0_ = f32[1536,3072]{1,0:T(8,128)} custom-call(s32[16]{0:T(128)S(1)} %dynamic_slice.12.arrive, s32[16]{0:T(128)S(1)} %dynamic_slice.13.order, s32[16]{0:T(128)S(1)} %reshape.487.natural, f32[768,3072]{1,0:T(8,128)} %bitcast.4.source, f32[8,384,384]{2,1,0:T(8,128)S(1)} %copy-done), custom_call_target="tpu_custom_call" | custom-call | flops 5435817984 | bytes 22020096 | tf_op jit(solution)/shard_map/settle/pallas_call | solution.py:436
  925.7 8.3 collective-permute-done.18.refs_1_
  935.5 49.5 %collective-permute-done.19.refs_2_ = f32[768,768]{1,0:T(8,128)} collective-permute-done((f32[768,768]{1,0:T(8,128)}, f32[768,768]{1,0:T(8,128)}, u32[]{:S(2)}, u32[]{:S(2)}) %collective-permute-start.19) | collective-permute-done | bytes 2359328 | tf_op jit(solution)/shard_map/ppermute | solution.py:467
  987.4 16.7 %settle.3 = f32[1536,3072]{1,0:T(8,128)} custom-call(s32[16]{0:T(128)S(1)} %dynamic_slice.12.arrive, s32[16]{0:T(128)S(1)} %dynamic_slice.13.order, s32[16]{0:T(128)S(1)} %reshape.488.natural, f32[768,3072]{1,0:T(8,128)} %bitcast.5.source, f32[8,384,384]{2,1,0:T(8,128)S(1)} %copy-done.1, f32[1536,3072]{1,0:T(8,128)} %settle.2.refs_0_), custom_call_target="tpu_custom_call", output_to_operand_aliasing={{}: (5, {})} | custom-call | flops 5435817984 | bytes 22020096 | tf_op jit(solution)/shard_map/settle/pallas_call | solution.py:436
  1004.1 16.6 %rotate.11 = f32[1536,3072]{1,0:T(8,128)} custom-call(s32[16]{0:T(128)S(1)} %dynamic_slice.12.arrive, s32[16]{0:T(128)S(1)} %dynamic_slice.13.order, f32[768,768]{1,0:T(8,128)S(1)} %get-tuple-element.171.refs_0_, f32[768,768]{1,0:T(8,128)S(1)} %copy-done.14, f32[768,768]{1,0:T(8,128)} %collective-permute-done.19.refs_2_, ...), custom_call_target="tpu_custom_call", output_to_operand_aliasing={{}: (7, {})} | custom-call | flops 5435817984 | bytes 22020096 | tf_op jit(solution)/shard_map/rotate/pallas_call | solution.py:308
  (161 shorter events, 89.1 us)
Async XLA Ops:
  7.2 305.0 %all-reduce.4.cloned.1.call-start = ((), (), s32[]{:S(2)}) async-start(), calls=%async_computation.2 | async-start | bytes 3276800 | tf_op jit(solution)/shard_map/psum | solution.py:517
  11.1 22.2 %copy-start.21 = (u32[32]{0:T(128)S(1)}, u32[32]{0:T(128)}, u32[]{:S(2)}) copy-start(u32[32]{0:T(128)} %constant.136) | copy-start | bytes 388
  11.1 23.4 %copy-start.20 = (s32[32]{0:T(128)S(1)}, s32[32]{0:T(128)}, u32[]{:S(2)}) copy-start(s32[32]{0:T(128)} %param.6) | copy-start | bytes 388
  29.6 105.0 %collective-permute-start = (f32[1536,768]{1,0:T(8,128)}, f32[1536,768]{1,0:T(8,128)}, u32[]{:S(2)}, u32[]{:S(2)}) collective-permute-start(f32[1536,768]{1,0:T(8,128)} %get-tuple-element.94), channel_id=1, source_target_pairs={{0,8},{8,0},{16,24},{24,16},{1,9},{9,1},{17,25},{25,17},{2,10},{10... | collective-permute-start | bytes 14155784 | tf_op jit(solution)/shard_map/ppermute | solution.py:467
  31.2 204.7 %collective-permute-start.1 = (f32[1536,768]{1,0:T(8,128)}, f32[1536,768]{1,0:T(8,128)}, u32[]{:S(2)}, u32[]{:S(2)}) collective-permute-start(f32[1536,768]{1,0:T(8,128)} %get-tuple-element.95), channel_id=1, source_target_pairs={{0,16},{8,24},{16,0},{24,8},{1,17},{9,25},{17,1},{25,9},{2,18},{10... | collective-permute-start | bytes 14155784 | tf_op jit(solution)/shard_map/ppermute | solution.py:467
  32.7 203.2 %collective-permute-start.2 = (f32[1536,768]{1,0:T(8,128)}, f32[1536,768]{1,0:T(8,128)}, u32[]{:S(2)}, u32[]{:S(2)}) collective-permute-start(f32[1536,768]{1,0:T(8,128)} %get-tuple-element.96), channel_id=1, source_target_pairs={{0,24},{8,16},{16,8},{24,0},{1,25},{9,17},{17,9},{25,1},{2,26},{10... | collective-permute-start | bytes 14155784 | tf_op jit(solution)/shard_map/ppermute | solution.py:467
  250.7 102.4 %collective-permute-start.3 = (f32[768,768]{1,0:T(8,128)}, f32[768,768]{1,0:T(8,128)}, u32[]{:S(2)}, u32[]{:S(2)}) collective-permute-start(f32[768,768]{1,0:T(8,128)} %get-tuple-element.107), channel_id=1, source_target_pairs={{0,8},{8,0},{16,24},{24,16},{1,9},{9,1},{17,25},{25,17},{2,10},{10... | collective-permute-start | bytes 7077896 | tf_op jit(solution)/shard_map/ppermute | solution.py:467
  252.0 102.7 %collective-permute-start.4 = (f32[768,768]{1,0:T(8,128)}, f32[768,768]{1,0:T(8,128)}, u32[]{:S(2)}, u32[]{:S(2)}) collective-permute-start(f32[768,768]{1,0:T(8,128)} %get-tuple-element.108), channel_id=1, source_target_pairs={{0,16},{8,24},{16,0},{24,8},{1,17},{9,25},{17,1},{25,9},{2,18},{10... | collective-permute-start | bytes 7077896 | tf_op jit(solution)/shard_map/ppermute | solution.py:467
  252.8 101.9 %collective-permute-start.5 = (f32[768,768]{1,0:T(8,128)}, f32[768,768]{1,0:T(8,128)}, u32[]{:S(2)}, u32[]{:S(2)}) collective-permute-start(f32[768,768]{1,0:T(8,128)} %get-tuple-element.109), channel_id=1, source_target_pairs={{0,24},{8,16},{16,8},{24,0},{1,25},{9,17},{17,9},{25,1},{2,26},{10... | collective-permute-start | bytes 7077896 | tf_op jit(solution)/shard_map/ppermute | solution.py:467
  354.7 54.2 %collective-permute-start.6 = (f32[768,768]{1,0:T(8,128)S(1)}, f32[768,768]{1,0:T(8,128)S(1)}, u32[]{:S(2)}, u32[]{:S(2)}) collective-permute-start(f32[768,768]{1,0:T(8,128)S(1)} %get-tuple-element.127), channel_id=1, source_target_pairs={{0,8},{8,0},{16,24},{24,16},{1,9},{9,1},{17,25},{25,17},{2,10},{10... | collective-permute-start | bytes 7077896 | tf_op jit(solution)/shard_map/ppermute | solution.py:467
  355.3 101.4 %collective-permute-start.7 = (f32[768,768]{1,0:T(8,128)}, f32[768,768]{1,0:T(8,128)}, u32[]{:S(2)}, u32[]{:S(2)}) collective-permute-start(f32[768,768]{1,0:T(8,128)} %get-tuple-element.128), channel_id=1, source_target_pairs={{0,16},{8,24},{16,0},{24,8},{1,17},{9,25},{17,1},{25,9},{2,18},{10... | collective-permute-start | bytes 7077896 | tf_op jit(solution)/shard_map/ppermute | solution.py:467
  356.4 100.2 %collective-permute-start.8 = (f32[768,768]{1,0:T(8,128)}, f32[768,768]{1,0:T(8,128)}, u32[]{:S(2)}, u32[]{:S(2)}) collective-permute-start(f32[768,768]{1,0:T(8,128)} %get-tuple-element.129), channel_id=1, source_target_pairs={{0,24},{8,16},{16,8},{24,0},{1,25},{9,17},{17,9},{25,1},{2,26},{10... | collective-permute-start | bytes 7077896 | tf_op jit(solution)/shard_map/ppermute | solution.py:467
  463.2 214.6 %all-to-all-start.1 = ((f32[8,96,3072]{2,1,0:T(8,128)}), f32[8,96,3072]{2,1,0:T(8,128)}, u32[]{:S(2)}, u32[]{:S(2)}) async-start(f32[8,96,3072]{2,1,0:T(8,128)} %slab_pack.3), calls=%async_computation.1 | async-start | bytes 18874368 | tf_op jit(solution)/shard_map/all_to_all | solution.py:548
  469.2 54.3 %collective-permute-start.9 = (f32[768,768]{1,0:T(8,128)}, f32[768,768]{1,0:T(8,128)S(1)}, u32[]{:S(2)}, u32[]{:S(2)}) collective-permute-start(f32[768,768]{1,0:T(8,128)} %copy-done.16), channel_id=1, source_target_pairs={{0,8},{8,0},{16,24},{24,16},{1,9},{9,1},{17,25},{25,17},{2,10},{10... | collective-permute-start | bytes 7077896 | tf_op jit(solution)/shard_map/ppermute | solution.py:467
  470.2 53.8 %collective-permute-start.10 = (f32[768,768]{1,0:T(8,128)}, f32[768,768]{1,0:T(8,128)S(1)}, u32[]{:S(2)}, u32[]{:S(2)}) collective-permute-start(f32[768,768]{1,0:T(8,128)} %get-tuple-element.132), channel_id=1, source_target_pairs={{0,16},{8,24},{16,0},{24,8},{1,17},{9,25},{17,1},{25,9},{2,18},{10... | collective-permute-start | bytes 7077896 | tf_op jit(solution)/shard_map/ppermute | solution.py:467
  471.0 103.3 %collective-permute-start.11 = (f32[768,768]{1,0:T(8,128)}, f32[768,768]{1,0:T(8,128)}, u32[]{:S(2)}, u32[]{:S(2)}) collective-permute-start(f32[768,768]{1,0:T(8,128)} %get-tuple-element.133), channel_id=1, source_target_pairs={{0,24},{8,16},{16,8},{24,0},{1,25},{9,17},{17,9},{25,1},{2,26},{10... | collective-permute-start | bytes 7077896 | tf_op jit(solution)/shard_map/ppermute | solution.py:467
  472.7 105.3 %copy-start.8 = (f32[768,768]{1,0:T(8,128)S(1)}, f32[768,768]{1,0:T(8,128)}, u32[]{:S(2)}) copy-start(f32[768,768]{1,0:T(8,128)} %copy-done.7) | copy-start | bytes 7077892
  481.8 113.2 %copy-start.11 = (f32[768,768]{1,0:T(8,128)}, f32[768,768]{1,0:T(8,128)S(1)}, u32[]{:S(2)}) copy-start(f32[768,768]{1,0:T(8,128)S(1)} %get-tuple-element.146.refs_0_) | copy-start | bytes 7077892
  523.5 92.0 %copy-start.6 = (f32[768,768]{1,0:T(8,128)}, f32[768,768]{1,0:T(8,128)S(1)}, u32[]{:S(2)}) copy-start(f32[768,768]{1,0:T(8,128)S(1)} %collective-permute-done.9.refs_1_) | copy-start | bytes 7077892
  524.0 71.0 %copy-start.17 = (f32[768,768]{1,0:T(8,128)}, f32[768,768]{1,0:T(8,128)S(1)}, u32[]{:S(2)}) copy-start(f32[768,768]{1,0:T(8,128)S(1)} %collective-permute-done.10.refs_2_) | copy-start | bytes 7077892
  574.3 56.8 %collective-permute-start.12 = (f32[768,768]{1,0:T(8,128)}, f32[768,768]{1,0:T(8,128)}, u32[]{:S(2)}, u32[]{:S(2)}) collective-permute-start(f32[768,768]{1,0:T(8,128)} %get-tuple-element.143), channel_id=1, source_target_pairs={{0,8},{8,0},{16,24},{24,16},{1,9},{9,1},{17,25},{25,17},{2,10},{10... | collective-permute-start | bytes 7077896 | tf_op jit(solution)/shard_map/ppermute | solution.py:467
  575.0 102.8 %collective-permute-start.13 = (f32[768,768]{1,0:T(8,128)}, f32[768,768]{1,0:T(8,128)}, u32[]{:S(2)}, u32[]{:S(2)}) collective-permute-start(f32[768,768]{1,0:T(8,128)} %get-tuple-element.144), channel_id=1, source_target_pairs={{0,16},{8,24},{16,0},{24,8},{1,17},{9,25},{17,1},{25,9},{2,18},{10... | collective-permute-start | bytes 7077896 | tf_op jit(solution)/shard_map/ppermute | solution.py:467
  576.5 101.3 %collective-permute-start.14 = (f32[768,768]{1,0:T(8,128)}, f32[768,768]{1,0:T(8,128)}, u32[]{:S(2)}, u32[]{:S(2)}) collective-permute-start(f32[768,768]{1,0:T(8,128)} %get-tuple-element.145), channel_id=1, source_target_pairs={{0,24},{8,16},{16,8},{24,0},{1,25},{9,17},{17,9},{25,1},{2,26},{10... | collective-permute-start | bytes 7077896 | tf_op jit(solution)/shard_map/ppermute | solution.py:467
  677.8 307.3 %all-to-all-start = ((f32[8,96,3072]{2,1,0:T(8,128)}), f32[8,96,3072]{2,1,0:T(8,128)}, u32[]{:S(2)}, u32[]{:S(2)}) async-start(f32[8,96,3072]{2,1,0:T(8,128)} %slab_pack.2), calls=%async_computation | async-start | bytes 18874368 | tf_op jit(solution)/shard_map/all_to_all | solution.py:548
  683.4 189.7 %all-reduce.6.cloned.1.call-start = ((), (), s32[]{:S(2)}) async-start(), calls=%async_computation.3 | async-start | bytes 3276800 | tf_op jit(solution)/shard_map/psum | solution.py:517
  683.4 196.3 %collective-permute-start.15 = (f32[768,768]{1,0:T(8,128)}, f32[768,768]{1,0:T(8,128)}, u32[]{:S(2)}, u32[]{:S(2)}) collective-permute-start(f32[768,768]{1,0:T(8,128)} %copy-done.15), channel_id=1, source_target_pairs={{0,8},{8,0},{16,24},{24,16},{1,9},{9,1},{17,25},{25,17},{2,10},{10... | collective-permute-start | bytes 7077896 | tf_op jit(solution)/shard_map/ppermute | solution.py:467
  685.0 194.7 %collective-permute-start.16 = (f32[768,768]{1,0:T(8,128)}, f32[768,768]{1,0:T(8,128)}, u32[]{:S(2)}, u32[]{:S(2)}) collective-permute-start(f32[768,768]{1,0:T(8,128)} %get-tuple-element.156), channel_id=1, source_target_pairs={{0,16},{8,24},{16,0},{24,8},{1,17},{9,25},{17,1},{25,9},{2,18},{10... | collective-permute-start | bytes 7077896 | tf_op jit(solution)/shard_map/ppermute | solution.py:467
  685.6 194.1 %collective-permute-start.17 = (f32[768,768]{1,0:T(8,128)}, f32[768,768]{1,0:T(8,128)}, u32[]{:S(2)}, u32[]{:S(2)}) collective-permute-start(f32[768,768]{1,0:T(8,128)} %get-tuple-element.157), channel_id=1, source_target_pairs={{0,24},{8,16},{16,8},{24,0},{1,25},{9,17},{17,9},{25,1},{2,26},{10... | collective-permute-start | bytes 7077896 | tf_op jit(solution)/shard_map/ppermute | solution.py:467
  879.7 54.4 %collective-permute-start.18 = (f32[768,768]{1,0:T(8,128)}, f32[768,768]{1,0:T(8,128)S(1)}, u32[]{:S(2)}, u32[]{:S(2)}) collective-permute-start(f32[768,768]{1,0:T(8,128)} %get-tuple-element.159), channel_id=1, source_target_pairs={{0,8},{8,0},{16,24},{24,16},{1,9},{9,1},{17,25},{25,17},{2,10},{10... | collective-permute-start | bytes 7077896 | tf_op jit(solution)/shard_map/ppermute | solution.py:467
  881.2 103.8 %collective-permute-start.19 = (f32[768,768]{1,0:T(8,128)}, f32[768,768]{1,0:T(8,128)}, u32[]{:S(2)}, u32[]{:S(2)}) collective-permute-start(f32[768,768]{1,0:T(8,128)} %get-tuple-element.160), channel_id=1, source_target_pairs={{0,16},{8,24},{16,0},{24,8},{1,17},{9,25},{17,1},{25,9},{2,18},{10... | collective-permute-start | bytes 7077896 | tf_op jit(solution)/shard_map/ppermute | solution.py:467
  882.4 102.6 %collective-permute-start.20 = (f32[768,768]{1,0:T(8,128)}, f32[768,768]{1,0:T(8,128)}, u32[]{:S(2)}, u32[]{:S(2)}) collective-permute-start(f32[768,768]{1,0:T(8,128)} %get-tuple-element.161), channel_id=1, source_target_pairs={{0,24},{8,16},{16,8},{24,0},{1,25},{9,17},{17,9},{25,1},{2,26},{10... | collective-permute-start | bytes 7077896 | tf_op jit(solution)/shard_map/ppermute | solution.py:467
  891.8 17.3 %copy-start = (f32[8,384,384]{2,1,0:T(8,128)S(1)}, f32[8,384,384]{2,1,0:T(8,128)}, u32[]{:S(2)}) copy-start(f32[8,384,384]{2,1,0:T(8,128)} %maximum_maximum_fusion.1.turn.refs_4_) | copy-start | bytes 14155780
  (17 other events, 65.6 us)
Sparse Core Ops, SparseCore 0:
  250.5 61.6 all-reduce.3
  687.0 186.0 all-reduce.5

commit v2 on v1

--- a/solution.py
+++ b/solution.py
@@ -207,7 +207,7 @@
 
 
 def tile_of(rows):
-    return 256 if rows % 256 == 0 else rows
+    return 384 if rows % 384 == 0 else rows
 
 
 def pair_tile(win, slot, start, tile):
@@ -329,6 +329,29 @@
         ),
         name="rotate",
     )(arrive, order, *sources, turns, *given)
+
+
+def gather_kernel(rows_at, x_ref, out):
+    out[0] = x_ref[...]
+
+
+def gather_rows(x, rows_at):
+    count = rows_at.shape[0]
+    return pl.pallas_call(
+        gather_kernel,
+        grid_spec=pltpu.PrefetchScalarGridSpec(
+            num_scalar_prefetch=1,
+            grid=(count,),
+            in_specs=[pl.BlockSpec((ROWB, x.shape[1]), lambda i, at: (at[i], 0))],
+            out_specs=pl.BlockSpec((1, ROWB, x.shape[1]), lambda i, at: (i, 0, 0)),
+        ),
+        out_shape=jax.ShapeDtypeStruct((count, ROWB, x.shape[1]), jnp.float32),
+        compiler_params=pltpu.CompilerParams(vmem_limit_bytes=VMEM_LIMIT),
+        cost_estimate=pl.CostEstimate(
+            flops=0, bytes_accessed=8 * count * ROWB * x.shape[1], transcendentals=0
+        ),
+        name="gather_rows",
+    )(rows_at, x)
 
 
 def slab_pack_kernel(groups, *refs):
@@ -378,23 +401,25 @@
     )(*sources)
 
 
-def settle_kernel(strips, given, arrive, order, natural, source, turn, *refs):
-    out, win, done, sems, out_sems = refs[given:]
-    rows = source.shape[0]
-
-    def start(q, slot):
-        for side in range(2):
-            strip = arrive[2 * q + side] * strips + (3 * order[2 * q + side]) // 2
-            columns = pl.ds(pl.multiple_of(strip * 128, 128), WIN)
-            pltpu.make_async_copy(
-                source.at[:, columns], win.at[slot, side], sems.at[slot, side]
-            ).start()
-
-    def wait(slot):
-        for side in range(2):
-            pltpu.make_async_copy(
-                source.at[:, pl.ds(0, WIN)], win.at[slot, side], sems.at[slot, side]
-            ).wait()
+def settle_kernel(groups, strips, given, arrive, order, natural, *refs):
+    sources, turn = refs[:groups], refs[groups]
+    out, win, done, sems, out_sems = refs[groups + 1 + given :]
+    rows = win.shape[2]
+    if groups == 1:
+        source = sources[0]
+
+        def start(q, slot):
+            for side in range(2):
+                strip = arrive[2 * q + side] * strips + (3 * order[2 * q + side]) // 2
+                pltpu.make_async_copy(
+                    source.at[:, pl.ds(pl.multiple_of(strip * 128, 128), WIN)],
+                    win.at[slot, side],
+                    sems.at[slot, side],
+                ).start()
+
+        _, wait = fetcher(arrive, order, sources, win, sems, 0, rows)
+    else:
+        start, wait = fetcher(arrive, order, sources, win, sems, 0, rows)
 
     q, slot = pipelined(start, wait)
     tile = tile_of(rows)
@@ -428,17 +453,16 @@
             written(1 - slot)
 
 
-def settle(source, arrive, order, natural, turns, strips, shape, into=None):
-    source = source.reshape(-1, source.shape[2])
-    rows = source.shape[0]
+def settle(sources, arrive, order, natural, turns, strips, shape, into=None):
+    groups, rows = len(sources), sources[0].shape[0]
     pairs = arrive.shape[0] // 2
     given = [] if into is None else [into]
     return pl.pallas_call(
-        functools.partial(settle_kernel, strips, len(given)),
+        functools.partial(settle_kernel, groups, strips, len(given)),
         grid_spec=pltpu.PrefetchScalarGridSpec(
             num_scalar_prefetch=3,
             grid=(pairs,),
-            in_specs=[pl.BlockSpec(memory_space=pl.ANY)]
+            in_specs=[pl.BlockSpec(memory_space=pl.ANY)] * groups
             + [pl.BlockSpec((1, 2 * BLK, 2 * BLK), lambda q, *_: (q, 0, 0))]
             + [pl.BlockSpec(memory_space=pl.ANY)] * len(given),
             out_specs=pl.BlockSpec(memory_space=pl.ANY),
@@ -450,7 +474,7 @@
             ],
         ),
         out_shape=jax.ShapeDtypeStruct(shape, jnp.float32),
-        input_output_aliases={5: 0} if given else {},
+        input_output_aliases={groups + 4: 0} if given else {},
         compiler_params=pltpu.CompilerParams(vmem_limit_bytes=VMEM_LIMIT),
         cost_estimate=pl.CostEstimate(
             flops=6 * pairs * rows * 4 * BLK * BLK,
@@ -458,7 +482,7 @@
             transcendentals=0,
         ),
         name="settle",
-    )(arrive, order, natural, source, turns, *given)
+    )(arrive, order, natural, *sources, turns, *given)
 
 
 def swap(arrays, axis):
@@ -469,8 +493,7 @@
 
 
 def after(arrays, earlier):
-    arrays, earlier = lax.optimization_barrier((list(arrays), list(earlier)))
-    return arrays, earlier
+    return lax.optimization_barrier((arrays, earlier))
 
 
 def shards(groups, slabs, r_slabs, basis, owners, plan):
@@ -480,9 +503,10 @@
     strips = unit_width(units) // 128
     row_blocks = owners.shape[0]
     each = row_blocks // slabs
-    chunks = 2 if each % 2 == 0 else 1
-    per = each // chunks
-    part = rows // chunks
+    early = 1 if each > 1 else 0
+    late = each - early
+    late_cuts = [1, late - 1] if late > 1 else [late]
+    part = rows // 2
     pair_index = lax.axis_index("pair")
     slab_index = lax.axis_index("slab")
 
@@ -495,7 +519,16 @@
 
     goes_to = owners // row_blocks
     rank = rank_among(goes_to)
-    spot = (rank // per) * (slabs * per) + goes_to * per + rank % per
+    bounds, low = [], 0
+    for size in [early] * (early > 0) + late_cuts:
+        bounds.append((low, low + size))
+        low += size
+    spot = sum(
+        jnp.where(
+            (rank >= lo) & (rank < hi), slabs * lo + goes_to * (hi - lo) + rank - lo, 0
+        )
+        for lo, hi in bounds
+    )
     index = jnp.arange(row_blocks, dtype=jnp.int32)
     rows_at = jnp.sum(jnp.where(spot[None, :] == index[:, None], index[None, :], 0), axis=1)
     table = lax.all_gather(owners, "slab", axis=0, tiled=True).reshape(slabs, row_blocks)
@@ -504,62 +537,92 @@
     per_rank = jnp.arange(each, dtype=jnp.int32)
     hit = (table_to == slab_index)[:, None, :] & (table_rank[:, None, :] == per_rank[None, :, None])
     where_to = jnp.sum(jnp.where(hit, (table % row_blocks)[:, None, :], 0), axis=2)
-    natural = [
-        where_to[:, c * per : (c + 1) * per].reshape(slabs * per) for c in range(chunks)
+    natural = [where_to[:, lo:hi].reshape(slabs * (hi - lo)) for lo, hi in bounds]
+
+    def straight(size, start=0):
+        return jnp.arange(size // ROWB, dtype=jnp.int32) + start // ROWB
+
+    def over_slab(blocks):
+        return lax.all_to_all(blocks, "slab", 0, 0, tiled=True)
+
+    r_sent = pack(r_slabs, send_0, rows_at[slabs * early :], ROWB, groups, units)
+    send_v, r_sent = after(send_0, r_sent)
+    r_late = swap(r_sent, "pair")
+    first = []
+    if early:
+        (rows_early,), r_sent = after([rows_at[: slabs * early]], r_sent)
+        home = over_slab(gather_rows(r_slabs, rows_early)).reshape(-1, r_slabs.shape[1])
+        sent = pack(home, send_0, straight(home.shape[0]), ROWB, groups, units)
+        sent, (r_late, natural) = after(sent, (r_late, natural))
+        first.append(swap(sent, "pair"))
+    first.append(r_late)
+    grams = [gram(got, arrive_0, order_0) for got in first]
+
+    v_sent = [
+        pack(basis, send_v, straight(part, c * part), ROWB, groups, units) for c in range(2)
     ]
-
-    steps = part // ROWB
-    straight = [
-        jnp.arange(steps, dtype=jnp.int32) + c * steps for c in range(chunks)
-    ]
-
-    def summed(*parts):
-        return lax.psum(functools.reduce(jnp.add, parts), "slab")
-
-    r_sent = pack(r_slabs, send_0, rows_at, ROWB, groups, units)
-    r_got = swap(r_sent, "pair")
-    v_sent = [pack(basis, send_0, straight[c], ROWB, groups, units) for c in range(chunks)]
-
-    v_got = [None] * chunks
-    v_sent[0], (r_got, natural) = after(v_sent[0], (r_got, natural))
-    v_got[0] = swap(v_sent[0], "pair")
-    turns = turns_of(summed(gram(r_got, arrive_0, order_0)))
-
-    def second(sources, row0):
-        turned = rotate(sources, arrive_0, order_0, turns, row0, part)
-        return pack(turned, send_1, straight[0], ROWB, groups, units)
-
-    r_two = []
-    for c in range(chunks):
-        sent = second(r_got, c * part)
-        if c == 0:
-            sent, v_got[0] = after(sent, v_got[0])
+    v_sent[0], (first[0], grams[1:], natural) = after(
+        v_sent[0], (first[0], grams[1:], natural)
+    )
+    if early:
+        grams[0] = gram(first[0], arrive_0, order_0)
+    v_got = [swap(v_sent[0], "pair"), None]
+    turns = turns_of(lax.psum(functools.reduce(jnp.add, grams), "slab"))
+
+    def second(sources, row0, size):
+        turned = rotate(sources, arrive_0, order_0, turns, row0, size)
+        return pack(turned, send_1, straight(size), ROWB, groups, units)
+
+    late_chunks, row0 = [], 0
+    for lo, hi in bounds[1 if early else 0 :]:
+        size = (hi - lo) * slabs * ROWB
+        late_chunks.append((first[-1], row0, size))
+        row0 += size
+    early_chunks = [(first[0], 0, early * slabs * ROWB)] if early else []
+    r_two, last = [], v_got[0]
+    for sources, row0, size in late_chunks + early_chunks:
+        sent = second(sources, row0, size)
+        sent, last = after(sent, last)
+        if r_two:
+            r_two[-1] = last
         else:
-            sent, r_two[-1] = after(sent, r_two[-1])
-        r_two.append(swap(sent, "pair"))
-    for c in range(1, chunks):
-        v_sent[c], r_two[-1] = after(v_sent[c], r_two[-1])
-        v_got[c] = swap(v_sent[c], "pair")
-
-    v_next = [second(v_got[0], 0)]
-    packed = [slab_pack(r_two[c], slabs) for c in range(chunks)]
-    sums = functools.reduce(jnp.add, [gram(r_two[c], arrive_1, order_1) for c in range(chunks)])
-    (v_next[0], packed[1:], sums), v_got[-1] = after((v_next[0], packed[1:], sums), v_got[-1])
-    r_home = [lax.all_to_all(packed[c], "slab", 0, 0, tiled=True) for c in range(chunks)]
-    v_two = [swap(v_next[0], "pair")]
-    turns_1 = turns_of(summed(sums))
-    for c in range(1, chunks):
-        sent, v_two[-1] = after(second(v_got[c], 0), v_two[-1])
-        v_two.append(swap(sent, "pair"))
-
-    r_out = v_out = None
-    for c in range(chunks):
-        if c > 0:
-            (v_two[c], r_home[c]), (r_out, v_out) = after((v_two[c], r_home[c]), (r_out, v_out))
+            v_got[0] = last
+        last = swap(sent, "pair")
+        r_two.append(last)
+
+    packed = [slab_pack(r_two[c], slabs) for c in range(len(late_chunks))]
+    v_sent[1], r_two[-1] = after(v_sent[1], r_two[-1])
+    v_got[1] = swap(v_sent[1], "pair")
+    r_home = [over_slab(blocks) for blocks in packed]
+    sums = functools.reduce(jnp.add, [gram(got, arrive_1, order_1) for got in r_two])
+    v_got[0], sums = after(v_got[0], sums)
+    sums = lax.psum(sums, "slab")
+
+    v_next, v_got[1] = after(second(v_got[0], 0, part), v_got[1])
+    v_two = [swap(v_next, "pair")]
+    (v_next, sums), v_two[0] = after((second(v_got[1], 0, part), sums), v_two[0])
+    v_two.append(swap(v_next, "pair"))
+    turns_1 = turns_of(sums)
+
+    v_out = rotate(v_two[0], arrive_1, order_1, turns_1, 0, part, None, basis.shape, 0)
+    r_out = None
+    if early:
         r_out = settle(
-            r_home[c], arrive_1, order_1, natural[c], turns_1, strips, r_slabs.shape, r_out
+            r_two[-1], arrive_1, order_1, natural[0], turns_1, strips, r_slabs.shape
         )
-        v_out = rotate(v_two[c], arrive_1, order_1, turns_1, 0, part, v_out, basis.shape, c)
+    for c, blocks in enumerate(r_home):
+        r_out = settle(
+            [blocks.reshape(-1, blocks.shape[2])],
+            arrive_1,
+            order_1,
+            natural[c + early],
+            turns_1,
+            strips,
+            r_slabs.shape,
+            r_out,
+        )
+    v_two[1], (r_out, v_out) = after(v_two[1], (r_out, v_out))
+    v_out = rotate(v_two[1], arrive_1, order_1, turns_1, 0, part, v_out, basis.shape, 1)
     return r_out, v_out
 
 

time: 1030 us -> 947 us (0.919); the launches traced: 1030 us -> 934 us
  waiting for transfers between devices: 668 us -> 411 us
  blocking collectives: 8.45 us -> 97 us
  Pallas kernels: 248 us -> 279 us
  local copies, waits for them, and re-layouts: 16.2 us -> 28.2 us
  starting transfers between devices: 36.2 us -> 48.2 us
  matrix products: 18.5 us -> 29 us
    ppermute x21 -> x27, waiting for transfers between devices: 450 us -> 311 us  [swap(): lax.ppermute(arrays[o], axis, [(i, i ^ o) for i in range(count)])]
    psum x2, waiting for transfers between devices: 218 us -> 101 us  [the longest x1 54.4 us: shards(): turns = turns_of(lax.psum(functools.reduce(jnp.add, grams), 'slab'))]
    unnamed x1, blocking collectives: 8.45 us -> 97 us
    pallas_call x2 -> x4, Pallas kernels: 33.3 us -> 47 us  [the longest x3 41.7 us: settle(): pl.pallas_call(functools.partial(settle_kernel, groups, strips, len(given...]
    pallas_call x3 -> x5, Pallas kernels: 32.9 us -> 43.3 us  [gram(): pl.pallas_call(functools.partial(gram_kernel, groups), grid_spec=pltpu.Pr...]
    unnamed x55 -> x113, local copies, waits for them, and re-layouts: 15.3 us -> 24.9 us
    pallas_call x6 -> x7, Pallas kernels: 103 us -> 110 us  [rotate(): pl.pallas_call(functools.partial(rotate_kernel, groups, row0, len(given))...]
    ppermute x21 -> x27, starting transfers between devices: 24.5 us -> 31.5 us  [swap(): lax.ppermute(arrays[o], axis, [(i, i ^ o) for i in range(count)])]
  transfers between devices with their start and end apart: 25 -> 32, of which waited for: 13 -> 14; matrix products, arithmetic and copies ran while one was open for 3% -> 5% of each run, Pallas kernels for 17% -> 25%
where the time goes in v2:
time: 947 us; the launch traced here: 934 us
  waiting for transfers between devices  411 us (43%)
  Pallas kernels  279 us (29%)
  blocking collectives  97 us (10%)
  starting transfers between devices  48.2 us (5%)
  matrix products  29 us (3%)
  local copies, waits for them, and re-layouts  28.2 us (3%)
  other arithmetic  26.3 us (3%)
  between operations  15.6 us (2%)
    ppermute x27, waiting for transfers between devices, swap(): lax.ppermute(arrays[o], axis, [(i, i ^ o) for i in range(count)])  311 us
    pallas_call x7, Pallas kernels, rotate(): pl.pallas_call(functools.partial(rotate_kernel, groups, row0, len(given))...  110 us
    unnamed x1, blocking collectives  97 us
    pallas_call x9, Pallas kernels, pack(): pl.pallas_call(functools.partial(pack_kernel, groups, units, blocks), gri...  69.9 us
    psum x1, waiting for transfers between devices, shards(): turns = turns_of(lax.psum(functools.reduce(jnp.add, grams), 'slab'))  54.4 us
    psum x1, waiting for transfers between devices, shards(): sums = lax.psum(sums, 'slab')  46.4 us
    pallas_call x5, Pallas kernels, gram(): pl.pallas_call(functools.partial(gram_kernel, groups), grid_spec=pltpu.Pr...  43.3 us
    pallas_call x3, Pallas kernels, settle(): pl.pallas_call(functools.partial(settle_kernel, groups, strips, len(given...  41.7 us
  transfers between devices with their start and end apart: 32, of which 14 were waited for; matrix products, arithmetic and copies ran while one was open for 5% of the time, Pallas kernels for 25%

profile of v2, /device:TPU:8, one launch (start us, length us, event | category | flops | bytes accessed | tf_op | source)
XLA Modules:
  0.0 934.4 jit_solution(9960764984257448324)
XLA Ops:
  12.7 12.8 %pack.9 = (f32[1152,768]{1,0:T(8,128)S(1)}, f32[1152,768]{1,0:T(8,128)}, f32[1152,768]{1,0:T(8,128)}, f32[1152,768]{1,0:T(8,128)}) custom-call(s32[16]{0:T(128)S(1)} %reshape.492.send, s32[24]{0:T(128)S(1)} %slice.43.rows_at, f32[1536,3072]{1,0:T(8,128)} %x_ref.1, f32[1536,3072]{1,0:T(8,128)} %x_ref.1, f32[1536,3072]{1,0:T(8,128)} %x_ref.1, f32[1536,3072]{1,0:T(8,128)} %x_ref.1), custom_call_target="tpu_custom_call" | custom-call | bytes 28311552 | tf_op jit(solution)/shard_map/pack/pallas_call | solution.py:132
  43.4 97.0 %all-reduce = s32[256]{0:T(256)S(1)} all-reduce(s32[256]{0:T(256)S(1)} %dynamic-update-slice), channel_id=1, replica_groups=mesh['pair'=4,'slab'=8] {'slab'}, use_global_device_ids=true, to_apply=%add | all-reduce | flops 256 | bytes 2048
  148.5 45.9 %collective-permute-done.1.refs_2_ = f32[1152,768]{1,0:T(8,128)} collective-permute-done((f32[1152,768]{1,0:T(8,128)}, f32[1152,768]{1,0:T(8,128)}, u32[]{:S(2)}, u32[]{:S(2)}) %collective-permute-start.1) | collective-permute-done | bytes 3538976 | tf_op jit(solution)/shard_map/ppermute | solution.py:491
  198.7 8.3 pack.11
  208.6 12.3 %cross_products.5 = f32[8,200,256]{2,1,0:T(8,128)S(1)} custom-call(s32[16]{0:T(128)S(1)} %dynamic_slice.12.arrive, s32[16]{0:T(128)S(1)} %dynamic_slice.13.order, f32[1152,768]{1,0:T(8,128)S(1)} %get-tuple-element.140.refs_0_, f32[1152,768]{1,0:T(8,128)} %collective-permute-done.refs_1_, f32[1152,768]{1,0:T(8,128)} %collective-permute-done.1.refs_2_, ...), custom_call_target="tpu_custom_call" | custom-call | flops 3623878656 | bytes 18874368 | tf_op jit(solution)/shard_map/cross_products/pallas_call | solution.py:268
  223.6 24.5 %collective-permute-done.4.refs_2_ = f32[384,768]{1,0:T(8,128)} collective-permute-done((f32[384,768]{1,0:T(8,128)}, f32[384,768]{1,0:T(8,128)}, u32[]{:S(2)}, u32[]{:S(2)}) %collective-permute-start.4) | collective-permute-done | bytes 1179680 | tf_op jit(solution)/shard_map/ppermute | solution.py:491
  248.1 8.6 cross_products.6
  266.5 54.4 %all-reduce.4.cloned.1.call-done = f32[8,200,256]{2,1,0:T(8,128)} async-done(((f32[8,200,256]{2,1,0:T(8,128)}), f32[8,200,256]{2,1,0:T(8,128)}) %all-reduce.4.cloned.1.call-update) | async-done | bytes 1638416 | tf_op jit(solution)/shard_map/psum | solution.py:570
  326.2 11.5 %fusion.19 = f32[8,192,192]{2,1,0:T(8,128)S(1)} fusion(f32[8,200,256]{2,1,0:T(8,128)S(1)} %copy-done.44, f32[8]{0:T(128)S(1)} %sqrt_add_fusion.1, f32[8,192]{1,0:T(8,128)S(1)} %bitcast.53, f32[8,192]{1,0:T(8,128)S(1)} %bitcast.63), kind=kOutput, calls=%fused_computation.101 | convolution fusion | flops 340623360 | bytes 2769408 | tf_op jit(solution)/shard_map/pik,pjk->pij/dot_general | solution.py:25
  346.4 12.2 %rotate.7.refs_0_.refs_1_.refs_2_.refs_3_ = f32[384,3072]{1,0:T(8,128)} custom-call(s32[16]{0:T(128)S(1)} %dynamic_slice.12.arrive, s32[16]{0:T(128)S(1)} %dynamic_slice.13.order, f32[1152,768]{1,0:T(8,128)S(1)} %get-tuple-element.140.refs_0_, f32[1152,768]{1,0:T(8,128)} %collective-permute-done.refs_1_, f32[1152,768]{1,0:T(8,128)} %collective-permute-done.1.refs_2_, ...), custom_call_target="tpu_custom_call" | custom-call | flops 2717908992 | bytes 11010048 | tf_op jit(solution)/shard_map/rotate/pallas_call | solution.py:308
  368.9 17.0 %rotate.8.refs_0_.refs_1_.refs_2_.refs_3_ = f32[768,3072]{1,0:T(8,128)} custom-call(s32[16]{0:T(128)S(1)} %dynamic_slice.12.arrive, s32[16]{0:T(128)S(1)} %dynamic_slice.13.order, f32[1152,768]{1,0:T(8,128)S(1)} %get-tuple-element.140.refs_0_, f32[1152,768]{1,0:T(8,128)} %collective-permute-done.refs_1_, f32[1152,768]{1,0:T(8,128)} %collective-permute-done.1.refs_2_, ...), custom_call_target="tpu_custom_call" | custom-call | flops 5435817984 | bytes 22020096 | tf_op jit(solution)/shard_map/rotate/pallas_call | solution.py:308
  394.3 22.4 %collective-permute-done.10.refs_2_ = f32[384,768]{1,0:T(8,128)S(1)} collective-permute-done((f32[384,768]{1,0:T(8,128)S(1)}, f32[384,768]{1,0:T(8,128)S(1)}, u32[]{:S(2)}, u32[]{:S(2)}) %collective-permute-start.10) | collective-permute-done | bytes 1179680 | tf_op jit(solution)/shard_map/ppermute | solution.py:491
  432.8 12.2 %rotate.9.refs_0_.refs_1_.refs_2_.refs_3_ = f32[384,3072]{1,0:T(8,128)} custom-call(s32[16]{0:T(128)S(1)} %dynamic_slice.12.arrive, s32[16]{0:T(128)S(1)} %dynamic_slice.13.order, f32[384,768]{1,0:T(8,128)S(1)} %copy-done.5, f32[384,768]{1,0:T(8,128)} %collective-permute-done.3.refs_1_, f32[384,768]{1,0:T(8,128)} %collective-permute-done.4.refs_2_, ...), custom_call_target="tpu_custom_call" | custom-call | flops 2717908992 | bytes 11010048 | tf_op jit(solution)/shard_map/rotate/pallas_call | solution.py:308
  452.4 31.2 %collective-permute-done.12.refs_1_ = f32[768,768]{1,0:T(8,128)S(1)} collective-permute-done((f32[768,768]{1,0:T(8,128)}, f32[768,768]{1,0:T(8,128)S(1)}, u32[]{:S(2)}, u32[]{:S(2)}) %collective-permute-start.12) | collective-permute-done | bytes 2359328 | tf_op jit(solution)/shard_map/ppermute | solution.py:491
  483.6 49.8 %collective-permute-done.13.refs_2_ = f32[768,768]{1,0:T(8,128)S(1)} collective-permute-done((f32[768,768]{1,0:T(8,128)}, f32[768,768]{1,0:T(8,128)S(1)}, u32[]{:S(2)}, u32[]{:S(2)}) %collective-permute-start.13) | collective-permute-done | bytes 2359328 | tf_op jit(solution)/shard_map/ppermute | solution.py:491
  550.9 9.5 %pack.15 = (f32[768,768]{1,0:T(8,128)S(1)}, f32[768,768]{1,0:T(8,128)}, f32[768,768]{1,0:T(8,128)}, f32[768,768]{1,0:T(8,128)}) custom-call(s32[16]{0:T(128)S(1)} %reshape.492.send, s32[16]{0:T(128)S(1)} %iota_add_fusion.rows_at, f32[1536,3072]{1,0:T(8,128)} %refs_3_.5, f32[1536,3072]{1,0:T(8,128)} %refs_3_.5, f32[1536,3072]{1,0:T(8,128)} %refs_3_.5, ...), custom_call_target="tpu_custom_call" | custom-call | bytes 18874368 | tf_op jit(solution)/shard_map/pack/pallas_call | solution.py:132
  561.8 14.6 %collective-permute-done.15.refs_1_ = f32[384,768]{1,0:T(8,128)S(1)} collective-permute-done((f32[384,768]{1,0:T(8,128)}, f32[384,768]{1,0:T(8,128)S(1)}, u32[]{:S(2)}, u32[]{:S(2)}) %collective-permute-start.15) | collective-permute-done | bytes 1179680 | tf_op jit(solution)/shard_map/ppermute | solution.py:491
  576.4 25.9 %collective-permute-done.16.refs_2_ = f32[384,768]{1,0:T(8,128)S(1)} collective-permute-done((f32[384,768]{1,0:T(8,128)}, f32[384,768]{1,0:T(8,128)S(1)}, u32[]{:S(2)}, u32[]{:S(2)}) %collective-permute-start.16) | collective-permute-done | bytes 1179680 | tf_op jit(solution)/shard_map/ppermute | solution.py:491
  613.8 9.7 %cross_products.8 = f32[8,200,256]{2,1,0:T(8,128)S(1)} custom-call(s32[16]{0:T(128)S(1)} %dynamic_slice.14.arrive, s32[16]{0:T(128)S(1)} %dynamic_slice.15.order, f32[768,768]{1,0:T(8,128)S(1)} %get-tuple-element.193.refs_0_, f32[768,768]{1,0:T(8,128)} %copy-done.2, f32[768,768]{1,0:T(8,128)} %copy-done.38, f32[768,768]{1,0:T(8,128)} %copy-done.39), custom_call_target="tpu_custom_call" | custom-call | flops 2415919104 | bytes 12582912 | tf_op jit(solution)/shard_map/cross_products/pallas_call | solution.py:268
  633.1 17.0 %rotate.10.refs_0_.refs_1_.refs_2_.refs_3_ = f32[768,3072]{1,0:T(8,128)} custom-call(s32[16]{0:T(128)S(1)} %dynamic_slice.12.arrive, s32[16]{0:T(128)S(1)} %dynamic_slice.13.order, f32[768,768]{1,0:T(8,128)S(1)} %copy-done.21, f32[768,768]{1,0:T(8,128)} %collective-permute-done.6.refs_1_, f32[768,768]{1,0:T(8,128)} %collective-permute-done.7.refs_2_, ...), custom_call_target="tpu_custom_call" | custom-call | flops 5435817984 | bytes 22020096 | tf_op jit(solution)/shard_map/rotate/pallas_call | solution.py:308
  650.2 9.0 pack.16
  659.2 46.5 %collective-permute-done.19.refs_2_ = f32[768,768]{1,0:T(8,128)} collective-permute-done((f32[768,768]{1,0:T(8,128)}, f32[768,768]{1,0:T(8,128)}, u32[]{:S(2)}, u32[]{:S(2)}) %collective-permute-start.19) | collective-permute-done | bytes 2359328 | tf_op jit(solution)/shard_map/ppermute | solution.py:491
  710.9 17.1 %rotate.11.refs_0_.refs_1_.refs_2_.refs_3_ = f32[768,3072]{1,0:T(8,128)} custom-call(s32[16]{0:T(128)S(1)} %dynamic_slice.12.arrive, s32[16]{0:T(128)S(1)} %dynamic_slice.13.order, f32[768,768]{1,0:T(8,128)S(1)} %copy-done.25, f32[768,768]{1,0:T(8,128)} %collective-permute-done.18.refs_1_, f32[768,768]{1,0:T(8,128)} %collective-permute-done.19.refs_2_, ...), custom_call_target="tpu_custom_call" | custom-call | flops 5435817984 | bytes 22020096 | tf_op jit(solution)/shard_map/rotate/pallas_call | solution.py:308
  727.9 8.4 pack.17
  739.1 46.4 %all-reduce.6.cloned.1.call-done = f32[8,200,256]{2,1,0:T(8,128)} async-done(((f32[8,200,256]{2,1,0:T(8,128)}), f32[8,200,256]{2,1,0:T(8,128)}) %all-reduce.6.cloned.1.call-update) | async-done | bytes 1638416 | tf_op jit(solution)/shard_map/psum | solution.py:599
  785.6 23.7 %collective-permute-done.22.refs_2_ = f32[768,768]{1,0:T(8,128)} collective-permute-done((f32[768,768]{1,0:T(8,128)}, f32[768,768]{1,0:T(8,128)}, u32[]{:S(2)}, u32[]{:S(2)}) %collective-permute-start.22) | collective-permute-done | bytes 2359328 | tf_op jit(solution)/shard_map/ppermute | solution.py:491
  828.3 11.8 %settle.3.refs_2_ = f32[1536,3072]{1,0:T(8,128)} custom-call(s32[16]{0:T(128)S(1)} %dynamic_slice.14.arrive, s32[16]{0:T(128)S(1)} %dynamic_slice.15.order, s32[8]{0:T(128)S(1)} %copy-done.30, f32[384,768]{1,0:T(8,128)S(1)} %get-tuple-element.205.refs_0_, f32[384,768]{1,0:T(8,128)S(1)} %copy-done.7, f32[384,768]{1,0:T(8,128)S(1)} %copy-done.9, ...), custom_call_target="tpu_custom_call" | custom-call | flops 2717908992 | bytes 11010048 | tf_op jit(solution)/shard_map/settle/pallas_call | solution.py:460
  840.2 17.1 %rotate.12.refs_5_ = f32[1536,3072]{1,0:T(8,128)} custom-call(s32[16]{0:T(128)S(1)} %dynamic_slice.14.arrive, s32[16]{0:T(128)S(1)} %dynamic_slice.15.order, f32[768,768]{1,0:T(8,128)S(1)} %get-tuple-element.242.refs_0_, f32[768,768]{1,0:T(8,128)} %collective-permute-done.21.refs_1_, f32[768,768]{1,0:T(8,128)} %collective-permute-done.22.refs_2_, ...), custom_call_target="tpu_custom_call" | custom-call | flops 5435817984 | bytes 22020096 | tf_op jit(solution)/shard_map/rotate/pallas_call | solution.py:308
  857.3 13.2 %settle.4.refs_2_ = f32[1536,3072]{1,0:T(8,128)} custom-call(s32[16]{0:T(128)S(1)} %dynamic_slice.14.arrive, s32[16]{0:T(128)S(1)} %dynamic_slice.15.order, s32[8]{0:T(128)S(1)} %copy-done.31, f32[384,3072]{1,0:T(8,128)} %bitcast.8.refs_0_, f32[8,384,384]{2,1,0:T(8,128)} %maximum_maximum_fusion.1.refs_4_.refs_1_, ...), custom_call_target="tpu_custom_call", output_to_operand_aliasing={{}: (5, {})} | custom-call | flops 2717908992 | bytes 11010048 | tf_op jit(solution)/shard_map/settle/pallas_call | solution.py:460
  872.9 16.7 %settle.5 = f32[1536,3072]{1,0:T(8,128)} custom-call(s32[16]{0:T(128)S(1)} %dynamic_slice.14.arrive, s32[16]{0:T(128)S(1)} %dynamic_slice.15.order, s32[16]{0:T(128)S(1)} %copy-done.29, f32[768,3072]{1,0:T(8,128)} %bitcast.7.refs_0_, f32[8,384,384]{2,1,0:T(8,128)S(1)} %copy-done, f32[1536,3072]{1,0:T(8,128)} %settle.4.refs_2_), custom_call_target="tpu_custom_call", output_to_operand_aliasing={{}: (5, {})} | custom-call | flops 5435817984 | bytes 22020096 | tf_op jit(solution)/shard_map/settle/pallas_call | solution.py:460
  889.6 20.7 %collective-permute-done.25.refs_2_ = f32[768,768]{1,0:T(8,128)} collective-permute-done((f32[768,768]{1,0:T(8,128)}, f32[768,768]{1,0:T(8,128)}, u32[]{:S(2)}, u32[]{:S(2)}) %collective-permute-start.25) | collective-permute-done | bytes 2359328 | tf_op jit(solution)/shard_map/ppermute | solution.py:491
  910.2 17.1 %rotate.13 = f32[1536,3072]{1,0:T(8,128)} custom-call(s32[16]{0:T(128)S(1)} %dynamic_slice.14.arrive, s32[16]{0:T(128)S(1)} %dynamic_slice.15.order, f32[768,768]{1,0:T(8,128)S(1)} %copy-done.23, f32[768,768]{1,0:T(8,128)} %collective-permute-done.24.refs_1_, f32[768,768]{1,0:T(8,128)} %collective-permute-done.25.refs_2_, ...), custom_call_target="tpu_custom_call", output_to_operand_aliasing={{}: (7, {})} | custom-call | flops 5435817984 | bytes 22020096 | tf_op jit(solution)/shard_map/rotate/pallas_call | solution.py:308
  (241 shorter events, 174.3 us)
Async XLA Ops:
  33.0 109.2 %all-to-all-start = ((f32[8,48,3072]{2,1,0:T(8,128)}), f32[8,48,3072]{2,1,0:T(8,128)}, u32[]{:S(2)}, u32[]{:S(2)}) async-start(f32[8,48,3072]{2,1,0:T(8,128)} %copy-done.1), calls=%async_computation | async-start | bytes 9437184 | tf_op jit(solution)/shard_map/all_to_all | solution.py:546
  38.5 282.4 %all-reduce.4.cloned.1.call-start = ((), (), s32[]{:S(2)}) async-start(), calls=%async_computation.3 | async-start | bytes 3276800 | tf_op jit(solution)/shard_map/psum | solution.py:570
  38.5 110.1 %collective-permute-start = (f32[1152,768]{1,0:T(8,128)}, f32[1152,768]{1,0:T(8,128)}, u32[]{:S(2)}, u32[]{:S(2)}) collective-permute-start(f32[1152,768]{1,0:T(8,128)} %get-tuple-element.132), channel_id=1, source_target_pairs={{0,8},{8,0},{16,24},{24,16},{1,9},{9,1},{17,25},{25,17},{2,10},{10... | collective-permute-start | bytes 10616840 | tf_op jit(solution)/shard_map/ppermute | solution.py:491
  40.0 154.5 %collective-permute-start.1 = (f32[1152,768]{1,0:T(8,128)}, f32[1152,768]{1,0:T(8,128)}, u32[]{:S(2)}, u32[]{:S(2)}) collective-permute-start(f32[1152,768]{1,0:T(8,128)} %get-tuple-element.133), channel_id=1, source_target_pairs={{0,16},{8,24},{16,0},{24,8},{1,17},{9,25},{17,1},{25,9},{2,18},{10... | collective-permute-start | bytes 10616840 | tf_op jit(solution)/shard_map/ppermute | solution.py:491
  41.5 153.0 %collective-permute-start.2 = (f32[1152,768]{1,0:T(8,128)}, f32[1152,768]{1,0:T(8,128)}, u32[]{:S(2)}, u32[]{:S(2)}) collective-permute-start(f32[1152,768]{1,0:T(8,128)} %get-tuple-element.134), channel_id=1, source_target_pairs={{0,24},{8,16},{16,8},{24,0},{1,25},{9,17},{17,9},{25,1},{2,26},{10... | collective-permute-start | bytes 10616840 | tf_op jit(solution)/shard_map/ppermute | solution.py:491
  194.4 29.2 %collective-permute-start.3 = (f32[384,768]{1,0:T(8,128)}, f32[384,768]{1,0:T(8,128)}, u32[]{:S(2)}, u32[]{:S(2)}) collective-permute-start(f32[384,768]{1,0:T(8,128)} %get-tuple-element.150), channel_id=1, source_target_pairs={{0,8},{8,0},{16,24},{24,16},{1,9},{9,1},{17,25},{25,17},{2,10},{10... | collective-permute-start | bytes 3538952 | tf_op jit(solution)/shard_map/ppermute | solution.py:491
  195.6 52.5 %collective-permute-start.4 = (f32[384,768]{1,0:T(8,128)}, f32[384,768]{1,0:T(8,128)}, u32[]{:S(2)}, u32[]{:S(2)}) collective-permute-start(f32[384,768]{1,0:T(8,128)} %get-tuple-element.151), channel_id=1, source_target_pairs={{0,16},{8,24},{16,0},{24,8},{1,17},{9,25},{17,1},{25,9},{2,18},{10... | collective-permute-start | bytes 3538952 | tf_op jit(solution)/shard_map/ppermute | solution.py:491
  196.4 51.7 %collective-permute-start.5 = (f32[384,768]{1,0:T(8,128)}, f32[384,768]{1,0:T(8,128)}, u32[]{:S(2)}, u32[]{:S(2)}) collective-permute-start(f32[384,768]{1,0:T(8,128)} %get-tuple-element.152), channel_id=1, source_target_pairs={{0,24},{8,16},{16,8},{24,0},{1,25},{9,17},{17,9},{25,1},{2,26},{10... | collective-permute-start | bytes 3538952 | tf_op jit(solution)/shard_map/ppermute | solution.py:491
  263.0 99.7 %collective-permute-start.6 = (f32[768,768]{1,0:T(8,128)}, f32[768,768]{1,0:T(8,128)}, u32[]{:S(2)}, u32[]{:S(2)}) collective-permute-start(f32[768,768]{1,0:T(8,128)} %copy-done.32), channel_id=1, source_target_pairs={{0,8},{8,0},{16,24},{24,16},{1,9},{9,1},{17,25},{25,17},{2,10},{10... | collective-permute-start | bytes 7077896 | tf_op jit(solution)/shard_map/ppermute | solution.py:491
  263.7 101.7 %collective-permute-start.7 = (f32[768,768]{1,0:T(8,128)}, f32[768,768]{1,0:T(8,128)}, u32[]{:S(2)}, u32[]{:S(2)}) collective-permute-start(f32[768,768]{1,0:T(8,128)} %get-tuple-element.167), channel_id=1, source_target_pairs={{0,16},{8,24},{16,0},{24,8},{1,17},{9,25},{17,1},{25,9},{2,18},{10... | collective-permute-start | bytes 7077896 | tf_op jit(solution)/shard_map/ppermute | solution.py:491
  264.9 100.5 %collective-permute-start.8 = (f32[768,768]{1,0:T(8,128)}, f32[768,768]{1,0:T(8,128)}, u32[]{:S(2)}, u32[]{:S(2)}) collective-permute-start(f32[768,768]{1,0:T(8,128)} %get-tuple-element.168), channel_id=1, source_target_pairs={{0,24},{8,16},{16,8},{24,0},{1,25},{9,17},{17,9},{25,1},{2,26},{10... | collective-permute-start | bytes 7077896 | tf_op jit(solution)/shard_map/ppermute | solution.py:491
  365.4 28.9 %collective-permute-start.9 = (f32[384,768]{1,0:T(8,128)S(1)}, f32[384,768]{1,0:T(8,128)S(1)}, u32[]{:S(2)}, u32[]{:S(2)}) collective-permute-start(f32[384,768]{1,0:T(8,128)S(1)} %get-tuple-element.178), channel_id=1, source_target_pairs={{0,8},{8,0},{16,24},{24,16},{1,9},{9,1},{17,25},{25,17},{2,10},{10... | collective-permute-start | bytes 3538952 | tf_op jit(solution)/shard_map/ppermute | solution.py:491
  366.8 49.9 %collective-permute-start.10 = (f32[384,768]{1,0:T(8,128)S(1)}, f32[384,768]{1,0:T(8,128)S(1)}, u32[]{:S(2)}, u32[]{:S(2)}) collective-permute-start(f32[384,768]{1,0:T(8,128)S(1)} %get-tuple-element.179), channel_id=1, source_target_pairs={{0,16},{8,24},{16,0},{24,8},{1,17},{9,25},{17,1},{25,9},{2,18},{10... | collective-permute-start | bytes 3538952 | tf_op jit(solution)/shard_map/ppermute | solution.py:491
  367.1 49.6 %collective-permute-start.11 = (f32[384,768]{1,0:T(8,128)S(1)}, f32[384,768]{1,0:T(8,128)S(1)}, u32[]{:S(2)}, u32[]{:S(2)}) collective-permute-start(f32[384,768]{1,0:T(8,128)S(1)} %get-tuple-element.180), channel_id=1, source_target_pairs={{0,24},{8,16},{16,8},{24,0},{1,25},{9,17},{17,9},{25,1},{2,26},{10... | collective-permute-start | bytes 3538952 | tf_op jit(solution)/shard_map/ppermute | solution.py:491
  423.3 118.8 %all-to-all-start.2 = ((f32[8,48,3072]{2,1,0:T(8,128)}), f32[8,48,3072]{2,1,0:T(8,128)}, u32[]{:S(2)}, u32[]{:S(2)}) async-start(f32[8,48,3072]{2,1,0:T(8,128)} %slab_pack.3), calls=%async_computation.2 | async-start | bytes 9437184 | tf_op jit(solution)/shard_map/all_to_all | solution.py:546
  429.3 54.3 %collective-permute-start.12 = (f32[768,768]{1,0:T(8,128)}, f32[768,768]{1,0:T(8,128)S(1)}, u32[]{:S(2)}, u32[]{:S(2)}) collective-permute-start(f32[768,768]{1,0:T(8,128)} %copy-done.34), channel_id=1, source_target_pairs={{0,8},{8,0},{16,24},{24,16},{1,9},{9,1},{17,25},{25,17},{2,10},{10... | collective-permute-start | bytes 7077896 | tf_op jit(solution)/shard_map/ppermute | solution.py:491
  429.6 103.8 %collective-permute-start.13 = (f32[768,768]{1,0:T(8,128)}, f32[768,768]{1,0:T(8,128)S(1)}, u32[]{:S(2)}, u32[]{:S(2)}) collective-permute-start(f32[768,768]{1,0:T(8,128)} %get-tuple-element.191), channel_id=1, source_target_pairs={{0,16},{8,24},{16,0},{24,8},{1,17},{9,25},{17,1},{25,9},{2,18},{10... | collective-permute-start | bytes 7077896 | tf_op jit(solution)/shard_map/ppermute | solution.py:491
  431.0 102.3 %collective-permute-start.14 = (f32[768,768]{1,0:T(8,128)}, f32[768,768]{1,0:T(8,128)S(1)}, u32[]{:S(2)}, u32[]{:S(2)}) collective-permute-start(f32[768,768]{1,0:T(8,128)} %get-tuple-element.192), channel_id=1, source_target_pairs={{0,24},{8,16},{16,8},{24,0},{1,25},{9,17},{17,9},{25,1},{2,26},{10... | collective-permute-start | bytes 7077896 | tf_op jit(solution)/shard_map/ppermute | solution.py:491
  542.1 328.4 %all-to-all-start.1 = ((f32[8,96,3072]{2,1,0:T(8,128)}), f32[8,96,3072]{2,1,0:T(8,128)}, u32[]{:S(2)}, u32[]{:S(2)}) async-start(f32[8,96,3072]{2,1,0:T(8,128)} %slab_pack.2), calls=%async_computation.1 | async-start | bytes 18874368 | tf_op jit(solution)/shard_map/all_to_all | solution.py:546
  547.4 238.1 %all-reduce.6.cloned.1.call-start = ((), (), s32[]{:S(2)}) async-start(), calls=%async_computation.4 | async-start | bytes 3276800 | tf_op jit(solution)/shard_map/psum | solution.py:599
  547.4 29.0 %collective-permute-start.15 = (f32[384,768]{1,0:T(8,128)}, f32[384,768]{1,0:T(8,128)S(1)}, u32[]{:S(2)}, u32[]{:S(2)}) collective-permute-start(f32[384,768]{1,0:T(8,128)} %copy-done.37), channel_id=1, source_target_pairs={{0,8},{8,0},{16,24},{24,16},{1,9},{9,1},{17,25},{25,17},{2,10},{10... | collective-permute-start | bytes 3538952 | tf_op jit(solution)/shard_map/ppermute | solution.py:491
  549.2 53.2 %collective-permute-start.16 = (f32[384,768]{1,0:T(8,128)}, f32[384,768]{1,0:T(8,128)S(1)}, u32[]{:S(2)}, u32[]{:S(2)}) collective-permute-start(f32[384,768]{1,0:T(8,128)} %copy-done.36), channel_id=1, source_target_pairs={{0,16},{8,24},{16,0},{24,8},{1,17},{9,25},{17,1},{25,9},{2,18},{10... | collective-permute-start | bytes 3538952 | tf_op jit(solution)/shard_map/ppermute | solution.py:491
  549.5 52.9 %collective-permute-start.17 = (f32[384,768]{1,0:T(8,128)}, f32[384,768]{1,0:T(8,128)S(1)}, u32[]{:S(2)}, u32[]{:S(2)}) collective-permute-start(f32[384,768]{1,0:T(8,128)} %copy-done.35), channel_id=1, source_target_pairs={{0,24},{8,16},{16,8},{24,0},{1,25},{9,17},{17,9},{25,1},{2,26},{10... | collective-permute-start | bytes 3538952 | tf_op jit(solution)/shard_map/ppermute | solution.py:491
  602.4 56.8 %collective-permute-start.18 = (f32[768,768]{1,0:T(8,128)}, f32[768,768]{1,0:T(8,128)}, u32[]{:S(2)}, u32[]{:S(2)}) collective-permute-start(f32[768,768]{1,0:T(8,128)} %get-tuple-element.218), channel_id=1, source_target_pairs={{0,8},{8,0},{16,24},{24,16},{1,9},{9,1},{17,25},{25,17},{2,10},{10... | collective-permute-start | bytes 7077896 | tf_op jit(solution)/shard_map/ppermute | solution.py:491
  602.8 102.9 %collective-permute-start.19 = (f32[768,768]{1,0:T(8,128)}, f32[768,768]{1,0:T(8,128)}, u32[]{:S(2)}, u32[]{:S(2)}) collective-permute-start(f32[768,768]{1,0:T(8,128)} %get-tuple-element.219), channel_id=1, source_target_pairs={{0,16},{8,24},{16,0},{24,8},{1,17},{9,25},{17,1},{25,9},{2,18},{10... | collective-permute-start | bytes 7077896 | tf_op jit(solution)/shard_map/ppermute | solution.py:491
  604.1 101.5 %collective-permute-start.20 = (f32[768,768]{1,0:T(8,128)}, f32[768,768]{1,0:T(8,128)}, u32[]{:S(2)}, u32[]{:S(2)}) collective-permute-start(f32[768,768]{1,0:T(8,128)} %get-tuple-element.220), channel_id=1, source_target_pairs={{0,24},{8,16},{16,8},{24,0},{1,25},{9,17},{17,9},{25,1},{2,26},{10... | collective-permute-start | bytes 7077896 | tf_op jit(solution)/shard_map/ppermute | solution.py:491
  705.7 79.9 %collective-permute-start.21 = (f32[768,768]{1,0:T(8,128)}, f32[768,768]{1,0:T(8,128)}, u32[]{:S(2)}, u32[]{:S(2)}) collective-permute-start(f32[768,768]{1,0:T(8,128)} %get-tuple-element.231), channel_id=1, source_target_pairs={{0,8},{8,0},{16,24},{24,16},{1,9},{9,1},{17,25},{25,17},{2,10},{10... | collective-permute-start | bytes 7077896 | tf_op jit(solution)/shard_map/ppermute | solution.py:491
  707.3 101.9 %collective-permute-start.22 = (f32[768,768]{1,0:T(8,128)}, f32[768,768]{1,0:T(8,128)}, u32[]{:S(2)}, u32[]{:S(2)}) collective-permute-start(f32[768,768]{1,0:T(8,128)} %get-tuple-element.232), channel_id=1, source_target_pairs={{0,16},{8,24},{16,0},{24,8},{1,17},{9,25},{17,1},{25,9},{2,18},{10... | collective-permute-start | bytes 7077896 | tf_op jit(solution)/shard_map/ppermute | solution.py:491
  707.6 101.6 %collective-permute-start.23 = (f32[768,768]{1,0:T(8,128)}, f32[768,768]{1,0:T(8,128)}, u32[]{:S(2)}, u32[]{:S(2)}) collective-permute-start(f32[768,768]{1,0:T(8,128)} %get-tuple-element.233), channel_id=1, source_target_pairs={{0,24},{8,16},{16,8},{24,0},{1,25},{9,17},{17,9},{25,1},{2,26},{10... | collective-permute-start | bytes 7077896 | tf_op jit(solution)/shard_map/ppermute | solution.py:491
  809.3 80.3 %collective-permute-start.24 = (f32[768,768]{1,0:T(8,128)}, f32[768,768]{1,0:T(8,128)}, u32[]{:S(2)}, u32[]{:S(2)}) collective-permute-start(f32[768,768]{1,0:T(8,128)} %copy-done.33), channel_id=1, source_target_pairs={{0,8},{8,0},{16,24},{24,16},{1,9},{9,1},{17,25},{25,17},{2,10},{10... | collective-permute-start | bytes 7077896 | tf_op jit(solution)/shard_map/ppermute | solution.py:491
  809.4 100.8 %collective-permute-start.25 = (f32[768,768]{1,0:T(8,128)}, f32[768,768]{1,0:T(8,128)}, u32[]{:S(2)}, u32[]{:S(2)}) collective-permute-start(f32[768,768]{1,0:T(8,128)} %get-tuple-element.236), channel_id=1, source_target_pairs={{0,16},{8,24},{16,0},{24,8},{1,17},{9,25},{17,1},{25,9},{2,18},{10... | collective-permute-start | bytes 7077896 | tf_op jit(solution)/shard_map/ppermute | solution.py:491
  811.1 99.1 %collective-permute-start.26 = (f32[768,768]{1,0:T(8,128)}, f32[768,768]{1,0:T(8,128)}, u32[]{:S(2)}, u32[]{:S(2)}) collective-permute-start(f32[768,768]{1,0:T(8,128)} %get-tuple-element.237), channel_id=1, source_target_pairs={{0,24},{8,16},{16,8},{24,0},{1,25},{9,17},{17,9},{25,1},{2,26},{10... | collective-permute-start | bytes 7077896 | tf_op jit(solution)/shard_map/ppermute | solution.py:491
  (53 other events, 958.8 us)
Sparse Core Ops, SparseCore 0:
  259.7 61.1 all-reduce.3
  709.3 76.1 all-reduce.5

commit v3 on v2

--- a/solution.py
+++ b/solution.py
@@ -238,8 +238,9 @@
     )
 
 
-def gram_kernel(groups, arrive, order, *refs):
-    sources, (out, win, sems) = refs[:groups], refs[groups:]
+def gram_kernel(groups, given, arrive, order, *refs):
+    sources, earlier = refs[:groups], refs[groups : groups + given]
+    out, win, sems = refs[groups + given :]
     rows = win.shape[2]
     q, slot = pipelined(*fetcher(arrive, order, sources, win, sems, 0, rows))
     tile = tile_of(rows)
@@ -260,18 +261,22 @@
     out[0, BLK:, :] = jnp.where(
         row == 0, low_half(norms[:, :WIN], odd), low_half(norms[:, WIN:], other_odd)
     )
-
-
-def gram(sources, arrive, order):
+    for sums in earlier:
+        out[...] += sums[...]
+
+
+def gram(sources, arrive, order, earlier=None):
     groups, rows = len(sources), sources[0].shape[0]
+    given = [] if earlier is None else [earlier]
+    sums = pl.BlockSpec((1, BLK + 8, WIN), lambda q, *_: (q, 0, 0))
     pairs = arrive.shape[0] // 2
     return pl.pallas_call(
-        functools.partial(gram_kernel, groups),
+        functools.partial(gram_kernel, groups, len(given)),
         grid_spec=pltpu.PrefetchScalarGridSpec(
             num_scalar_prefetch=2,
             grid=(pairs,),
-            in_specs=[pl.BlockSpec(memory_space=pl.ANY)] * groups,
-            out_specs=pl.BlockSpec((1, BLK + 8, WIN), lambda q, *_: (q, 0, 0)),
+            in_specs=[pl.BlockSpec(memory_space=pl.ANY)] * groups + [sums] * len(given),
+            out_specs=sums,
             scratch_shapes=[
                 pltpu.VMEM((2, 2, rows, WIN), jnp.float32),
                 pltpu.SemaphoreType.DMA((2, 2)),
@@ -285,7 +290,7 @@
             transcendentals=0,
         ),
         name="cross_products",
-    )(arrive, order, *sources)
+    )(arrive, order, *sources, *given)
 
 
 def rotate_kernel(groups, row0, given, arrive, order, *refs):
@@ -331,21 +336,44 @@
     )(arrive, order, *sources, turns, *given)
 
 
-def gather_kernel(rows_at, x_ref, out):
-    out[0] = x_ref[...]
+def gather_kernel(rows_at, x_ref, out, held, in_sems, out_sems):
+    count = out.shape[0]
+
+    def arrival(i):
+        start = pl.multiple_of(rows_at[i] * ROWB, 8)
+        return pltpu.make_async_copy(
+            x_ref.at[pl.ds(start, ROWB), :], held.at[i], in_sems.at[i]
+        )
+
+    def departure(i):
+        return pltpu.make_async_copy(held.at[i], out.at[i], out_sems.at[i])
+
+    for i in range(count):
+        arrival(i).start()
+    for i in range(count):
+        arrival(i).wait()
+        departure(i).start()
+    for i in range(count):
+        departure(i).wait()
 
 
 def gather_rows(x, rows_at):
     count = rows_at.shape[0]
+    shape = (count, ROWB, x.shape[1])
     return pl.pallas_call(
         gather_kernel,
         grid_spec=pltpu.PrefetchScalarGridSpec(
             num_scalar_prefetch=1,
-            grid=(count,),
-            in_specs=[pl.BlockSpec((ROWB, x.shape[1]), lambda i, at: (at[i], 0))],
-            out_specs=pl.BlockSpec((1, ROWB, x.shape[1]), lambda i, at: (i, 0, 0)),
-        ),
-        out_shape=jax.ShapeDtypeStruct((count, ROWB, x.shape[1]), jnp.float32),
+            grid=(1,),
+            in_specs=[pl.BlockSpec(memory_space=pl.ANY)],
+            out_specs=pl.BlockSpec(memory_space=pl.ANY),
+            scratch_shapes=[
+                pltpu.VMEM(shape, jnp.float32),
+                pltpu.SemaphoreType.DMA((count,)),
+                pltpu.SemaphoreType.DMA((count,)),
+            ],
+        ),
+        out_shape=jax.ShapeDtypeStruct(shape, jnp.float32),
         compiler_params=pltpu.CompilerParams(vmem_limit_bytes=VMEM_LIMIT),
         cost_estimate=pl.CostEstimate(
             flops=0, bytes_accessed=8 * count * ROWB * x.shape[1], transcendentals=0
@@ -556,18 +584,16 @@
         sent, (r_late, natural) = after(sent, (r_late, natural))
         first.append(swap(sent, "pair"))
     first.append(r_late)
-    grams = [gram(got, arrive_0, order_0) for got in first]
+    sums = gram(r_late, arrive_0, order_0)
 
     v_sent = [
         pack(basis, send_v, straight(part, c * part), ROWB, groups, units) for c in range(2)
     ]
-    v_sent[0], (first[0], grams[1:], natural) = after(
-        v_sent[0], (first[0], grams[1:], natural)
-    )
+    v_sent[0], (first[0], sums, natural) = after(v_sent[0], (first[0], sums, natural))
     if early:
-        grams[0] = gram(first[0], arrive_0, order_0)
+        sums = gram(first[0], arrive_0, order_0, sums)
     v_got = [swap(v_sent[0], "pair"), None]
-    turns = turns_of(lax.psum(functools.reduce(jnp.add, grams), "slab"))
+    turns = turns_of(lax.psum(sums, "slab"))
 
     def second(sources, row0, size):
         turned = rotate(sources, arrive_0, order_0, turns, row0, size)
@@ -594,7 +620,9 @@
     v_sent[1], r_two[-1] = after(v_sent[1], r_two[-1])
     v_got[1] = swap(v_sent[1], "pair")
     r_home = [over_slab(blocks) for blocks in packed]
-    sums = functools.reduce(jnp.add, [gram(got, arrive_1, order_1) for got in r_two])
+    sums = None
+    for got in r_two:
+        sums = gram(got, arrive_1, order_1, sums)
     v_got[0], sums = after(v_got[0], sums)
     sums = lax.psum(sums, "slab")
 

time: 947 us -> 944 us (level)
    unnamed x113 -> x117, local copies, waits for them, and re-layouts: 24.9 us -> 28.7 us
  transfers between devices with their start and end apart: 32 -> 32, of which waited for: 14 -> 16; matrix products, arithmetic and copies ran while one was open for 5% -> 5% of each run, Pallas kernels for 25% -> 25%
where the time goes in v3:
time: 944 us; the launch traced here: 931 us
  waiting for transfers between devices  410 us (43%)
  Pallas kernels  279 us (30%)
  blocking collectives  96.9 us (10%)
  starting transfers between devices  48.2 us (5%)
  local copies, waits for them, and re-layouts  32 us (3%)
  matrix products  29 us (3%)
  other arithmetic  20.2 us (2%)
  between operations  15.6 us (2%)
    ppermute x27, waiting for transfers between devices, swap(): lax.ppermute(arrays[o], axis, [(i, i ^ o) for i in range(count)])  309 us
    pallas_call x7, Pallas kernels, rotate(): pl.pallas_call(functools.partial(rotate_kernel, groups, row0, len(given))...  109 us
    unnamed x1, blocking collectives  96.9 us
    pallas_call x9, Pallas kernels, pack(): pl.pallas_call(functools.partial(pack_kernel, groups, units, blocks), gri...  70 us
    psum x1, waiting for transfers between devices, shards(): turns = turns_of(lax.psum(sums, 'slab'))  54.6 us
    pallas_call x5, Pallas kernels, gram(): pl.pallas_call(functools.partial(gram_kernel, groups, len(given)), grid_s...  46.5 us
    psum x1, waiting for transfers between devices, shards(): sums = lax.psum(sums, 'slab')  46.4 us
    pallas_call x3, Pallas kernels, settle(): pl.pallas_call(functools.partial(settle_kernel, groups, strips, len(given...  41.7 us
  transfers between devices with their start and end apart: 32, of which 16 were waited for; matrix products, arithmetic and copies ran while one was open for 5% of the time, Pallas kernels for 25%

profile of v3, /device:TPU:8, one launch (start us, length us, event | category | flops | bytes accessed | tf_op | source)
XLA Modules:
  0.0 930.8 jit_solution(7903449073946360660)
XLA Ops:
  12.7 12.7 %pack.9 = (f32[1152,768]{1,0:T(8,128)S(1)}, f32[1152,768]{1,0:T(8,128)}, f32[1152,768]{1,0:T(8,128)}, f32[1152,768]{1,0:T(8,128)}) custom-call(s32[16]{0:T(128)S(1)} %reshape.492.send, s32[24]{0:T(128)S(1)} %slice.43.rows_at, f32[1536,3072]{1,0:T(8,128)} %x_ref.1, f32[1536,3072]{1,0:T(8,128)} %x_ref.1, f32[1536,3072]{1,0:T(8,128)} %x_ref.1, f32[1536,3072]{1,0:T(8,128)} %x_ref.1), custom_call_target="tpu_custom_call" | custom-call | bytes 28311552 | tf_op jit(solution)/shard_map/pack/pallas_call | solution.py:132
  41.2 96.9 %all-reduce = s32[256]{0:T(256)S(1)} all-reduce(s32[256]{0:T(256)S(1)} %dynamic-update-slice), channel_id=1, replica_groups=mesh['pair'=4,'slab'=8] {'slab'}, use_global_device_ids=true, to_apply=%add | all-reduce | flops 256 | bytes 2048
  146.3 45.9 %collective-permute-done.1.refs_2_ = f32[1152,768]{1,0:T(8,128)} collective-permute-done((f32[1152,768]{1,0:T(8,128)}, f32[1152,768]{1,0:T(8,128)}, u32[]{:S(2)}, u32[]{:S(2)}) %collective-permute-start.1) | collective-permute-done | bytes 3538976 | tf_op jit(solution)/shard_map/ppermute | solution.py:519
  206.3 12.1 %cross_products.5.refs_4_ = f32[8,200,256]{2,1,0:T(8,128)S(1)} custom-call(s32[16]{0:T(128)S(1)} %dynamic_slice.12.arrive, s32[16]{0:T(128)S(1)} %dynamic_slice.13.order, f32[1152,768]{1,0:T(8,128)S(1)} %get-tuple-element.140.refs_0_, f32[1152,768]{1,0:T(8,128)} %collective-permute-done.refs_1_, f32[1152,768]{1,0:T(8,128)} %collective-permute-done.1.refs_2_, ...), custom_call_target="tpu_custom_call" | custom-call | flops 3623878656 | bytes 18874368 | tf_op jit(solution)/shard_map/cross_products/pallas_call | solution.py:273
  221.4 24.5 %collective-permute-done.4.refs_2_ = f32[384,768]{1,0:T(8,128)} collective-permute-done((f32[384,768]{1,0:T(8,128)}, f32[384,768]{1,0:T(8,128)}, u32[]{:S(2)}, u32[]{:S(2)}) %collective-permute-start.4) | collective-permute-done | bytes 1179680 | tf_op jit(solution)/shard_map/ppermute | solution.py:519
  245.9 10.0 %cross_products.6 = f32[8,200,256]{2,1,0:T(8,128)} custom-call(s32[16]{0:T(128)S(1)} %dynamic_slice.12.arrive, s32[16]{0:T(128)S(1)} %dynamic_slice.13.order, f32[384,768]{1,0:T(8,128)S(1)} %copy-done.7, f32[384,768]{1,0:T(8,128)} %collective-permute-done.3.refs_1_, f32[384,768]{1,0:T(8,128)} %collective-permute-done.4.refs_2_, ...), custom_call_target="tpu_custom_call" | custom-call | flops 1207959552 | bytes 6291456 | tf_op jit(solution)/shard_map/cross_products/pallas_call | solution.py:273
  262.8 54.6 %all-reduce.4.cloned.1.call-done = f32[8,200,256]{2,1,0:T(8,128)} async-done(((f32[8,200,256]{2,1,0:T(8,128)}), f32[8,200,256]{2,1,0:T(8,128)}) %all-reduce.4.cloned.1.call-update) | async-done | bytes 1638416 | tf_op jit(solution)/shard_map/psum | solution.py:596
  322.8 11.5 %fusion.19 = f32[8,192,192]{2,1,0:T(8,128)S(1)} fusion(f32[8,200,256]{2,1,0:T(8,128)S(1)} %copy-done.46, f32[8]{0:T(128)S(1)} %sqrt_add_fusion.1, f32[8,192]{1,0:T(8,128)S(1)} %bitcast.53, f32[8,192]{1,0:T(8,128)S(1)} %bitcast.63), kind=kOutput, calls=%fused_computation.100 | convolution fusion | flops 340623360 | bytes 2769408 | tf_op jit(solution)/shard_map/pik,pjk->pij/dot_general | solution.py:25
  342.9 12.2 %rotate.7.refs_0_.refs_1_.refs_2_.refs_3_ = f32[384,3072]{1,0:T(8,128)} custom-call(s32[16]{0:T(128)S(1)} %dynamic_slice.12.arrive, s32[16]{0:T(128)S(1)} %dynamic_slice.13.order, f32[1152,768]{1,0:T(8,128)S(1)} %get-tuple-element.140.refs_0_, f32[1152,768]{1,0:T(8,128)} %collective-permute-done.refs_1_, f32[1152,768]{1,0:T(8,128)} %collective-permute-done.1.refs_2_, ...), custom_call_target="tpu_custom_call" | custom-call | flops 2717908992 | bytes 11010048 | tf_op jit(solution)/shard_map/rotate/pallas_call | solution.py:313
  365.1 16.9 %rotate.9.refs_0_.refs_1_.refs_2_.refs_3_ = f32[768,3072]{1,0:T(8,128)} custom-call(s32[16]{0:T(128)S(1)} %dynamic_slice.12.arrive, s32[16]{0:T(128)S(1)} %dynamic_slice.13.order, f32[1152,768]{1,0:T(8,128)S(1)} %get-tuple-element.140.refs_0_, f32[1152,768]{1,0:T(8,128)} %collective-permute-done.refs_1_, f32[1152,768]{1,0:T(8,128)} %collective-permute-done.1.refs_2_, ...), custom_call_target="tpu_custom_call" | custom-call | flops 5435817984 | bytes 22020096 | tf_op jit(solution)/shard_map/rotate/pallas_call | solution.py:313
  390.5 22.7 %collective-permute-done.10.refs_2_ = f32[384,768]{1,0:T(8,128)S(1)} collective-permute-done((f32[384,768]{1,0:T(8,128)S(1)}, f32[384,768]{1,0:T(8,128)S(1)}, u32[]{:S(2)}, u32[]{:S(2)}) %collective-permute-start.10) | collective-permute-done | bytes 1179680 | tf_op jit(solution)/shard_map/ppermute | solution.py:519
  429.3 12.2 %rotate.8.refs_0_.refs_1_.refs_2_.refs_3_ = f32[384,3072]{1,0:T(8,128)} custom-call(s32[16]{0:T(128)S(1)} %dynamic_slice.12.arrive, s32[16]{0:T(128)S(1)} %dynamic_slice.13.order, f32[384,768]{1,0:T(8,128)S(1)} %copy-done.8, f32[384,768]{1,0:T(8,128)} %collective-permute-done.3.refs_1_, f32[384,768]{1,0:T(8,128)} %collective-permute-done.4.refs_2_, ...), custom_call_target="tpu_custom_call" | custom-call | flops 2717908992 | bytes 11010048 | tf_op jit(solution)/shard_map/rotate/pallas_call | solution.py:313
  448.9 31.3 %collective-permute-done.12.refs_1_ = f32[768,768]{1,0:T(8,128)S(1)} collective-permute-done((f32[768,768]{1,0:T(8,128)}, f32[768,768]{1,0:T(8,128)S(1)}, u32[]{:S(2)}, u32[]{:S(2)}) %collective-permute-start.12) | collective-permute-done | bytes 2359328 | tf_op jit(solution)/shard_map/ppermute | solution.py:519
  480.1 49.8 %collective-permute-done.13.refs_2_ = f32[768,768]{1,0:T(8,128)S(1)} collective-permute-done((f32[768,768]{1,0:T(8,128)}, f32[768,768]{1,0:T(8,128)S(1)}, u32[]{:S(2)}, u32[]{:S(2)}) %collective-permute-start.13) | collective-permute-done | bytes 2359328 | tf_op jit(solution)/shard_map/ppermute | solution.py:519
  547.5 9.5 %pack.13 = (f32[768,768]{1,0:T(8,128)S(1)}, f32[768,768]{1,0:T(8,128)}, f32[768,768]{1,0:T(8,128)}, f32[768,768]{1,0:T(8,128)}) custom-call(s32[16]{0:T(128)S(1)} %reshape.492.send, s32[16]{0:T(128)S(1)} %iota_add_fusion.rows_at, f32[1536,3072]{1,0:T(8,128)} %refs_3_.5, f32[1536,3072]{1,0:T(8,128)} %refs_3_.5, f32[1536,3072]{1,0:T(8,128)} %refs_3_.5, ...), custom_call_target="tpu_custom_call" | custom-call | bytes 18874368 | tf_op jit(solution)/shard_map/pack/pallas_call | solution.py:132
  558.4 14.6 %collective-permute-done.15.refs_1_ = f32[384,768]{1,0:T(8,128)S(1)} collective-permute-done((f32[384,768]{1,0:T(8,128)}, f32[384,768]{1,0:T(8,128)S(1)}, u32[]{:S(2)}, u32[]{:S(2)}) %collective-permute-start.15) | collective-permute-done | bytes 1179680 | tf_op jit(solution)/shard_map/ppermute | solution.py:519
  573.0 25.9 %collective-permute-done.16.refs_2_ = f32[384,768]{1,0:T(8,128)S(1)} collective-permute-done((f32[384,768]{1,0:T(8,128)}, f32[384,768]{1,0:T(8,128)S(1)}, u32[]{:S(2)}, u32[]{:S(2)}) %collective-permute-start.16) | collective-permute-done | bytes 1179680 | tf_op jit(solution)/shard_map/ppermute | solution.py:519
  611.7 9.6 %cross_products.8.refs_4_ = f32[8,200,256]{2,1,0:T(8,128)S(1)} custom-call(s32[16]{0:T(128)S(1)} %dynamic_slice.14.arrive, s32[16]{0:T(128)S(1)} %dynamic_slice.15.order, f32[768,768]{1,0:T(8,128)S(1)} %get-tuple-element.201.refs_0_, f32[768,768]{1,0:T(8,128)} %copy-done.2, f32[768,768]{1,0:T(8,128)} %copy-done.41, f32[768,768]{1,0:T(8,128)} %copy-done.42, ...), custom_call_target="tpu_custom_call" | custom-call | flops 2415919104 | bytes 12582912 | tf_op jit(solution)/shard_map/cross_products/pallas_call | solution.py:273
  622.5 8.5 cross_products.9
  631.0 16.9 %rotate.10.refs_0_.refs_1_.refs_2_.refs_3_ = f32[768,3072]{1,0:T(8,128)} custom-call(s32[16]{0:T(128)S(1)} %dynamic_slice.12.arrive, s32[16]{0:T(128)S(1)} %dynamic_slice.13.order, f32[768,768]{1,0:T(8,128)S(1)} %copy-done.24, f32[768,768]{1,0:T(8,128)} %collective-permute-done.6.refs_1_, f32[768,768]{1,0:T(8,128)} %collective-permute-done.7.refs_2_, ...), custom_call_target="tpu_custom_call" | custom-call | flops 5435817984 | bytes 22020096 | tf_op jit(solution)/shard_map/rotate/pallas_call | solution.py:313
  648.0 9.0 pack.16
  657.0 45.2 %collective-permute-done.19.refs_2_ = f32[768,768]{1,0:T(8,128)} collective-permute-done((f32[768,768]{1,0:T(8,128)}, f32[768,768]{1,0:T(8,128)}, u32[]{:S(2)}, u32[]{:S(2)}) %collective-permute-start.19) | collective-permute-done | bytes 2359328 | tf_op jit(solution)/shard_map/ppermute | solution.py:519
  707.4 17.0 %rotate.11.refs_0_.refs_1_.refs_2_.refs_3_ = f32[768,3072]{1,0:T(8,128)} custom-call(s32[16]{0:T(128)S(1)} %dynamic_slice.12.arrive, s32[16]{0:T(128)S(1)} %dynamic_slice.13.order, f32[768,768]{1,0:T(8,128)S(1)} %copy-done.28, f32[768,768]{1,0:T(8,128)} %collective-permute-done.18.refs_1_, f32[768,768]{1,0:T(8,128)} %collective-permute-done.19.refs_2_, ...), custom_call_target="tpu_custom_call" | custom-call | flops 5435817984 | bytes 22020096 | tf_op jit(solution)/shard_map/rotate/pallas_call | solution.py:313
  724.4 8.4 pack.17
  735.6 46.4 %all-reduce.6.cloned.1.call-done = f32[8,200,256]{2,1,0:T(8,128)} async-done(((f32[8,200,256]{2,1,0:T(8,128)}), f32[8,200,256]{2,1,0:T(8,128)}) %all-reduce.6.cloned.1.call-update) | async-done | bytes 1638416 | tf_op jit(solution)/shard_map/psum | solution.py:627
  782.0 23.8 %collective-permute-done.22.refs_2_ = f32[768,768]{1,0:T(8,128)} collective-permute-done((f32[768,768]{1,0:T(8,128)}, f32[768,768]{1,0:T(8,128)}, u32[]{:S(2)}, u32[]{:S(2)}) %collective-permute-start.22) | collective-permute-done | bytes 2359328 | tf_op jit(solution)/shard_map/ppermute | solution.py:519
  824.9 11.8 %settle.3.refs_2_ = f32[1536,3072]{1,0:T(8,128)} custom-call(s32[16]{0:T(128)S(1)} %dynamic_slice.14.arrive, s32[16]{0:T(128)S(1)} %dynamic_slice.15.order, s32[8]{0:T(128)S(1)} %copy-done.33, f32[384,768]{1,0:T(8,128)S(1)} %get-tuple-element.197.refs_0_, f32[384,768]{1,0:T(8,128)S(1)} %copy-done.10, f32[384,768]{1,0:T(8,128)S(1)} %copy-done.12, ...), custom_call_target="tpu_custom_call" | custom-call | flops 2717908992 | bytes 11010048 | tf_op jit(solution)/shard_map/settle/pallas_call | solution.py:488
  836.7 16.9 %rotate.12.refs_5_ = f32[1536,3072]{1,0:T(8,128)} custom-call(s32[16]{0:T(128)S(1)} %dynamic_slice.14.arrive, s32[16]{0:T(128)S(1)} %dynamic_slice.15.order, f32[768,768]{1,0:T(8,128)S(1)} %get-tuple-element.242.refs_0_, f32[768,768]{1,0:T(8,128)} %collective-permute-done.21.refs_1_, f32[768,768]{1,0:T(8,128)} %collective-permute-done.22.refs_2_, ...), custom_call_target="tpu_custom_call" | custom-call | flops 5435817984 | bytes 22020096 | tf_op jit(solution)/shard_map/rotate/pallas_call | solution.py:313
  853.7 13.3 %settle.4.refs_2_ = f32[1536,3072]{1,0:T(8,128)} custom-call(s32[16]{0:T(128)S(1)} %dynamic_slice.14.arrive, s32[16]{0:T(128)S(1)} %dynamic_slice.15.order, s32[8]{0:T(128)S(1)} %copy-done.34, f32[384,3072]{1,0:T(8,128)} %bitcast.8.refs_0_, f32[8,384,384]{2,1,0:T(8,128)} %maximum_maximum_fusion.1.refs_4_.refs_1_, ...), custom_call_target="tpu_custom_call", output_to_operand_aliasing={{}: (5, {})} | custom-call | flops 2717908992 | bytes 11010048 | tf_op jit(solution)/shard_map/settle/pallas_call | solution.py:488
  869.3 16.7 %settle.5 = f32[1536,3072]{1,0:T(8,128)} custom-call(s32[16]{0:T(128)S(1)} %dynamic_slice.14.arrive, s32[16]{0:T(128)S(1)} %dynamic_slice.15.order, s32[16]{0:T(128)S(1)} %copy-done.32, f32[768,3072]{1,0:T(8,128)} %bitcast.7.refs_0_, f32[8,384,384]{2,1,0:T(8,128)S(1)} %copy-done, f32[1536,3072]{1,0:T(8,128)} %settle.4.refs_2_), custom_call_target="tpu_custom_call", output_to_operand_aliasing={{}: (5, {})} | custom-call | flops 5435817984 | bytes 22020096 | tf_op jit(solution)/shard_map/settle/pallas_call | solution.py:488
  886.0 20.8 %collective-permute-done.25.refs_2_ = f32[768,768]{1,0:T(8,128)} collective-permute-done((f32[768,768]{1,0:T(8,128)}, f32[768,768]{1,0:T(8,128)}, u32[]{:S(2)}, u32[]{:S(2)}) %collective-permute-start.25) | collective-permute-done | bytes 2359328 | tf_op jit(solution)/shard_map/ppermute | solution.py:519
  906.8 16.9 %rotate.13 = f32[1536,3072]{1,0:T(8,128)} custom-call(s32[16]{0:T(128)S(1)} %dynamic_slice.14.arrive, s32[16]{0:T(128)S(1)} %dynamic_slice.15.order, f32[768,768]{1,0:T(8,128)S(1)} %copy-done.26, f32[768,768]{1,0:T(8,128)} %collective-permute-done.24.refs_1_, f32[768,768]{1,0:T(8,128)} %collective-permute-done.25.refs_2_, ...), custom_call_target="tpu_custom_call", output_to_operand_aliasing={{}: (7, {})} | custom-call | flops 5435817984 | bytes 22020096 | tf_op jit(solution)/shard_map/rotate/pallas_call | solution.py:313
  (243 shorter events, 170.6 us)
Async XLA Ops:
  30.7 109.2 %all-to-all-start = ((f32[8,48,3072]{2,1,0:T(8,128)}), f32[8,48,3072]{2,1,0:T(8,128)}, u32[]{:S(2)}, u32[]{:S(2)}) async-start(f32[8,48,3072]{2,1,0:T(8,128)} %copy-done.1), calls=%async_computation | async-start | bytes 9437184 | tf_op jit(solution)/shard_map/all_to_all | solution.py:574
  36.2 281.3 %all-reduce.4.cloned.1.call-start = ((), (), s32[]{:S(2)}) async-start(), calls=%async_computation.3 | async-start | bytes 3276800 | tf_op jit(solution)/shard_map/psum | solution.py:596
  36.2 110.1 %collective-permute-start = (f32[1152,768]{1,0:T(8,128)}, f32[1152,768]{1,0:T(8,128)}, u32[]{:S(2)}, u32[]{:S(2)}) collective-permute-start(f32[1152,768]{1,0:T(8,128)} %get-tuple-element.132), channel_id=1, source_target_pairs={{0,8},{8,0},{16,24},{24,16},{1,9},{9,1},{17,25},{25,17},{2,10},{10... | collective-permute-start | bytes 10616840 | tf_op jit(solution)/shard_map/ppermute | solution.py:519
  37.7 154.5 %collective-permute-start.1 = (f32[1152,768]{1,0:T(8,128)}, f32[1152,768]{1,0:T(8,128)}, u32[]{:S(2)}, u32[]{:S(2)}) collective-permute-start(f32[1152,768]{1,0:T(8,128)} %get-tuple-element.133), channel_id=1, source_target_pairs={{0,16},{8,24},{16,0},{24,8},{1,17},{9,25},{17,1},{25,9},{2,18},{10... | collective-permute-start | bytes 10616840 | tf_op jit(solution)/shard_map/ppermute | solution.py:519
  39.2 153.0 %collective-permute-start.2 = (f32[1152,768]{1,0:T(8,128)}, f32[1152,768]{1,0:T(8,128)}, u32[]{:S(2)}, u32[]{:S(2)}) collective-permute-start(f32[1152,768]{1,0:T(8,128)} %get-tuple-element.134), channel_id=1, source_target_pairs={{0,24},{8,16},{16,8},{24,0},{1,25},{9,17},{17,9},{25,1},{2,26},{10... | collective-permute-start | bytes 10616840 | tf_op jit(solution)/shard_map/ppermute | solution.py:519
  192.2 29.2 %collective-permute-start.3 = (f32[384,768]{1,0:T(8,128)}, f32[384,768]{1,0:T(8,128)}, u32[]{:S(2)}, u32[]{:S(2)}) collective-permute-start(f32[384,768]{1,0:T(8,128)} %get-tuple-element.150), channel_id=1, source_target_pairs={{0,8},{8,0},{16,24},{24,16},{1,9},{9,1},{17,25},{25,17},{2,10},{10... | collective-permute-start | bytes 3538952 | tf_op jit(solution)/shard_map/ppermute | solution.py:519
  193.4 52.5 %collective-permute-start.4 = (f32[384,768]{1,0:T(8,128)}, f32[384,768]{1,0:T(8,128)}, u32[]{:S(2)}, u32[]{:S(2)}) collective-permute-start(f32[384,768]{1,0:T(8,128)} %get-tuple-element.151), channel_id=1, source_target_pairs={{0,16},{8,24},{16,0},{24,8},{1,17},{9,25},{17,1},{25,9},{2,18},{10... | collective-permute-start | bytes 3538952 | tf_op jit(solution)/shard_map/ppermute | solution.py:519
  194.3 51.6 %collective-permute-start.5 = (f32[384,768]{1,0:T(8,128)}, f32[384,768]{1,0:T(8,128)}, u32[]{:S(2)}, u32[]{:S(2)}) collective-permute-start(f32[384,768]{1,0:T(8,128)} %get-tuple-element.152), channel_id=1, source_target_pairs={{0,24},{8,16},{16,8},{24,0},{1,25},{9,17},{17,9},{25,1},{2,26},{10... | collective-permute-start | bytes 3538952 | tf_op jit(solution)/shard_map/ppermute | solution.py:519
  259.3 100.0 %collective-permute-start.6 = (f32[768,768]{1,0:T(8,128)}, f32[768,768]{1,0:T(8,128)}, u32[]{:S(2)}, u32[]{:S(2)}) collective-permute-start(f32[768,768]{1,0:T(8,128)} %copy-done.35), channel_id=1, source_target_pairs={{0,8},{8,0},{16,24},{24,16},{1,9},{9,1},{17,25},{25,17},{2,10},{10... | collective-permute-start | bytes 7077896 | tf_op jit(solution)/shard_map/ppermute | solution.py:519
  260.0 100.9 %collective-permute-start.7 = (f32[768,768]{1,0:T(8,128)}, f32[768,768]{1,0:T(8,128)}, u32[]{:S(2)}, u32[]{:S(2)}) collective-permute-start(f32[768,768]{1,0:T(8,128)} %get-tuple-element.167), channel_id=1, source_target_pairs={{0,16},{8,24},{16,0},{24,8},{1,17},{9,25},{17,1},{25,9},{2,18},{10... | collective-permute-start | bytes 7077896 | tf_op jit(solution)/shard_map/ppermute | solution.py:519
  261.4 100.2 %collective-permute-start.8 = (f32[768,768]{1,0:T(8,128)}, f32[768,768]{1,0:T(8,128)}, u32[]{:S(2)}, u32[]{:S(2)}) collective-permute-start(f32[768,768]{1,0:T(8,128)} %get-tuple-element.168), channel_id=1, source_target_pairs={{0,24},{8,16},{16,8},{24,0},{1,25},{9,17},{17,9},{25,1},{2,26},{10... | collective-permute-start | bytes 7077896 | tf_op jit(solution)/shard_map/ppermute | solution.py:519
  361.6 28.9 %collective-permute-start.9 = (f32[384,768]{1,0:T(8,128)S(1)}, f32[384,768]{1,0:T(8,128)S(1)}, u32[]{:S(2)}, u32[]{:S(2)}) collective-permute-start(f32[384,768]{1,0:T(8,128)S(1)} %get-tuple-element.186), channel_id=1, source_target_pairs={{0,8},{8,0},{16,24},{24,16},{1,9},{9,1},{17,25},{25,17},{2,10},{10... | collective-permute-start | bytes 3538952 | tf_op jit(solution)/shard_map/ppermute | solution.py:519
  363.2 50.0 %collective-permute-start.10 = (f32[384,768]{1,0:T(8,128)S(1)}, f32[384,768]{1,0:T(8,128)S(1)}, u32[]{:S(2)}, u32[]{:S(2)}) collective-permute-start(f32[384,768]{1,0:T(8,128)S(1)} %get-tuple-element.187), channel_id=1, source_target_pairs={{0,16},{8,24},{16,0},{24,8},{1,17},{9,25},{17,1},{25,9},{2,18},{10... | collective-permute-start | bytes 3538952 | tf_op jit(solution)/shard_map/ppermute | solution.py:519
  363.8 49.4 %collective-permute-start.11 = (f32[384,768]{1,0:T(8,128)S(1)}, f32[384,768]{1,0:T(8,128)S(1)}, u32[]{:S(2)}, u32[]{:S(2)}) collective-permute-start(f32[384,768]{1,0:T(8,128)S(1)} %get-tuple-element.188), channel_id=1, source_target_pairs={{0,24},{8,16},{16,8},{24,0},{1,25},{9,17},{17,9},{25,1},{2,26},{10... | collective-permute-start | bytes 3538952 | tf_op jit(solution)/shard_map/ppermute | solution.py:519
  419.8 118.8 %all-to-all-start.2 = ((f32[8,48,3072]{2,1,0:T(8,128)}), f32[8,48,3072]{2,1,0:T(8,128)}, u32[]{:S(2)}, u32[]{:S(2)}) async-start(f32[8,48,3072]{2,1,0:T(8,128)} %slab_pack.3), calls=%async_computation.2 | async-start | bytes 9437184 | tf_op jit(solution)/shard_map/all_to_all | solution.py:574
  425.8 54.3 %collective-permute-start.12 = (f32[768,768]{1,0:T(8,128)}, f32[768,768]{1,0:T(8,128)S(1)}, u32[]{:S(2)}, u32[]{:S(2)}) collective-permute-start(f32[768,768]{1,0:T(8,128)} %copy-done.37), channel_id=1, source_target_pairs={{0,8},{8,0},{16,24},{24,16},{1,9},{9,1},{17,25},{25,17},{2,10},{10... | collective-permute-start | bytes 7077896 | tf_op jit(solution)/shard_map/ppermute | solution.py:519
  426.1 103.8 %collective-permute-start.13 = (f32[768,768]{1,0:T(8,128)}, f32[768,768]{1,0:T(8,128)S(1)}, u32[]{:S(2)}, u32[]{:S(2)}) collective-permute-start(f32[768,768]{1,0:T(8,128)} %get-tuple-element.191), channel_id=1, source_target_pairs={{0,16},{8,24},{16,0},{24,8},{1,17},{9,25},{17,1},{25,9},{2,18},{10... | collective-permute-start | bytes 7077896 | tf_op jit(solution)/shard_map/ppermute | solution.py:519
  427.6 102.4 %collective-permute-start.14 = (f32[768,768]{1,0:T(8,128)}, f32[768,768]{1,0:T(8,128)S(1)}, u32[]{:S(2)}, u32[]{:S(2)}) collective-permute-start(f32[768,768]{1,0:T(8,128)} %get-tuple-element.192), channel_id=1, source_target_pairs={{0,24},{8,16},{16,8},{24,0},{1,25},{9,17},{17,9},{25,1},{2,26},{10... | collective-permute-start | bytes 7077896 | tf_op jit(solution)/shard_map/ppermute | solution.py:519
  538.7 328.3 %all-to-all-start.1 = ((f32[8,96,3072]{2,1,0:T(8,128)}), f32[8,96,3072]{2,1,0:T(8,128)}, u32[]{:S(2)}, u32[]{:S(2)}) async-start(f32[8,96,3072]{2,1,0:T(8,128)} %slab_pack.2), calls=%async_computation.1 | async-start | bytes 18874368 | tf_op jit(solution)/shard_map/all_to_all | solution.py:574
  544.0 238.1 %all-reduce.6.cloned.1.call-start = ((), (), s32[]{:S(2)}) async-start(), calls=%async_computation.4 | async-start | bytes 3276800 | tf_op jit(solution)/shard_map/psum | solution.py:627
  544.0 29.0 %collective-permute-start.15 = (f32[384,768]{1,0:T(8,128)}, f32[384,768]{1,0:T(8,128)S(1)}, u32[]{:S(2)}, u32[]{:S(2)}) collective-permute-start(f32[384,768]{1,0:T(8,128)} %copy-done.40), channel_id=1, source_target_pairs={{0,8},{8,0},{16,24},{24,16},{1,9},{9,1},{17,25},{25,17},{2,10},{10... | collective-permute-start | bytes 3538952 | tf_op jit(solution)/shard_map/ppermute | solution.py:519
  545.7 53.2 %collective-permute-start.16 = (f32[384,768]{1,0:T(8,128)}, f32[384,768]{1,0:T(8,128)S(1)}, u32[]{:S(2)}, u32[]{:S(2)}) collective-permute-start(f32[384,768]{1,0:T(8,128)} %copy-done.39), channel_id=1, source_target_pairs={{0,16},{8,24},{16,0},{24,8},{1,17},{9,25},{17,1},{25,9},{2,18},{10... | collective-permute-start | bytes 3538952 | tf_op jit(solution)/shard_map/ppermute | solution.py:519
  546.0 53.0 %collective-permute-start.17 = (f32[384,768]{1,0:T(8,128)}, f32[384,768]{1,0:T(8,128)S(1)}, u32[]{:S(2)}, u32[]{:S(2)}) collective-permute-start(f32[384,768]{1,0:T(8,128)} %copy-done.38), channel_id=1, source_target_pairs={{0,24},{8,16},{16,8},{24,0},{1,25},{9,17},{17,9},{25,1},{2,26},{10... | collective-permute-start | bytes 3538952 | tf_op jit(solution)/shard_map/ppermute | solution.py:519
  598.9 58.1 %collective-permute-start.18 = (f32[768,768]{1,0:T(8,128)}, f32[768,768]{1,0:T(8,128)}, u32[]{:S(2)}, u32[]{:S(2)}) collective-permute-start(f32[768,768]{1,0:T(8,128)} %get-tuple-element.218), channel_id=1, source_target_pairs={{0,8},{8,0},{16,24},{24,16},{1,9},{9,1},{17,25},{25,17},{2,10},{10... | collective-permute-start | bytes 7077896 | tf_op jit(solution)/shard_map/ppermute | solution.py:519
  599.3 102.9 %collective-permute-start.19 = (f32[768,768]{1,0:T(8,128)}, f32[768,768]{1,0:T(8,128)}, u32[]{:S(2)}, u32[]{:S(2)}) collective-permute-start(f32[768,768]{1,0:T(8,128)} %get-tuple-element.219), channel_id=1, source_target_pairs={{0,16},{8,24},{16,0},{24,8},{1,17},{9,25},{17,1},{25,9},{2,18},{10... | collective-permute-start | bytes 7077896 | tf_op jit(solution)/shard_map/ppermute | solution.py:519
  600.7 101.5 %collective-permute-start.20 = (f32[768,768]{1,0:T(8,128)}, f32[768,768]{1,0:T(8,128)}, u32[]{:S(2)}, u32[]{:S(2)}) collective-permute-start(f32[768,768]{1,0:T(8,128)} %get-tuple-element.220), channel_id=1, source_target_pairs={{0,24},{8,16},{16,8},{24,0},{1,25},{9,17},{17,9},{25,1},{2,26},{10... | collective-permute-start | bytes 7077896 | tf_op jit(solution)/shard_map/ppermute | solution.py:519
  702.2 79.8 %collective-permute-start.21 = (f32[768,768]{1,0:T(8,128)}, f32[768,768]{1,0:T(8,128)}, u32[]{:S(2)}, u32[]{:S(2)}) collective-permute-start(f32[768,768]{1,0:T(8,128)} %get-tuple-element.231), channel_id=1, source_target_pairs={{0,8},{8,0},{16,24},{24,16},{1,9},{9,1},{17,25},{25,17},{2,10},{10... | collective-permute-start | bytes 7077896 | tf_op jit(solution)/shard_map/ppermute | solution.py:519
  703.9 101.9 %collective-permute-start.22 = (f32[768,768]{1,0:T(8,128)}, f32[768,768]{1,0:T(8,128)}, u32[]{:S(2)}, u32[]{:S(2)}) collective-permute-start(f32[768,768]{1,0:T(8,128)} %get-tuple-element.232), channel_id=1, source_target_pairs={{0,16},{8,24},{16,0},{24,8},{1,17},{9,25},{17,1},{25,9},{2,18},{10... | collective-permute-start | bytes 7077896 | tf_op jit(solution)/shard_map/ppermute | solution.py:519
  704.2 101.6 %collective-permute-start.23 = (f32[768,768]{1,0:T(8,128)}, f32[768,768]{1,0:T(8,128)}, u32[]{:S(2)}, u32[]{:S(2)}) collective-permute-start(f32[768,768]{1,0:T(8,128)} %get-tuple-element.233), channel_id=1, source_target_pairs={{0,24},{8,16},{16,8},{24,0},{1,25},{9,17},{17,9},{25,1},{2,26},{10... | collective-permute-start | bytes 7077896 | tf_op jit(solution)/shard_map/ppermute | solution.py:519
  805.8 80.2 %collective-permute-start.24 = (f32[768,768]{1,0:T(8,128)}, f32[768,768]{1,0:T(8,128)}, u32[]{:S(2)}, u32[]{:S(2)}) collective-permute-start(f32[768,768]{1,0:T(8,128)} %copy-done.36), channel_id=1, source_target_pairs={{0,8},{8,0},{16,24},{24,16},{1,9},{9,1},{17,25},{25,17},{2,10},{10... | collective-permute-start | bytes 7077896 | tf_op jit(solution)/shard_map/ppermute | solution.py:519
  805.9 100.8 %collective-permute-start.25 = (f32[768,768]{1,0:T(8,128)}, f32[768,768]{1,0:T(8,128)}, u32[]{:S(2)}, u32[]{:S(2)}) collective-permute-start(f32[768,768]{1,0:T(8,128)} %get-tuple-element.236), channel_id=1, source_target_pairs={{0,16},{8,24},{16,0},{24,8},{1,17},{9,25},{17,1},{25,9},{2,18},{10... | collective-permute-start | bytes 7077896 | tf_op jit(solution)/shard_map/ppermute | solution.py:519
  807.7 99.1 %collective-permute-start.26 = (f32[768,768]{1,0:T(8,128)}, f32[768,768]{1,0:T(8,128)}, u32[]{:S(2)}, u32[]{:S(2)}) collective-permute-start(f32[768,768]{1,0:T(8,128)} %get-tuple-element.237), channel_id=1, source_target_pairs={{0,24},{8,16},{16,8},{24,0},{1,25},{9,17},{17,9},{25,1},{2,26},{10... | collective-permute-start | bytes 7077896 | tf_op jit(solution)/shard_map/ppermute | solution.py:519
  (55 other events, 965.5 us)
Sparse Core Ops, SparseCore 0:
  256.1 61.3 all-reduce.3
  705.8 76.1 all-reduce.5

commit v4 on v3

--- a/solution.py
+++ b/solution.py
@@ -13,6 +13,7 @@
 EPSILON = 1e-06
 HIGH = lax.Precision.HIGH
 VMEM_LIMIT = 48 * 1024 * 1024
+SMALL = pl.CostEstimate(flops=1, bytes_accessed=1, transcendentals=0)
 
 
 def rotations(cross_gram, norms_a, norms_b):
@@ -140,11 +141,7 @@
         ),
         out_shape=[jax.ShapeDtypeStruct((total * block_rows, width), jnp.float32)] * groups,
         compiler_params=pltpu.CompilerParams(vmem_limit_bytes=VMEM_LIMIT),
-        cost_estimate=pl.CostEstimate(
-            flops=0,
-            bytes_accessed=2 * 4 * total * block_rows * x.shape[1],
-            transcendentals=0,
-        ),
+        cost_estimate=SMALL,
         name="pack",
     )(send, rows_at, *[x] * blocks)
 
@@ -284,11 +281,7 @@
         ),
         out_shape=jax.ShapeDtypeStruct((pairs, BLK + 8, WIN), jnp.float32),
         compiler_params=pltpu.CompilerParams(vmem_limit_bytes=VMEM_LIMIT),
-        cost_estimate=pl.CostEstimate(
-            flops=6 * pairs * rows * WIN * WIN,
-            bytes_accessed=8 * pairs * rows * WIN,
-            transcendentals=0,
-        ),
+        cost_estimate=SMALL,
         name="cross_products",
     )(arrive, order, *sources, *given)
 
@@ -327,11 +320,7 @@
         out_shape=jax.ShapeDtypeStruct(shape, jnp.float32),
         input_output_aliases={groups + 3: 0} if given else {},
         compiler_params=pltpu.CompilerParams(vmem_limit_bytes=VMEM_LIMIT),
-        cost_estimate=pl.CostEstimate(
-            flops=6 * pairs * rows * 4 * BLK * BLK,
-            bytes_accessed=4 * pairs * rows * (2 * WIN + 2 * BLK),
-            transcendentals=0,
-        ),
+        cost_estimate=SMALL,
         name="rotate",
     )(arrive, order, *sources, turns, *given)
 
@@ -375,9 +364,7 @@
         ),
         out_shape=jax.ShapeDtypeStruct(shape, jnp.float32),
         compiler_params=pltpu.CompilerParams(vmem_limit_bytes=VMEM_LIMIT),
-        cost_estimate=pl.CostEstimate(
-            flops=0, bytes_accessed=8 * count * ROWB * x.shape[1], transcendentals=0
-        ),
+        cost_estimate=SMALL,
         name="gather_rows",
     )(rows_at, x)
 
@@ -422,9 +409,7 @@
         ],
         out_shape=jax.ShapeDtypeStruct(shape, jnp.float32),
         compiler_params=pltpu.CompilerParams(vmem_limit_bytes=VMEM_LIMIT),
-        cost_estimate=pl.CostEstimate(
-            flops=0, bytes_accessed=8 * slabs * rows * groups * width, transcendentals=0
-        ),
+        cost_estimate=SMALL,
         name="slab_pack",
     )(*sources)
 
@@ -504,11 +489,7 @@
         out_shape=jax.ShapeDtypeStruct(shape, jnp.float32),
         input_output_aliases={groups + 4: 0} if given else {},
         compiler_params=pltpu.CompilerParams(vmem_limit_bytes=VMEM_LIMIT),
-        cost_estimate=pl.CostEstimate(
-            flops=6 * pairs * rows * 4 * BLK * BLK,
-            bytes_accessed=4 * pairs * rows * (2 * WIN + 2 * BLK),
-            transcendentals=0,
-        ),
+        cost_estimate=SMALL,
         name="settle",
     )(arrive, order, natural, *sources, turns, *given)
 
@@ -573,21 +554,30 @@
     def over_slab(blocks):
         return lax.all_to_all(blocks, "slab", 0, 0, tiled=True)
 
-    r_sent = pack(r_slabs, send_0, rows_at[slabs * early :], ROWB, groups, units)
-    send_v, r_sent = after(send_0, r_sent)
-    r_late = swap(r_sent, "pair")
+    r_late, last, send, rows_early = [], None, send_0, rows_at[: slabs * early]
+    for lo, hi in bounds[1 if early else 0 :]:
+        sent = pack(r_slabs, send, rows_at[slabs * lo : slabs * hi], ROWB, groups, units)
+        if last is None:
+            send, sent = after(send, sent)
+        else:
+            rows_early, last[1] = after(rows_early, last[1])
+            gathered = gather_rows(r_slabs, rows_early)
+            (sent, gathered), r_late[-1] = after((sent, gathered), last)
+        last = swap(sent, "pair")
+        r_late.append(last)
     first = []
     if early:
-        (rows_early,), r_sent = after([rows_at[: slabs * early]], r_sent)
-        home = over_slab(gather_rows(r_slabs, rows_early)).reshape(-1, r_slabs.shape[1])
+        home = over_slab(gathered).reshape(-1, r_slabs.shape[1])
         sent = pack(home, send_0, straight(home.shape[0]), ROWB, groups, units)
-        sent, (r_late, natural) = after(sent, (r_late, natural))
+        sent, (r_late[-1], natural) = after(sent, (r_late[-1], natural))
         first.append(swap(sent, "pair"))
-    first.append(r_late)
-    sums = gram(r_late, arrive_0, order_0)
+    first += r_late
+    sums = None
+    for got in r_late:
+        sums = gram(got, arrive_0, order_0, sums)
 
     v_sent = [
-        pack(basis, send_v, straight(part, c * part), ROWB, groups, units) for c in range(2)
+        pack(basis, send, straight(part, c * part), ROWB, groups, units) for c in range(2)
     ]
     v_sent[0], (first[0], sums, natural) = after(v_sent[0], (first[0], sums, natural))
     if early:
@@ -599,15 +589,9 @@
         turned = rotate(sources, arrive_0, order_0, turns, row0, size)
         return pack(turned, send_1, straight(size), ROWB, groups, units)
 
-    late_chunks, row0 = [], 0
-    for lo, hi in bounds[1 if early else 0 :]:
-        size = (hi - lo) * slabs * ROWB
-        late_chunks.append((first[-1], row0, size))
-        row0 += size
-    early_chunks = [(first[0], 0, early * slabs * ROWB)] if early else []
     r_two, last = [], v_got[0]
-    for sources, row0, size in late_chunks + early_chunks:
-        sent = second(sources, row0, size)
+    for sources in first[early:] + first[:early]:
+        sent = second(sources, 0, sources[0].shape[0])
         sent, last = after(sent, last)
         if r_two:
             r_two[-1] = last
@@ -616,7 +600,7 @@
         last = swap(sent, "pair")
         r_two.append(last)
 
-    packed = [slab_pack(r_two[c], slabs) for c in range(len(late_chunks))]
+    packed = [slab_pack(r_two[c], slabs) for c in range(len(r_late))]
     v_sent[1], r_two[-1] = after(v_sent[1], r_two[-1])
     v_got[1] = swap(v_sent[1], "pair")
     r_home = [over_slab(blocks) for blocks in packed]

time: 944 us -> 945 us (level)
  local copies, waits for them, and re-layouts: 32 us -> 46.3 us
  waiting for transfers between devices: 410 us -> 397 us
  matrix products: 29 us -> 19.3 us
    unnamed x117 -> x141, local copies, waits for them, and re-layouts: 28.7 us -> 43.6 us
    ppermute x27 -> x30, waiting for transfers between devices: 309 us -> 294 us  [swap(): lax.ppermute(arrays[o], axis, [(i, i ^ o) for i in range(count)])]
    dot_general x2, matrix products: 13.1 us -> 3.52 us  [rotations(): outer_a = jnp.einsum('pik,pjk->pij', coupling, coupling, precision=HIGH)]
    pallas_call x5 -> x6, Pallas kernels: 46.5 us -> 50.5 us  [gram(): pl.pallas_call(functools.partial(gram_kernel, groups, len(given)), grid_s...]
    ppermute x27 -> x30, starting transfers between devices: 31.5 us -> 35 us  [swap(): lax.ppermute(arrays[o], axis, [(i, i ^ o) for i in range(count)])]
    pallas_call x9 -> x10, Pallas kernels: 70 us -> 69.5 us  [pack(): pl.pallas_call(functools.partial(pack_kernel, groups, units, blocks), gri...]
  transfers between devices with their start and end apart: 32 -> 35, of which waited for: 16 -> 18; matrix products, arithmetic and copies ran while one was open for 5% -> 4% of each run, Pallas kernels for 25% -> 27%
where the time goes in v4:
time: 945 us; the launch traced here: 931 us
  waiting for transfers between devices  397 us (42%)
  Pallas kernels  282 us (30%)
  blocking collectives  96.9 us (10%)
  starting transfers between devices  52.7 us (6%)
  local copies, waits for them, and re-layouts  46.3 us (5%)
  other arithmetic  20.6 us (2%)
  matrix products  19.3 us (2%)
  between operations  15.9 us (2%)
    ppermute x30, waiting for transfers between devices, swap(): lax.ppermute(arrays[o], axis, [(i, i ^ o) for i in range(count)])  294 us
    pallas_call x7, Pallas kernels, rotate(): pl.pallas_call(functools.partial(rotate_kernel, groups, row0, len(given))...  108 us
    unnamed x1, blocking collectives  96.9 us
    pallas_call x10, Pallas kernels, pack(): pl.pallas_call(functools.partial(pack_kernel, groups, units, blocks), gri...  69.5 us
    psum x1, waiting for transfers between devices, shards(): turns = turns_of(lax.psum(sums, 'slab'))  56.7 us
    pallas_call x6, Pallas kernels, gram(): pl.pallas_call(functools.partial(gram_kernel, groups, len(given)), grid_s...  50.5 us
    psum x1, waiting for transfers between devices, shards(): sums = lax.psum(sums, 'slab')  46.5 us
    unnamed x141, local copies, waits for them, and re-layouts  43.6 us
  transfers between devices with their start and end apart: 35, of which 18 were waited for; matrix products, arithmetic and copies ran while one was open for 4% of the time, Pallas kernels for 27%

profile of v4, /device:TPU:8, one launch (start us, length us, event | category | flops | bytes accessed | tf_op | source)
XLA Modules:
  0.0 931.0 jit_solution(7626346337093501555)
XLA Ops:
  28.9 17.0 %collective-permute-done.refs_1_ = f32[384,768]{1,0:T(8,128)S(1)} collective-permute-done((f32[384,768]{1,0:T(8,128)S(1)}, f32[384,768]{1,0:T(8,128)S(1)}, u32[]{:S(2)}, u32[]{:S(2)}) %collective-permute-start) | collective-permute-done | bytes 1179680 | tf_op jit(solution)/shard_map/ppermute | solution.py:500
  52.3 19.0 %collective-permute-done.1.refs_2_ = f32[384,768]{1,0:T(8,128)S(1)} collective-permute-done((f32[384,768]{1,0:T(8,128)S(1)}, f32[384,768]{1,0:T(8,128)S(1)}, u32[]{:S(2)}, u32[]{:S(2)}) %collective-permute-start.1) | collective-permute-done | bytes 1179680 | tf_op jit(solution)/shard_map/ppermute | solution.py:500
  83.8 96.9 %all-reduce = s32[256]{0:T(256)S(1)} all-reduce(s32[256]{0:T(256)S(1)} %dynamic-update-slice), channel_id=1, replica_groups=mesh['pair'=4,'slab'=8] {'slab'}, use_global_device_ids=true, to_apply=%add | all-reduce | flops 256 | bytes 2048
  192.4 8.3 pack.12
  215.3 9.6 %cross_products.7.refs_4_ = f32[8,200,256]{2,1,0:T(8,128)S(1)} custom-call(s32[16]{0:T(128)S(1)} %dynamic_slice.12.arrive, s32[16]{0:T(128)S(1)} %dynamic_slice.13.order, f32[768,768]{1,0:T(8,128)S(1)} %get-tuple-element.177.refs_0_, f32[768,768]{1,0:T(8,128)} %collective-permute-done.3.refs_1_, f32[768,768]{1,0:T(8,128)} %collective-permute-done.4.refs_2_, ...), custom_call_target="tpu_custom_call" | custom-call | flops 1 | bytes 1 | tf_op jit(solution)/shard_map/cross_products/pallas_call | solution.py:270
  226.1 15.6 %collective-permute-done.7.refs_2_ = f32[384,768]{1,0:T(8,128)} collective-permute-done((f32[384,768]{1,0:T(8,128)}, f32[384,768]{1,0:T(8,128)}, u32[]{:S(2)}, u32[]{:S(2)}) %collective-permute-start.7) | collective-permute-done | bytes 1179680 | tf_op jit(solution)/shard_map/ppermute | solution.py:500
  243.4 9.9 %cross_products.8 = f32[8,200,256]{2,1,0:T(8,128)} custom-call(s32[16]{0:T(128)S(1)} %dynamic_slice.12.arrive, s32[16]{0:T(128)S(1)} %dynamic_slice.13.order, f32[384,768]{1,0:T(8,128)S(1)} %copy-done.17, f32[384,768]{1,0:T(8,128)} %collective-permute-done.6.refs_1_, f32[384,768]{1,0:T(8,128)} %collective-permute-done.7.refs_2_, ...), custom_call_target="tpu_custom_call" | custom-call | flops 1 | bytes 1 | tf_op jit(solution)/shard_map/cross_products/pallas_call | solution.py:270
  259.7 56.7 %all-reduce.4.cloned.1.call-done = f32[8,200,256]{2,1,0:T(8,128)} async-done(((f32[8,200,256]{2,1,0:T(8,128)}), f32[8,200,256]{2,1,0:T(8,128)}) %all-reduce.4.cloned.1.call-update) | async-done | bytes 1638416 | tf_op jit(solution)/shard_map/psum | solution.py:586
  336.8 10.9 %rotate.7.refs_0_.refs_1_.refs_2_.refs_3_ = f32[384,3072]{1,0:T(8,128)} custom-call(s32[16]{0:T(128)S(1)} %dynamic_slice.12.arrive, s32[16]{0:T(128)S(1)} %dynamic_slice.13.order, f32[384,768]{1,0:T(8,128)S(1)} %get-tuple-element.156.refs_0_, f32[384,768]{1,0:T(8,128)S(1)} %copy-done.9, f32[384,768]{1,0:T(8,128)S(1)} %copy-done.12, ...), custom_call_target="tpu_custom_call" | custom-call | flops 1 | bytes 1 | tf_op jit(solution)/shard_map/rotate/pallas_call | solution.py:306
  363.3 17.0 %rotate.9.refs_0_.refs_1_.refs_2_.refs_3_ = f32[768,3072]{1,0:T(8,128)} custom-call(s32[16]{0:T(128)S(1)} %dynamic_slice.12.arrive, s32[16]{0:T(128)S(1)} %dynamic_slice.13.order, f32[768,768]{1,0:T(8,128)S(1)} %get-tuple-element.177.refs_0_, f32[768,768]{1,0:T(8,128)} %collective-permute-done.3.refs_1_, f32[768,768]{1,0:T(8,128)} %collective-permute-done.4.refs_2_, ...), custom_call_target="tpu_custom_call" | custom-call | flops 1 | bytes 1 | tf_op jit(solution)/shard_map/rotate/pallas_call | solution.py:306
  390.0 20.1 %collective-permute-done.13.refs_2_ = f32[384,768]{1,0:T(8,128)S(1)} collective-permute-done((f32[384,768]{1,0:T(8,128)S(1)}, f32[384,768]{1,0:T(8,128)S(1)}, u32[]{:S(2)}, u32[]{:S(2)}) %collective-permute-start.13) | collective-permute-done | bytes 1179680 | tf_op jit(solution)/shard_map/ppermute | solution.py:500
  428.9 12.2 %rotate.8.refs_0_.refs_1_.refs_2_.refs_3_ = f32[384,3072]{1,0:T(8,128)} custom-call(s32[16]{0:T(128)S(1)} %dynamic_slice.12.arrive, s32[16]{0:T(128)S(1)} %dynamic_slice.13.order, f32[384,768]{1,0:T(8,128)S(1)} %copy-done.18, f32[384,768]{1,0:T(8,128)} %collective-permute-done.6.refs_1_, f32[384,768]{1,0:T(8,128)} %collective-permute-done.7.refs_2_, ...), custom_call_target="tpu_custom_call" | custom-call | flops 1 | bytes 1 | tf_op jit(solution)/shard_map/rotate/pallas_call | solution.py:306
  448.5 31.3 %collective-permute-done.15.refs_1_ = f32[768,768]{1,0:T(8,128)S(1)} collective-permute-done((f32[768,768]{1,0:T(8,128)}, f32[768,768]{1,0:T(8,128)S(1)}, u32[]{:S(2)}, u32[]{:S(2)}) %collective-permute-start.15) | collective-permute-done | bytes 2359328 | tf_op jit(solution)/shard_map/ppermute | solution.py:500
  479.7 50.3 %collective-permute-done.16.refs_2_ = f32[768,768]{1,0:T(8,128)S(1)} collective-permute-done((f32[768,768]{1,0:T(8,128)}, f32[768,768]{1,0:T(8,128)S(1)}, u32[]{:S(2)}, u32[]{:S(2)}) %collective-permute-start.16) | collective-permute-done | bytes 2359328 | tf_op jit(solution)/shard_map/ppermute | solution.py:500
  547.6 9.5 %pack.15 = (f32[768,768]{1,0:T(8,128)S(1)}, f32[768,768]{1,0:T(8,128)}, f32[768,768]{1,0:T(8,128)}, f32[768,768]{1,0:T(8,128)}) custom-call(s32[16]{0:T(128)S(1)} %reshape.492.send, s32[16]{0:T(128)S(1)} %iota_add_fusion.rows_at, f32[1536,3072]{1,0:T(8,128)} %refs_3_.7, f32[1536,3072]{1,0:T(8,128)} %refs_3_.7, f32[1536,3072]{1,0:T(8,128)} %refs_3_.7, ...), custom_call_target="tpu_custom_call" | custom-call | flops 1 | bytes 1 | tf_op jit(solution)/shard_map/pack/pallas_call | solution.py:133
  558.5 14.6 %collective-permute-done.18.refs_1_ = f32[384,768]{1,0:T(8,128)S(1)} collective-permute-done((f32[384,768]{1,0:T(8,128)}, f32[384,768]{1,0:T(8,128)S(1)}, u32[]{:S(2)}, u32[]{:S(2)}) %collective-permute-start.18) | collective-permute-done | bytes 1179680 | tf_op jit(solution)/shard_map/ppermute | solution.py:500
  573.1 23.9 %collective-permute-done.19.refs_2_ = f32[384,768]{1,0:T(8,128)S(1)} collective-permute-done((f32[384,768]{1,0:T(8,128)}, f32[384,768]{1,0:T(8,128)S(1)}, u32[]{:S(2)}, u32[]{:S(2)}) %collective-permute-start.19) | collective-permute-done | bytes 1179680 | tf_op jit(solution)/shard_map/ppermute | solution.py:500
  611.2 9.8 %cross_products.10.refs_4_ = f32[8,200,256]{2,1,0:T(8,128)S(1)} custom-call(s32[16]{0:T(128)S(1)} %dynamic_slice.14.arrive, s32[16]{0:T(128)S(1)} %dynamic_slice.15.order, f32[768,768]{1,0:T(8,128)S(1)} %get-tuple-element.229.refs_0_, f32[768,768]{1,0:T(8,128)} %copy-done.2, f32[768,768]{1,0:T(8,128)} %copy-done.52, f32[768,768]{1,0:T(8,128)} %copy-done.53, ...), custom_call_target="tpu_custom_call" | custom-call | flops 1 | bytes 1 | tf_op jit(solution)/shard_map/cross_products/pallas_call | solution.py:270
  622.3 8.5 cross_products.11
  630.8 17.0 %rotate.10.refs_0_.refs_1_.refs_2_.refs_3_ = f32[768,3072]{1,0:T(8,128)} custom-call(s32[16]{0:T(128)S(1)} %dynamic_slice.12.arrive, s32[16]{0:T(128)S(1)} %dynamic_slice.13.order, f32[768,768]{1,0:T(8,128)S(1)} %copy-done.34, f32[768,768]{1,0:T(8,128)} %collective-permute-done.9.refs_1_, f32[768,768]{1,0:T(8,128)} %collective-permute-done.10.refs_2_, ...), custom_call_target="tpu_custom_call" | custom-call | flops 1 | bytes 1 | tf_op jit(solution)/shard_map/rotate/pallas_call | solution.py:306
  647.8 9.0 pack.18
  656.9 45.3 %collective-permute-done.22.refs_2_ = f32[768,768]{1,0:T(8,128)} collective-permute-done((f32[768,768]{1,0:T(8,128)}, f32[768,768]{1,0:T(8,128)}, u32[]{:S(2)}, u32[]{:S(2)}) %collective-permute-start.22) | collective-permute-done | bytes 2359328 | tf_op jit(solution)/shard_map/ppermute | solution.py:500
  707.4 17.0 %rotate.11.refs_0_.refs_1_.refs_2_.refs_3_ = f32[768,3072]{1,0:T(8,128)} custom-call(s32[16]{0:T(128)S(1)} %dynamic_slice.12.arrive, s32[16]{0:T(128)S(1)} %dynamic_slice.13.order, f32[768,768]{1,0:T(8,128)S(1)} %copy-done.38, f32[768,768]{1,0:T(8,128)} %collective-permute-done.21.refs_1_, f32[768,768]{1,0:T(8,128)} %collective-permute-done.22.refs_2_, ...), custom_call_target="tpu_custom_call" | custom-call | flops 1 | bytes 1 | tf_op jit(solution)/shard_map/rotate/pallas_call | solution.py:306
  724.5 8.4 pack.19
  735.7 46.5 %all-reduce.6.cloned.1.call-done = f32[8,200,256]{2,1,0:T(8,128)} async-done(((f32[8,200,256]{2,1,0:T(8,128)}), f32[8,200,256]{2,1,0:T(8,128)}) %all-reduce.6.cloned.1.call-update) | async-done | bytes 1638416 | tf_op jit(solution)/shard_map/psum | solution.py:611
  782.2 23.3 %collective-permute-done.25.refs_2_ = f32[768,768]{1,0:T(8,128)} collective-permute-done((f32[768,768]{1,0:T(8,128)}, f32[768,768]{1,0:T(8,128)}, u32[]{:S(2)}, u32[]{:S(2)}) %collective-permute-start.25) | collective-permute-done | bytes 2359328 | tf_op jit(solution)/shard_map/ppermute | solution.py:500
  824.6 11.8 %settle.3.refs_2_ = f32[1536,3072]{1,0:T(8,128)} custom-call(s32[16]{0:T(128)S(1)} %dynamic_slice.14.arrive, s32[16]{0:T(128)S(1)} %dynamic_slice.15.order, s32[8]{0:T(128)S(1)} %copy-done.43, f32[384,768]{1,0:T(8,128)S(1)} %get-tuple-element.225.refs_0_, f32[384,768]{1,0:T(8,128)S(1)} %copy-done.20, f32[384,768]{1,0:T(8,128)S(1)} %copy-done.22, ...), custom_call_target="tpu_custom_call" | custom-call | flops 1 | bytes 1 | tf_op jit(solution)/shard_map/settle/pallas_call | solution.py:473
  836.4 13.2 %settle.4.refs_2_ = f32[1536,3072]{1,0:T(8,128)} custom-call(s32[16]{0:T(128)S(1)} %dynamic_slice.14.arrive, s32[16]{0:T(128)S(1)} %dynamic_slice.15.order, s32[8]{0:T(128)S(1)} %copy-done.44, f32[384,3072]{1,0:T(8,128)} %bitcast.8.refs_0_, f32[8,384,384]{2,1,0:T(8,128)} %maximum_maximum_fusion.1.refs_4_.refs_1_, ...), custom_call_target="tpu_custom_call", output_to_operand_aliasing={{}: (5, {})} | custom-call | flops 1 | bytes 1 | tf_op jit(solution)/shard_map/settle/pallas_call | solution.py:473
  849.6 17.0 %rotate.12.refs_5_ = f32[1536,3072]{1,0:T(8,128)} custom-call(s32[16]{0:T(128)S(1)} %dynamic_slice.14.arrive, s32[16]{0:T(128)S(1)} %dynamic_slice.15.order, f32[768,768]{1,0:T(8,128)S(1)} %get-tuple-element.270.refs_0_, f32[768,768]{1,0:T(8,128)} %collective-permute-done.24.refs_1_, f32[768,768]{1,0:T(8,128)} %collective-permute-done.25.refs_2_, ...), custom_call_target="tpu_custom_call" | custom-call | flops 1 | bytes 1 | tf_op jit(solution)/shard_map/rotate/pallas_call | solution.py:306
  869.0 16.7 %settle.5 = f32[1536,3072]{1,0:T(8,128)} custom-call(s32[16]{0:T(128)S(1)} %dynamic_slice.14.arrive, s32[16]{0:T(128)S(1)} %dynamic_slice.15.order, s32[16]{0:T(128)S(1)} %copy-done.42, f32[768,3072]{1,0:T(8,128)} %bitcast.7.refs_0_, f32[8,384,384]{2,1,0:T(8,128)S(1)} %copy-done, f32[1536,3072]{1,0:T(8,128)} %settle.4.refs_2_), custom_call_target="tpu_custom_call", output_to_operand_aliasing={{}: (5, {})} | custom-call | flops 1 | bytes 1 | tf_op jit(solution)/shard_map/settle/pallas_call | solution.py:473
  885.7 20.9 %collective-permute-done.28.refs_2_ = f32[768,768]{1,0:T(8,128)} collective-permute-done((f32[768,768]{1,0:T(8,128)}, f32[768,768]{1,0:T(8,128)}, u32[]{:S(2)}, u32[]{:S(2)}) %collective-permute-start.28) | collective-permute-done | bytes 2359328 | tf_op jit(solution)/shard_map/ppermute | solution.py:500
  906.6 17.1 %rotate.13 = f32[1536,3072]{1,0:T(8,128)} custom-call(s32[16]{0:T(128)S(1)} %dynamic_slice.14.arrive, s32[16]{0:T(128)S(1)} %dynamic_slice.15.order, f32[768,768]{1,0:T(8,128)S(1)} %copy-done.36, f32[768,768]{1,0:T(8,128)} %collective-permute-done.27.refs_1_, f32[768,768]{1,0:T(8,128)} %collective-permute-done.28.refs_2_, ...), custom_call_target="tpu_custom_call", output_to_operand_aliasing={{}: (7, {})} | custom-call | flops 1 | bytes 1 | tf_op jit(solution)/shard_map/rotate/pallas_call | solution.py:306
  (276 shorter events, 210.6 us)
Async XLA Ops:
  18.6 52.7 %collective-permute-start.1 = (f32[384,768]{1,0:T(8,128)S(1)}, f32[384,768]{1,0:T(8,128)S(1)}, u32[]{:S(2)}, u32[]{:S(2)}) collective-permute-start(f32[384,768]{1,0:T(8,128)S(1)} %get-tuple-element.154), channel_id=1, source_target_pairs={{0,16},{8,24},{16,0},{24,8},{1,17},{9,25},{17,1},{25,9},{2,18},{10... | collective-permute-start | bytes 3538952 | tf_op jit(solution)/shard_map/ppermute | solution.py:500
  20.1 52.2 %collective-permute-start.2 = (f32[384,768]{1,0:T(8,128)S(1)}, f32[384,768]{1,0:T(8,128)S(1)}, u32[]{:S(2)}, u32[]{:S(2)}) collective-permute-start(f32[384,768]{1,0:T(8,128)S(1)} %get-tuple-element.155), channel_id=1, source_target_pairs={{0,24},{8,16},{16,8},{24,0},{1,25},{9,17},{17,9},{25,1},{2,26},{10... | collective-permute-start | bytes 3538952 | tf_op jit(solution)/shard_map/ppermute | solution.py:500
  73.3 109.2 %all-to-all-start = ((f32[8,48,3072]{2,1,0:T(8,128)}), f32[8,48,3072]{2,1,0:T(8,128)}, u32[]{:S(2)}, u32[]{:S(2)}) async-start(f32[8,48,3072]{2,1,0:T(8,128)} %copy-done.1), calls=%async_computation | async-start | bytes 9437184 | tf_op jit(solution)/shard_map/all_to_all | solution.py:555
  78.8 237.6 %all-reduce.4.cloned.1.call-start = ((), (), s32[]{:S(2)}) async-start(), calls=%async_computation.3 | async-start | bytes 3276800 | tf_op jit(solution)/shard_map/psum | solution.py:586
  78.8 110.1 %collective-permute-start.3 = (f32[768,768]{1,0:T(8,128)}, f32[768,768]{1,0:T(8,128)}, u32[]{:S(2)}, u32[]{:S(2)}) collective-permute-start(f32[768,768]{1,0:T(8,128)} %copy-done.46), channel_id=1, source_target_pairs={{0,8},{8,0},{16,24},{24,16},{1,9},{9,1},{17,25},{25,17},{2,10},{10... | collective-permute-start | bytes 7077896 | tf_op jit(solution)/shard_map/ppermute | solution.py:500
  79.0 109.9 %collective-permute-start.4 = (f32[768,768]{1,0:T(8,128)}, f32[768,768]{1,0:T(8,128)}, u32[]{:S(2)}, u32[]{:S(2)}) collective-permute-start(f32[768,768]{1,0:T(8,128)} %get-tuple-element.171), channel_id=1, source_target_pairs={{0,16},{8,24},{16,0},{24,8},{1,17},{9,25},{17,1},{25,9},{2,18},{10... | collective-permute-start | bytes 7077896 | tf_op jit(solution)/shard_map/ppermute | solution.py:500
  80.8 108.0 %collective-permute-start.5 = (f32[768,768]{1,0:T(8,128)}, f32[768,768]{1,0:T(8,128)}, u32[]{:S(2)}, u32[]{:S(2)}) collective-permute-start(f32[768,768]{1,0:T(8,128)} %get-tuple-element.172), channel_id=1, source_target_pairs={{0,24},{8,16},{16,8},{24,0},{1,25},{9,17},{17,9},{25,1},{2,26},{10... | collective-permute-start | bytes 7077896 | tf_op jit(solution)/shard_map/ppermute | solution.py:500
  188.9 37.3 %collective-permute-start.6 = (f32[384,768]{1,0:T(8,128)}, f32[384,768]{1,0:T(8,128)}, u32[]{:S(2)}, u32[]{:S(2)}) collective-permute-start(f32[384,768]{1,0:T(8,128)} %get-tuple-element.174), channel_id=1, source_target_pairs={{0,8},{8,0},{16,24},{24,16},{1,9},{9,1},{17,25},{25,17},{2,10},{10... | collective-permute-start | bytes 3538952 | tf_op jit(solution)/shard_map/ppermute | solution.py:500
  189.2 52.6 %collective-permute-start.7 = (f32[384,768]{1,0:T(8,128)}, f32[384,768]{1,0:T(8,128)}, u32[]{:S(2)}, u32[]{:S(2)}) collective-permute-start(f32[384,768]{1,0:T(8,128)} %get-tuple-element.175), channel_id=1, source_target_pairs={{0,16},{8,24},{16,0},{24,8},{1,17},{9,25},{17,1},{25,9},{2,18},{10... | collective-permute-start | bytes 3538952 | tf_op jit(solution)/shard_map/ppermute | solution.py:500
  191.0 52.4 %collective-permute-start.8 = (f32[384,768]{1,0:T(8,128)}, f32[384,768]{1,0:T(8,128)}, u32[]{:S(2)}, u32[]{:S(2)}) collective-permute-start(f32[384,768]{1,0:T(8,128)} %get-tuple-element.176), channel_id=1, source_target_pairs={{0,24},{8,16},{16,8},{24,0},{1,25},{9,17},{17,9},{25,1},{2,26},{10... | collective-permute-start | bytes 3538952 | tf_op jit(solution)/shard_map/ppermute | solution.py:500
  256.2 95.8 %collective-permute-start.9 = (f32[768,768]{1,0:T(8,128)}, f32[768,768]{1,0:T(8,128)}, u32[]{:S(2)}, u32[]{:S(2)}) collective-permute-start(f32[768,768]{1,0:T(8,128)} %copy-done.45), channel_id=1, source_target_pairs={{0,8},{8,0},{16,24},{24,16},{1,9},{9,1},{17,25},{25,17},{2,10},{10... | collective-permute-start | bytes 7077896 | tf_op jit(solution)/shard_map/ppermute | solution.py:500
  257.1 102.7 %collective-permute-start.10 = (f32[768,768]{1,0:T(8,128)}, f32[768,768]{1,0:T(8,128)}, u32[]{:S(2)}, u32[]{:S(2)}) collective-permute-start(f32[768,768]{1,0:T(8,128)} %get-tuple-element.195), channel_id=1, source_target_pairs={{0,16},{8,24},{16,0},{24,8},{1,17},{9,25},{17,1},{25,9},{2,18},{10... | collective-permute-start | bytes 7077896 | tf_op jit(solution)/shard_map/ppermute | solution.py:500
  258.6 101.2 %collective-permute-start.11 = (f32[768,768]{1,0:T(8,128)}, f32[768,768]{1,0:T(8,128)}, u32[]{:S(2)}, u32[]{:S(2)}) collective-permute-start(f32[768,768]{1,0:T(8,128)} %get-tuple-element.196), channel_id=1, source_target_pairs={{0,24},{8,16},{16,8},{24,0},{1,25},{9,17},{17,9},{25,1},{2,26},{10... | collective-permute-start | bytes 7077896 | tf_op jit(solution)/shard_map/ppermute | solution.py:500
  361.1 48.9 %collective-permute-start.13 = (f32[384,768]{1,0:T(8,128)S(1)}, f32[384,768]{1,0:T(8,128)S(1)}, u32[]{:S(2)}, u32[]{:S(2)}) collective-permute-start(f32[384,768]{1,0:T(8,128)S(1)} %get-tuple-element.215), channel_id=1, source_target_pairs={{0,16},{8,24},{16,0},{24,8},{1,17},{9,25},{17,1},{25,9},{2,18},{10... | collective-permute-start | bytes 3538952 | tf_op jit(solution)/shard_map/ppermute | solution.py:500
  361.8 50.0 %collective-permute-start.14 = (f32[384,768]{1,0:T(8,128)S(1)}, f32[384,768]{1,0:T(8,128)S(1)}, u32[]{:S(2)}, u32[]{:S(2)}) collective-permute-start(f32[384,768]{1,0:T(8,128)S(1)} %get-tuple-element.216), channel_id=1, source_target_pairs={{0,24},{8,16},{16,8},{24,0},{1,25},{9,17},{17,9},{25,1},{2,26},{10... | collective-permute-start | bytes 3538952 | tf_op jit(solution)/shard_map/ppermute | solution.py:500
  418.5 120.3 %all-to-all-start.2 = ((f32[8,48,3072]{2,1,0:T(8,128)}), f32[8,48,3072]{2,1,0:T(8,128)}, u32[]{:S(2)}, u32[]{:S(2)}) async-start(f32[8,48,3072]{2,1,0:T(8,128)} %slab_pack.3), calls=%async_computation.2 | async-start | bytes 9437184 | tf_op jit(solution)/shard_map/all_to_all | solution.py:555
  425.4 54.3 %collective-permute-start.15 = (f32[768,768]{1,0:T(8,128)}, f32[768,768]{1,0:T(8,128)S(1)}, u32[]{:S(2)}, u32[]{:S(2)}) collective-permute-start(f32[768,768]{1,0:T(8,128)} %copy-done.48), channel_id=1, source_target_pairs={{0,8},{8,0},{16,24},{24,16},{1,9},{9,1},{17,25},{25,17},{2,10},{10... | collective-permute-start | bytes 7077896 | tf_op jit(solution)/shard_map/ppermute | solution.py:500
  426.2 103.8 %collective-permute-start.16 = (f32[768,768]{1,0:T(8,128)}, f32[768,768]{1,0:T(8,128)S(1)}, u32[]{:S(2)}, u32[]{:S(2)}) collective-permute-start(f32[768,768]{1,0:T(8,128)} %get-tuple-element.219), channel_id=1, source_target_pairs={{0,16},{8,24},{16,0},{24,8},{1,17},{9,25},{17,1},{25,9},{2,18},{10... | collective-permute-start | bytes 7077896 | tf_op jit(solution)/shard_map/ppermute | solution.py:500
  427.8 102.3 %collective-permute-start.17 = (f32[768,768]{1,0:T(8,128)}, f32[768,768]{1,0:T(8,128)S(1)}, u32[]{:S(2)}, u32[]{:S(2)}) collective-permute-start(f32[768,768]{1,0:T(8,128)} %get-tuple-element.220), channel_id=1, source_target_pairs={{0,24},{8,16},{16,8},{24,0},{1,25},{9,17},{17,9},{25,1},{2,26},{10... | collective-permute-start | bytes 7077896 | tf_op jit(solution)/shard_map/ppermute | solution.py:500
  538.8 327.9 %all-to-all-start.1 = ((f32[8,96,3072]{2,1,0:T(8,128)}), f32[8,96,3072]{2,1,0:T(8,128)}, u32[]{:S(2)}, u32[]{:S(2)}) async-start(f32[8,96,3072]{2,1,0:T(8,128)} %slab_pack.2), calls=%async_computation.1 | async-start | bytes 18874368 | tf_op jit(solution)/shard_map/all_to_all | solution.py:555
  544.1 238.1 %all-reduce.6.cloned.1.call-start = ((), (), s32[]{:S(2)}) async-start(), calls=%async_computation.4 | async-start | bytes 3276800 | tf_op jit(solution)/shard_map/psum | solution.py:611
  544.6 52.5 %collective-permute-start.19 = (f32[384,768]{1,0:T(8,128)}, f32[384,768]{1,0:T(8,128)S(1)}, u32[]{:S(2)}, u32[]{:S(2)}) collective-permute-start(f32[384,768]{1,0:T(8,128)} %copy-done.50), channel_id=1, source_target_pairs={{0,16},{8,24},{16,0},{24,8},{1,17},{9,25},{17,1},{25,9},{2,18},{10... | collective-permute-start | bytes 3538952 | tf_op jit(solution)/shard_map/ppermute | solution.py:500
  546.1 52.4 %collective-permute-start.20 = (f32[384,768]{1,0:T(8,128)}, f32[384,768]{1,0:T(8,128)S(1)}, u32[]{:S(2)}, u32[]{:S(2)}) collective-permute-start(f32[384,768]{1,0:T(8,128)} %copy-done.49), channel_id=1, source_target_pairs={{0,24},{8,16},{16,8},{24,0},{1,25},{9,17},{17,9},{25,1},{2,26},{10... | collective-permute-start | bytes 3538952 | tf_op jit(solution)/shard_map/ppermute | solution.py:500
  598.6 58.3 %collective-permute-start.21 = (f32[768,768]{1,0:T(8,128)}, f32[768,768]{1,0:T(8,128)}, u32[]{:S(2)}, u32[]{:S(2)}) collective-permute-start(f32[768,768]{1,0:T(8,128)} %get-tuple-element.246), channel_id=1, source_target_pairs={{0,8},{8,0},{16,24},{24,16},{1,9},{9,1},{17,25},{25,17},{2,10},{10... | collective-permute-start | bytes 7077896 | tf_op jit(solution)/shard_map/ppermute | solution.py:500
  599.4 102.8 %collective-permute-start.22 = (f32[768,768]{1,0:T(8,128)}, f32[768,768]{1,0:T(8,128)}, u32[]{:S(2)}, u32[]{:S(2)}) collective-permute-start(f32[768,768]{1,0:T(8,128)} %get-tuple-element.247), channel_id=1, source_target_pairs={{0,16},{8,24},{16,0},{24,8},{1,17},{9,25},{17,1},{25,9},{2,18},{10... | collective-permute-start | bytes 7077896 | tf_op jit(solution)/shard_map/ppermute | solution.py:500
  601.0 101.3 %collective-permute-start.23 = (f32[768,768]{1,0:T(8,128)}, f32[768,768]{1,0:T(8,128)}, u32[]{:S(2)}, u32[]{:S(2)}) collective-permute-start(f32[768,768]{1,0:T(8,128)} %get-tuple-element.248), channel_id=1, source_target_pairs={{0,24},{8,16},{16,8},{24,0},{1,25},{9,17},{17,9},{25,1},{2,26},{10... | collective-permute-start | bytes 7077896 | tf_op jit(solution)/shard_map/ppermute | solution.py:500
  702.2 80.0 %collective-permute-start.24 = (f32[768,768]{1,0:T(8,128)}, f32[768,768]{1,0:T(8,128)}, u32[]{:S(2)}, u32[]{:S(2)}) collective-permute-start(f32[768,768]{1,0:T(8,128)} %get-tuple-element.259), channel_id=1, source_target_pairs={{0,8},{8,0},{16,24},{24,16},{1,9},{9,1},{17,25},{25,17},{2,10},{10... | collective-permute-start | bytes 7077896 | tf_op jit(solution)/shard_map/ppermute | solution.py:500
  703.7 101.8 %collective-permute-start.25 = (f32[768,768]{1,0:T(8,128)}, f32[768,768]{1,0:T(8,128)}, u32[]{:S(2)}, u32[]{:S(2)}) collective-permute-start(f32[768,768]{1,0:T(8,128)} %get-tuple-element.260), channel_id=1, source_target_pairs={{0,16},{8,24},{16,0},{24,8},{1,17},{9,25},{17,1},{25,9},{2,18},{10... | collective-permute-start | bytes 7077896 | tf_op jit(solution)/shard_map/ppermute | solution.py:500
  704.2 101.4 %collective-permute-start.26 = (f32[768,768]{1,0:T(8,128)}, f32[768,768]{1,0:T(8,128)}, u32[]{:S(2)}, u32[]{:S(2)}) collective-permute-start(f32[768,768]{1,0:T(8,128)} %get-tuple-element.261), channel_id=1, source_target_pairs={{0,24},{8,16},{16,8},{24,0},{1,25},{9,17},{17,9},{25,1},{2,26},{10... | collective-permute-start | bytes 7077896 | tf_op jit(solution)/shard_map/ppermute | solution.py:500
  805.6 80.2 %collective-permute-start.27 = (f32[768,768]{1,0:T(8,128)}, f32[768,768]{1,0:T(8,128)}, u32[]{:S(2)}, u32[]{:S(2)}) collective-permute-start(f32[768,768]{1,0:T(8,128)} %copy-done.47), channel_id=1, source_target_pairs={{0,8},{8,0},{16,24},{24,16},{1,9},{9,1},{17,25},{25,17},{2,10},{10... | collective-permute-start | bytes 7077896 | tf_op jit(solution)/shard_map/ppermute | solution.py:500
  805.9 100.8 %collective-permute-start.28 = (f32[768,768]{1,0:T(8,128)}, f32[768,768]{1,0:T(8,128)}, u32[]{:S(2)}, u32[]{:S(2)}) collective-permute-start(f32[768,768]{1,0:T(8,128)} %get-tuple-element.264), channel_id=1, source_target_pairs={{0,16},{8,24},{16,0},{24,8},{1,17},{9,25},{17,1},{25,9},{2,18},{10... | collective-permute-start | bytes 7077896 | tf_op jit(solution)/shard_map/ppermute | solution.py:500
  807.7 98.9 %collective-permute-start.29 = (f32[768,768]{1,0:T(8,128)}, f32[768,768]{1,0:T(8,128)}, u32[]{:S(2)}, u32[]{:S(2)}) collective-permute-start(f32[768,768]{1,0:T(8,128)} %get-tuple-element.265), channel_id=1, source_target_pairs={{0,24},{8,16},{16,8},{24,0},{1,25},{9,17},{17,9},{25,1},{2,26},{10... | collective-permute-start | bytes 7077896 | tf_op jit(solution)/shard_map/ppermute | solution.py:500
  (70 other events, 921.5 us)
Sparse Core Ops, SparseCore 0:
  253.5 62.8 all-reduce.3
  705.9 76.2 all-reduce.5
